TPU v7x, 512 devices: a whole 4x8x8 slice. The times are simulated.
512 devices in a mesh: pos: 128 (over z, y, core), cuts: 4 (over x).
Axes of the slice: x: 4, y: 8, z: 8, core: 2. Of those that a mesh axis runs over, the one named last changes fastest.
Arguments:
- specimen: float32 [2, 4, 16384, 512], P(None, 'cuts', 'pos'), may hold values from -4 to 4
- probe: float32 [2, 128, 128], replicated, may hold values from -4 to 4
- amplitude: float32 [1024, 128, 128], P('pos'), may hold values from 0 to 2
- offsets: int32 [2, 1024], P(None, 'pos'), may hold values from 0 to 16256, as said below
- live: int32 [128], P('pos'), may hold values from 1 to 8, 512 in all
Outputs:
- slice_grad: float32 [2, 4, 16384, 512], P(None, 'cuts', 'pos')
- probe_grad: float32 [2, 128, 128], P(None, 'cuts')
Inputs may be any that keep to these rules, and one draw needn't show every extreme that they name: `offsets`: position slot p belongs to index p div 8 of pos, and its row offset lies in that index's rows: from (p div 8) * 128 to that plus 128 - 1; every window lies inside the specimen (row offset at most 16256, column offset at most 384); the first slot's window starts at row 0 and column 0, the last slot's at row 16256 and column 384. `live`: the counts sum to half of all 1024 slots; some index of pos has all 8 slots used.
All inputs are finite; a program needn't handle non-finite values. No bound on the sum of `live` on one device may be relied on, other than what follows from the above.
Results may differ from a plain program's by a relative error of at most 0.00029.
Values sent between devices are 32-bit elements; how exact they have to be, the bound alone decides.
No kernel may reach another device: no remote copies, remote signals or barrier semaphores. Data moves between devices by JAX's collectives and lax.ppermute only.
A program may use at most 64 MiB of HBM per device.

v0:
```python
import math

import jax
import jax.numpy as jnp
from jax import lax
from jax.sharding import PartitionSpec as P

FRESNEL = 0.7


def passed_along(block, axis, distance):
    devices = range(lax.axis_size(axis))
    route = [(i - distance, i) for i in devices if i - distance in devices]
    return lax.ppermute(block, axis, route)


def make_tables(pattern):
    index = jnp.arange(pattern, dtype=jnp.int32)
    product = index[:, None] * index[None, :] % pattern
    angle = 2.0 * math.pi / pattern * product.astype(jnp.float32)
    scale = 1.0 / math.sqrt(pattern)
    four_real = jnp.cos(angle) * scale
    four_imag = -jnp.sin(angle) * scale
    signed = jnp.where(index < pattern // 2, index, index - pattern)
    phase = FRESNEL * math.pi / pattern * (signed * signed).astype(jnp.float32)
    spacing = (index[:, None] - index[None, :]) % pattern
    turns = spacing[:, :, None] * index[None, None, :] % pattern
    argument = phase[None, None, :] + 2.0 * math.pi / pattern * turns.astype(jnp.float32)
    prop_real = jnp.mean(jnp.cos(argument), axis=2)
    prop_imag = jnp.mean(jnp.sin(argument), axis=2)
    return (four_real, four_imag, prop_real, prop_imag)


def complex_mult(a_real, a_imag, b_real, b_imag):
    return (a_real * b_real - a_imag * b_imag, a_real * b_imag + a_imag * b_real)


def conj_mult(a_real, a_imag, b_real, b_imag):
    return (a_real * b_real + a_imag * b_imag, a_real * b_imag - a_imag * b_real)


def mat_left(table, batch):
    return jnp.einsum("mk,bkn->bmn", table, batch, precision=lax.Precision.HIGHEST)


def mat_right(batch, table):
    return jnp.einsum("bmk,kn->bmn", batch, table, precision=lax.Precision.HIGHEST)


def both_sides(wave_real, wave_imag, table_real, table_imag):
    left_real = mat_left(table_real, wave_real) - mat_left(table_imag, wave_imag)
    left_imag = mat_left(table_real, wave_imag) + mat_left(table_imag, wave_real)
    right_real = mat_right(left_real, table_real) - mat_right(left_imag, table_imag)
    right_imag = mat_right(left_real, table_imag) + mat_right(left_imag, table_real)
    return (right_real, right_imag)


def far_residual(exit_real, exit_imag, amplitude, weight, tables):
    four_real, four_imag = (tables[0], tables[1])
    far_real, far_imag = both_sides(exit_real, exit_imag, four_real, four_imag)
    magnitude = jnp.sqrt(far_real * far_real + far_imag * far_imag)
    factor = weight[:, None, None] * (1.0 - amplitude / jnp.maximum(magnitude, 1.0))
    return both_sides(factor * far_real, factor * far_imag, four_real, -four_imag)


def scatter_add(canvas, values, row_offsets, col_offsets):
    anchor = jnp.zeros((), jnp.int32)

    def add_one(position, current_canvas):
        corner = (anchor, row_offsets[position], col_offsets[position])
        current = lax.dynamic_slice(current_canvas, corner, values.shape[1:])
        return lax.dynamic_update_slice(current_canvas, current + values[position], corner)

    return lax.fori_loop(0, values.shape[0], add_one, canvas)


def local(specimen, probe, amplitude, offsets, live):
    pattern = probe.shape[1]
    stripe = specimen.shape[2]
    columns = specimen.shape[3]
    slot_count = amplitude.shape[0]
    across = lax.axis_size("pos")
    slice_count = lax.axis_size("cuts")
    tile_index = lax.axis_index("pos")
    layer_index = lax.axis_index("cuts")
    tables = make_tables(pattern)
    prop_real, prop_imag = (tables[2], tables[3])
    own_rows = specimen[:, 0]
    next_rows = passed_along(own_rows, "pos", -1)
    extended = jnp.concatenate([own_rows, next_rows], axis=1)
    row_offsets = offsets[0] - tile_index * stripe
    col_offsets = offsets[1]
    weight = (jnp.arange(slot_count, dtype=jnp.int32) < live[0]).astype(jnp.float32)
    anchor = jnp.zeros((), jnp.int32)

    def window(row_at, col_at):
        return lax.dynamic_slice(extended, (anchor, row_at, col_at), (2, pattern, pattern))

    windows = jax.vmap(window)(row_offsets, col_offsets)
    base_real = jnp.broadcast_to(probe[0], (slot_count, pattern, pattern))
    base_imag = jnp.broadcast_to(probe[1], (slot_count, pattern, pattern))
    patch_real = windows[:, 0]
    patch_imag = windows[:, 1]
    wave_real, wave_imag = (base_real, base_imag)
    inc_real, inc_imag = (base_real, base_imag)
    for hop_index in range(1, slice_count):
        exit_real, exit_imag = complex_mult(wave_real, wave_imag, patch_real, patch_imag)
        moved_real, moved_imag = both_sides(exit_real, exit_imag, prop_real, prop_imag)
        wave_real, wave_imag = passed_along((moved_real, moved_imag), "cuts", 1)
        arrived = layer_index == hop_index
        inc_real = jnp.where(arrived, wave_real, inc_real)
        inc_imag = jnp.where(arrived, wave_imag, inc_imag)
    exit_real, exit_imag = complex_mult(inc_real, inc_imag, patch_real, patch_imag)
    back_real, back_imag = far_residual(exit_real, exit_imag, amplitude, weight, tables)
    is_last = layer_index == slice_count - 1
    back_real = jnp.where(is_last, back_real, jnp.zeros_like(back_real))
    back_imag = jnp.where(is_last, back_imag, jnp.zeros_like(back_imag))
    for hop_index in range(slice_count - 2, -1, -1):
        carry_real, carry_imag = conj_mult(patch_real, patch_imag, back_real, back_imag)
        upward_real, upward_imag = both_sides(carry_real, carry_imag, prop_real, -prop_imag)
        got_real, got_imag = passed_along((upward_real, upward_imag), "cuts", -1)
        arrived = layer_index == hop_index
        back_real = jnp.where(arrived, got_real, back_real)
        back_imag = jnp.where(arrived, got_imag, back_imag)
    grad_real, grad_imag = conj_mult(inc_real, inc_imag, back_real, back_imag)
    carry_real, carry_imag = conj_mult(patch_real, patch_imag, back_real, back_imag)
    probe_term = jnp.stack([jnp.sum(carry_real, axis=0), jnp.sum(carry_imag, axis=0)])
    probe_term = jnp.where(layer_index == 0, probe_term, jnp.zeros_like(probe_term))
    lighting = weight[:, None, None] * (probe[0] * probe[0] + probe[1] * probe[1])[None]
    values = jnp.stack([grad_real, grad_imag, lighting], axis=1)
    canvas = jnp.zeros((3, stripe + pattern, columns), jnp.float32)
    canvas = scatter_add(canvas, values, row_offsets, col_offsets)
    rim_rows = passed_along(canvas[:, stripe:], "pos", 1)
    inner = canvas[:, :stripe].at[:, :pattern].add(rim_rows)
    slice_grad = (inner[:2] / (inner[2] + 1.0))[:, None]
    probe_part = lax.psum_scatter(probe_term, "cuts", scatter_dimension=1, tiled=True)
    probe_grad = lax.psum(probe_part, "pos") / math.sqrt(slot_count * across)
    return (slice_grad, probe_grad)


def solution(mesh):
    in_specs = (P(None, "cuts", "pos", None), P(), P("pos", None, None), P(None, "pos"), P("pos"))
    out_specs = (P(None, "cuts", "pos", None), P(None, "cuts", None))
    return jax.shard_map(local, mesh=mesh, in_specs=in_specs, out_specs=out_specs, check_vma=False)
```

profile of v0, /device:TPU:1, one launch (start us, length us, event | category | flops | bytes accessed | tf_op | source)
XLA Modules:
  0.0 877.9 jit_solution(7260552434117524395)
XLA Ops:
  7.2 8.8 %collective-permute-start = (f32[2,128,512]{2,1,0:T(8,128)}, f32[2,128,512]{2,1,0:T(8,128)S(1)}, u32[]{:S(2)}, u32[]{:S(2)}) collective-permute-start(f32[2,128,512]{2,1,0:T(8,128)} %bitcast.387), channel_id=1, source_target_pairs={{4,0},{8,4},{12,8},{16,12},{20,16},{24,20},{28,24},{32,28},{36,32}... | collective-permute-start | bytes 1572872 | tf_op jit(solution)/shard_map/ppermute | solution.py:14
  16.1 37.5 %sine_reduce_fusion = (f32[128,128]{1,0:T(8,128)S(1)}, f32[128,128]{1,0:T(8,128)S(1)}) fusion(s32[128,128]{1,0:T(8,128)S(1)} %add_select_fusion.2, f32[128]{0:T(128)S(1)} %fusion.177), kind=kLoop, calls=%fused_computation.10 | loop fusion | flops 35618816 | bytes 197120 | tf_op jit(solution)/shard_map/reduce_sum | solution.py:30
  53.8 16.0 %while.17 = (s32[]{:T(128)}, f32[2,256,512]{2,1,0:T(8,128)S(1)}, s32[8,3]{0,1:T(4,128)S(1)}, f32[8,2,128,128]{3,2,0,1:T(8,128)S(1)}, s32[]{:T(128)}) while((s32[]{:T(128)}, f32[2,256,512]{2,1,0:T(8,128)S(1)}, s32[8,3]{0,1:T(4,128)S(1)}, f32[8,2,128,128]{3,2,0,1:T(8,128)S(1)}, s32[]{:T(128)}) %tuple.75), condition=%wide.while_cond.1, body=%wide.while_body.1.sunk | while | flops 2 | bytes 262261 | solution.py:97
  54.4 1.4 bitcast_dynamic-update-slice_fusion.2
  56.4 1.4 bitcast_dynamic-update-slice_fusion.2
  58.4 1.4 bitcast_dynamic-update-slice_fusion.2
  60.4 1.4 bitcast_dynamic-update-slice_fusion.2
  62.4 1.4 bitcast_dynamic-update-slice_fusion.2
  64.4 1.4 bitcast_dynamic-update-slice_fusion.2
  66.4 1.4 bitcast_dynamic-update-slice_fusion.2
  68.4 1.4 bitcast_dynamic-update-slice_fusion.2
  76.9 1.3 collective-permute-start.1
  79.2 1.8 collective-permute-start.2
  81.0 8.8 %collective-permute-done.1 = f32[8,128,128]{2,1,0:T(8,128)S(1)} collective-permute-done((f32[8,128,128]{2,1,0:T(8,128)S(1)}, f32[8,128,128]{2,1,0:T(8,128)S(1)}, u32[]{:S(2)}, u32[]{:S(2)}) %collective-permute-start.1) | collective-permute-done | bytes 524320 | tf_op jit(solution)/shard_map/ppermute | solution.py:14
  89.8 10.9 %collective-permute-done.2 = f32[8,128,128]{2,1,0:T(8,128)S(1)} collective-permute-done((f32[8,128,128]{2,1,0:T(8,128)S(1)}, f32[8,128,128]{2,1,0:T(8,128)S(1)}, u32[]{:S(2)}, u32[]{:S(2)}) %collective-permute-start.2) | collective-permute-done | bytes 524320 | tf_op jit(solution)/shard_map/ppermute | solution.py:14
  107.9 3.8 collective-permute-start.3
  112.8 2.1 collective-permute-start.4
  114.9 7.8 collective-permute-done.3
  122.7 11.2 %collective-permute-done.4 = f32[8,128,128]{2,1,0:T(8,128)S(1)} collective-permute-done((f32[8,128,128]{2,1,0:T(8,128)S(1)}, f32[8,128,128]{2,1,0:T(8,128)S(1)}, u32[]{:S(2)}, u32[]{:S(2)}) %collective-permute-start.4) | collective-permute-done | bytes 524320 | tf_op jit(solution)/shard_map/ppermute | solution.py:14
  141.1 4.9 collective-permute-start.6
  147.1 1.7 collective-permute-start.5
  149.4 5.9 collective-permute-done.6
  155.3 11.2 %collective-permute-done.5 = f32[8,128,128]{2,1,0:T(8,128)S(1)} collective-permute-done((f32[8,128,128]{2,1,0:T(8,128)S(1)}, f32[8,128,128]{2,1,0:T(8,128)S(1)}, u32[]{:S(2)}, u32[]{:S(2)}) %collective-permute-start.5) | collective-permute-done | bytes 524320 | tf_op jit(solution)/shard_map/ppermute | solution.py:14
  169.2 1.1 fusion.18
  170.4 1.1 fusion.99
  171.5 1.1 fusion.85
  173.8 1.1 convolution_subtract_fusion.8
  174.9 1.2 subtract_multiply_fusion
  176.2 1.2 fusion.49
  177.3 1.6 fusion.45
  178.9 1.2 fusion.16
  180.1 1.1 fusion.80
  181.2 1.1 fusion.94
  182.4 1.2 fusion.15
  183.5 1.1 fusion.13
  184.7 1.1 fusion.35
  189.8 1.2 fusion.75
  193.0 1.3 collective-permute-start.7
  195.3 1.3 collective-permute-start.8
  196.6 11.7 %collective-permute-done.7 = f32[8,128,128]{2,1,0:T(8,128)S(1)} collective-permute-done((f32[8,128,128]{2,1,0:T(8,128)S(1)}, f32[8,128,128]{2,1,0:T(8,128)S(1)}, u32[]{:S(2)}, u32[]{:S(2)}) %collective-permute-start.7) | collective-permute-done | bytes 524320 | tf_op jit(solution)/shard_map/ppermute | solution.py:14
  208.3 11.2 %collective-permute-done.8 = f32[8,128,128]{2,1,0:T(8,128)S(1)} collective-permute-done((f32[8,128,128]{2,1,0:T(8,128)S(1)}, f32[8,128,128]{2,1,0:T(8,128)S(1)}, u32[]{:S(2)}, u32[]{:S(2)}) %collective-permute-start.8) | collective-permute-done | bytes 524320 | tf_op jit(solution)/shard_map/ppermute | solution.py:14
  226.9 1.3 collective-permute-start.9
  229.2 1.5 collective-permute-start.10
  230.7 8.8 collective-permute-done.9
  239.5 11.2 %collective-permute-done.10 = f32[8,128,128]{2,1,0:T(8,128)S(1)} collective-permute-done((f32[8,128,128]{2,1,0:T(8,128)S(1)}, f32[8,128,128]{2,1,0:T(8,128)S(1)}, u32[]{:S(2)}, u32[]{:S(2)}) %collective-permute-start.10) | collective-permute-done | bytes 524320 | tf_op jit(solution)/shard_map/ppermute | solution.py:14
  257.1 1.8 convolution_subtract_fusion
  258.9 1.3 collective-permute-start.11
  260.2 1.8 convolution_add_fusion
  262.0 1.3 collective-permute-start.12
  263.4 7.5 collective-permute-done.11
  270.9 11.2 %collective-permute-done.12 = f32[8,128,128]{2,1,0:T(8,128)} collective-permute-done((f32[8,128,128]{2,1,0:T(8,128)}, f32[8,128,128]{2,1,0:T(8,128)}, u32[]{:S(2)}, u32[]{:S(2)}) %collective-permute-start.12) | collective-permute-done | bytes 524320 | tf_op jit(solution)/shard_map/ppermute | solution.py:14
  282.1 1.5 fusion.41
  284.1 64.9 %while.16 = (s32[]{:T(128)}, f32[3,256,512]{2,1,0:T(8,128)S(1)}, s32[8]{0:T(128)S(1)}, s32[8]{0:T(128)S(1)}, f32[8,3,128,128]{3,2,0,1:T(8,128)S(1)}, /*index=5*/s32[]{:T(128)}, s32[]{:T(128)}, s32[]{:T(128)}, s32[]{:T(128)}) while((s32[]{:T(128)}, f32[3,256,512]{2,1,0:T(8,128)S(1)}, s32[8]{0:T(128)S(1)}, s32[8]{0:T(128)S(1)}, ...), condition=%wide.region_3.4_spmd, body=%wide.region_2.3_spmd.sunk | while | flops 49160 | bytes 983241 | solution.py:74
  289.3 2.8 dynamic_update_slice.8
  297.4 2.7 dynamic_update_slice.8
  305.3 3.0 dynamic_update_slice.8
  313.5 2.8 dynamic_update_slice.8
  321.6 2.9 dynamic_update_slice.8
  329.7 3.0 dynamic_update_slice.8
  338.0 3.0 dynamic_update_slice.8
  346.2 2.9 dynamic_update_slice.8
  349.1 2.2 collective-permute-start.13
  352.0 25.6 %reduce-scatter.2.cloned.1.call-done = f32[2,32,128]{2,1,0:T(8,128)} async-done(((f32[2,128,128]{2,1,0:T(8,128)}), f32[2,32,128]{2,1,0:T(8,128)}) %reduce-scatter.2.cloned.1.call-update) | async-done | bytes 32784 | tf_op jit(solution)/shard_map/reduce_scatter | solution.py:136
  377.6 491.5 %psum.7 = f32[2,32,128]{2,1,0:T(8,128)S(1)} all-reduce(f32[2,32,128]{2,1,0:T(8,128)} %reduce-scatter.2.cloned.1.call-done), channel_id=1, replica_groups=mesh['pos'=128,'cuts'=4] {'pos'}, use_global_device_ids=true, to_apply=%region_7.8 | all-reduce | flops 8192 | bytes 65536 | tf_op jit(solution)/shard_map/psum | solution.py:137
  (138 shorter events, 68.1 us)
Async XLA Ops:
  7.2 370.5 %reduce-scatter.2.cloned.1.call-start = ((), (), s32[]{:S(2)}) async-start(), calls=%async_computation.1 | async-start | bytes 163840 | tf_op jit(solution)/shard_map/reduce_scatter | solution.py:136
  7.2 46.5 %collective-permute-start = (f32[2,128,512]{2,1,0:T(8,128)}, f32[2,128,512]{2,1,0:T(8,128)S(1)}, u32[]{:S(2)}, u32[]{:S(2)}) collective-permute-start(f32[2,128,512]{2,1,0:T(8,128)} %bitcast.387), channel_id=1, source_target_pairs={{4,0},{8,4},{12,8},{16,12},{20,16},{24,20},{28,24},{32,28},{36,32}... | collective-permute-start | bytes 1572872 | tf_op jit(solution)/shard_map/ppermute | solution.py:14
  16.1 37.6 %copy-start.8 = (s32[2,8]{1,0:T(2,128)S(1)}, s32[2,8]{1,0:T(2,128)}, u32[]{:S(2)}) copy-start(s32[2,8]{1,0:T(2,128)} %param.14) | copy-start | bytes 196
  16.1 37.6 %copy-start.7 = (f32[2,128,128]{2,1,0:T(8,128)S(1)}, f32[2,128,128]{2,1,0:T(8,128)}, u32[]{:S(2)}) copy-start(f32[2,128,128]{2,1,0:T(8,128)} %param.12) | copy-start | bytes 393220
  16.1 37.6 %copy-start.5 = (f32[2,1,128,512]{3,2,1,0:T(8,128)S(1)}, f32[2,1,128,512]{3,2,1,0:T(8,128)}, u32[]{:S(2)}) copy-start(f32[2,1,128,512]{3,2,1,0:T(8,128)} %param.11) | copy-start | bytes 1572868
  76.9 12.9 %collective-permute-start.1 = (f32[8,128,128]{2,1,0:T(8,128)S(1)}, f32[8,128,128]{2,1,0:T(8,128)S(1)}, u32[]{:S(2)}, u32[]{:S(2)}) collective-permute-start(f32[8,128,128]{2,1,0:T(8,128)S(1)} %convolution_subtract_fusion.14), channel_id=1, source_target_pairs={{0,1},{1,2},{2,3},{4,5},{5,6},{6,7},{8,9},{9,10},{10,11},{12,13},{... | collective-permute-start | bytes 1572872 | tf_op jit(solution)/shard_map/ppermute | solution.py:14
  79.2 21.5 %collective-permute-start.2 = (f32[8,128,128]{2,1,0:T(8,128)S(1)}, f32[8,128,128]{2,1,0:T(8,128)S(1)}, u32[]{:S(2)}, u32[]{:S(2)}) collective-permute-start(f32[8,128,128]{2,1,0:T(8,128)S(1)} %convolution_add_fusion.14), channel_id=1, source_target_pairs={{0,1},{1,2},{2,3},{4,5},{5,6},{6,7},{8,9},{9,10},{10,11},{12,13},{... | collective-permute-start | bytes 1572872 | tf_op jit(solution)/shard_map/ppermute | solution.py:14
  89.8 11.0 %copy-start = (f32[8,128,128]{2,1,0:T(8,128)}, f32[8,128,128]{2,1,0:T(8,128)S(1)}, u32[]{:S(2)}) copy-start(f32[8,128,128]{2,1,0:T(8,128)S(1)} %collective-permute-done.1) | copy-start | bytes 1572868
  100.7 1.2 copy-start.2
  107.9 14.8 %collective-permute-start.3 = (f32[8,128,128]{2,1,0:T(8,128)S(1)}, f32[8,128,128]{2,1,0:T(8,128)S(1)}, u32[]{:S(2)}, u32[]{:S(2)}) collective-permute-start(f32[8,128,128]{2,1,0:T(8,128)S(1)} %convolution_subtract_fusion.12), channel_id=1, source_target_pairs={{0,1},{1,2},{2,3},{4,5},{5,6},{6,7},{8,9},{9,10},{10,11},{12,13},{... | collective-permute-start | bytes 1572872 | tf_op jit(solution)/shard_map/ppermute | solution.py:14
  112.8 21.2 %collective-permute-start.4 = (f32[8,128,128]{2,1,0:T(8,128)S(1)}, f32[8,128,128]{2,1,0:T(8,128)S(1)}, u32[]{:S(2)}, u32[]{:S(2)}) collective-permute-start(f32[8,128,128]{2,1,0:T(8,128)S(1)} %convolution_add_fusion.12), channel_id=1, source_target_pairs={{0,1},{1,2},{2,3},{4,5},{5,6},{6,7},{8,9},{9,10},{10,11},{12,13},{... | collective-permute-start | bytes 1572872 | tf_op jit(solution)/shard_map/ppermute | solution.py:14
  122.7 11.4 %copy-start.3 = (f32[8,128,128]{2,1,0:T(8,128)}, f32[8,128,128]{2,1,0:T(8,128)S(1)}, u32[]{:S(2)}) copy-start(f32[8,128,128]{2,1,0:T(8,128)S(1)} %collective-permute-done.3) | copy-start | bytes 1572868
  133.9 1.2 copy-start.4
  140.1 26.4 %copy-start.1 = (f32[8,128,128]{2,1,0:T(8,128)S(1)}, f32[8,128,128]{2,1,0:T(8,128)}, u32[]{:S(2)}) copy-start(f32[8,128,128]{2,1,0:T(8,128)} %copy-done) | copy-start | bytes 1572868
  141.1 14.2 %collective-permute-start.6 = (f32[8,128,128]{2,1,0:T(8,128)S(1)}, f32[8,128,128]{2,1,0:T(8,128)}, u32[]{:S(2)}, u32[]{:S(2)}) collective-permute-start(f32[8,128,128]{2,1,0:T(8,128)S(1)} %convolution_add_fusion.10), channel_id=1, source_target_pairs={{0,1},{1,2},{2,3},{4,5},{5,6},{6,7},{8,9},{9,10},{10,11},{12,13},{... | collective-permute-start | bytes 1572872 | tf_op jit(solution)/shard_map/ppermute | solution.py:14
  147.1 19.5 %collective-permute-start.5 = (f32[8,128,128]{2,1,0:T(8,128)S(1)}, f32[8,128,128]{2,1,0:T(8,128)S(1)}, u32[]{:S(2)}, u32[]{:S(2)}) collective-permute-start(f32[8,128,128]{2,1,0:T(8,128)S(1)} %convolution_subtract_fusion.10), channel_id=1, source_target_pairs={{0,1},{1,2},{2,3},{4,5},{5,6},{6,7},{8,9},{9,10},{10,11},{12,13},{... | collective-permute-start | bytes 1572872 | tf_op jit(solution)/shard_map/ppermute | solution.py:14
  172.6 2.3 copy-start.6
  193.0 15.3 %collective-permute-start.7 = (f32[8,128,128]{2,1,0:T(8,128)S(1)}, f32[8,128,128]{2,1,0:T(8,128)S(1)}, u32[]{:S(2)}, u32[]{:S(2)}) collective-permute-start(f32[8,128,128]{2,1,0:T(8,128)S(1)} %convolution_subtract_fusion.4), channel_id=1, source_target_pairs={{1,0},{2,1},{3,2},{5,4},{6,5},{7,6},{9,8},{10,9},{11,10},{13,12},{... | collective-permute-start | bytes 1572872 | tf_op jit(solution)/shard_map/ppermute | solution.py:14
  195.3 24.2 %collective-permute-start.8 = (f32[8,128,128]{2,1,0:T(8,128)S(1)}, f32[8,128,128]{2,1,0:T(8,128)S(1)}, u32[]{:S(2)}, u32[]{:S(2)}) collective-permute-start(f32[8,128,128]{2,1,0:T(8,128)S(1)} %convolution_add_fusion.4), channel_id=1, source_target_pairs={{1,0},{2,1},{3,2},{5,4},{6,5},{7,6},{9,8},{10,9},{11,10},{13,12},{... | collective-permute-start | bytes 1572872 | tf_op jit(solution)/shard_map/ppermute | solution.py:14
  226.9 12.6 %collective-permute-start.9 = (f32[8,128,128]{2,1,0:T(8,128)S(1)}, f32[8,128,128]{2,1,0:T(8,128)S(1)}, u32[]{:S(2)}, u32[]{:S(2)}) collective-permute-start(f32[8,128,128]{2,1,0:T(8,128)S(1)} %convolution_subtract_fusion.2), channel_id=1, source_target_pairs={{1,0},{2,1},{3,2},{5,4},{6,5},{7,6},{9,8},{10,9},{11,10},{13,12},{... | collective-permute-start | bytes 1572872 | tf_op jit(solution)/shard_map/ppermute | solution.py:14
  229.2 21.5 %collective-permute-start.10 = (f32[8,128,128]{2,1,0:T(8,128)S(1)}, f32[8,128,128]{2,1,0:T(8,128)S(1)}, u32[]{:S(2)}, u32[]{:S(2)}) collective-permute-start(f32[8,128,128]{2,1,0:T(8,128)S(1)} %convolution_add_fusion.2), channel_id=1, source_target_pairs={{1,0},{2,1},{3,2},{5,4},{6,5},{7,6},{9,8},{10,9},{11,10},{13,12},{... | collective-permute-start | bytes 1572872 | tf_op jit(solution)/shard_map/ppermute | solution.py:14
  258.9 12.0 %collective-permute-start.11 = (f32[8,128,128]{2,1,0:T(8,128)}, f32[8,128,128]{2,1,0:T(8,128)}, u32[]{:S(2)}, u32[]{:S(2)}) collective-permute-start(f32[8,128,128]{2,1,0:T(8,128)} %convolution_subtract_fusion), channel_id=1, source_target_pairs={{1,0},{2,1},{3,2},{5,4},{6,5},{7,6},{9,8},{10,9},{11,10},{13,12},{... | collective-permute-start | bytes 1572872 | tf_op jit(solution)/shard_map/ppermute | solution.py:14
  262.0 20.1 %collective-permute-start.12 = (f32[8,128,128]{2,1,0:T(8,128)}, f32[8,128,128]{2,1,0:T(8,128)}, u32[]{:S(2)}, u32[]{:S(2)}) collective-permute-start(f32[8,128,128]{2,1,0:T(8,128)} %convolution_add_fusion), channel_id=1, source_target_pairs={{1,0},{2,1},{3,2},{5,4},{6,5},{7,6},{9,8},{10,9},{11,10},{13,12},{... | collective-permute-start | bytes 1572872 | tf_op jit(solution)/shard_map/ppermute | solution.py:14
  349.1 520.7 %collective-permute-start.13 = (f32[3,128,512]{2,1,0:T(8,128)S(1)}, f32[3,128,512]{2,1,0:T(8,128)S(1)}, u32[]{:S(2)}, u32[]{:S(2)}) collective-permute-start(f32[3,128,512]{2,1,0:T(8,128)S(1)} %slice.60), channel_id=1, source_target_pairs={{0,4},{4,8},{8,12},{12,16},{16,20},{20,24},{24,28},{28,32},{32,36}... | collective-permute-start | bytes 2359304 | tf_op jit(solution)/shard_map/ppermute | solution.py:14
Sparse Core Ops, SparseCore 0:
  352.1 25.4 reduce-scatter.1
where the time goes:
time: 890 us; the launch traced here: 878 us
  blocking collectives  492 us (55%)
  waiting for transfers between devices  143 us (16%)
  matrix products  68.3 us (8%)
  local copies, waits for them, and re-layouts  48.7 us (5%)
  other arithmetic  44.3 us (5%)
  starting transfers between devices  34.6 us (4%)
  loops' own time  31.5 us (4%)
  between operations  15.8 us (2%)
    psum x1, blocking collectives, local(): probe_grad = lax.psum(probe_part, 'pos') / math.sqrt(slot_count * across)  492 us
    ppermute x14, waiting for transfers between devices, passed_along(): return lax.ppermute(block, axis, route)  117 us
    reduce_sum x1, other arithmetic, make_tables(): prop_imag = jnp.mean(jnp.sin(argument), axis=2)  37.5 us
    dot_general x32, matrix products, mat_right(): jnp.einsum('bmk,kn->bmn', batch, table, precision=lax.Precision.HIGHEST)  34.9 us
    ppermute x14, starting transfers between devices, passed_along(): return lax.ppermute(block, axis, route)  34.6 us
    dot_general x32, matrix products, mat_left(): jnp.einsum('mk,bkn->bmn', table, batch, precision=lax.Precision.HIGHEST)  33.4 us
    another operation x1, loops' own time, scatter_add(): return lax.fori_loop(0, values.shape[0], add_one, canvas)  31.3 us
    reduce_scatter x1, waiting for transfers between devices, local(): lax.psum_scatter(probe_term, 'cuts', scatter_dimension=1, tiled=True)  25.6 us
  transfers between devices with their start and end apart: 15, of which 13 were waited for; matrix products, arithmetic and copies ran while one was open for 5% of the time, Pallas kernels for 0%

commit v1 on v0

v1 whole, which is shorter than its diff:
```python
import functools
import math

import jax
import jax.numpy as jnp
import numpy as np
from jax import lax
from jax.experimental import pallas as pl
from jax.experimental.pallas import tpu as pltpu
from jax.sharding import PartitionSpec as P

FRESNEL = 0.7
VMEM = pltpu.CompilerParams(vmem_limit_bytes=48 * 1024 * 1024)


def make_tables(n):
    index = np.arange(n)
    four = np.exp(-2j * math.pi / n * (index[:, None] * index[None, :] % n)) / math.sqrt(n)
    signed = np.where(index < n // 2, index, index - n)
    spacing = (index[:, None] - index[None, :]) % n
    turns = spacing[:, :, None] * index[None, None, :] % n
    phase = FRESNEL * math.pi / n * (signed * signed)
    prop = np.mean(np.exp(1j * (phase[None, None, :] + 2.0 * math.pi / n * turns)), axis=2)
    return four, prop


def split_pair(table):
    whole = np.block([[table.real, table.imag], [-table.imag, table.real]]).astype(np.float32)
    lead = whole.astype(jnp.bfloat16)
    return np.stack([lead, (whole - lead.astype(np.float32)).astype(jnp.bfloat16)])


def table_stack(n):
    four, prop = make_tables(n)
    return np.stack([split_pair(prop), split_pair(prop.conj()), split_pair(four), split_pair(four.conj())])


def parts(x):
    lead = x.astype(jnp.bfloat16)
    return lead, (x - lead.astype(jnp.float32)).astype(jnp.bfloat16)


def dot(a, b):
    return jnp.dot(a, b, preferred_element_type=jnp.float32)


def both_sides(wave, tables, which):
    real, imag = wave
    count, n, _ = real.shape
    whole = jnp.concatenate([real.reshape(count * n, n), imag.reshape(count * n, n)], axis=1)
    lead, trail = parts(whole)
    right_lead, right_trail = tables[which, 0], tables[which, 1]
    mid = dot(lead, right_lead) + (dot(trail, right_lead) + dot(lead, right_trail))
    mid = jnp.concatenate(
        [
            jnp.concatenate([mid[p * n : (p + 1) * n, h * n : (h + 1) * n] for p in range(count)], axis=1)
            for h in range(2)
        ],
        axis=0,
    )
    lead, trail = parts(mid)
    left_lead, left_trail = tables[which ^ 1, 0], tables[which ^ 1, 1]
    out = dot(left_lead, lead) + (dot(left_lead, trail) + dot(left_trail, lead))
    real = jnp.stack([out[:n, p * n : (p + 1) * n] for p in range(count)])
    imag = jnp.stack([out[n:, p * n : (p + 1) * n] for p in range(count)])
    return real, imag


def complex_mult(a, b):
    return a[0] * b[0] - a[1] * b[1], a[0] * b[1] + a[1] * b[0]


def conj_mult(a, b):
    return a[0] * b[0] + a[1] * b[1], a[0] * b[1] - a[1] * b[0]


def spot(info, slot, columns, n):
    row = info[0, slot]
    col = info[1, slot]
    top = pl.multiple_of(row // 8 * 8, 8)
    band = pl.multiple_of(jnp.minimum(col // n * n, columns - 2 * n), n)
    return (pl.ds(top, n + 8), pl.ds(band, 2 * n)), row - top, col - band


def cut_out(box, down, right):
    n = box.shape[1] // 2
    turn = lax.rem(n - right, n)
    lane = lax.broadcasted_iota(jnp.int32, (n + 8, n), 1)
    wide = jnp.where(lane < n - right, pltpu.roll(box[:, :n], turn, axis=1), pltpu.roll(box[:, n:], turn, axis=1))
    groups = pltpu.roll(wide.reshape(n // 8 + 1, 8, n), lax.rem(8 - down, 8), axis=1)
    line = lax.broadcasted_iota(jnp.int32, (n // 8, 8, n), 1)
    return jnp.where(line < 8 - down, groups[:-1], groups[1:]).reshape(n, n)


def placed(value, down, right):
    n = value.shape[0]
    groups = pltpu.roll(value.reshape(n // 8, 8, n), down, axis=1)
    empty = jnp.zeros((1, 8, n), jnp.float32)
    line = lax.broadcasted_iota(jnp.int32, (n // 8 + 1, 8, n), 1)
    tall = jnp.where(
        line >= down, jnp.concatenate([groups, empty], axis=0), jnp.concatenate([empty, groups], axis=0)
    ).reshape(n + 8, n)
    tall = pltpu.roll(tall, lax.rem(right, n), axis=1)
    lane = lax.broadcasted_iota(jnp.int32, (n + 8, n), 1)
    return jnp.concatenate([jnp.where(lane >= right, tall, 0.0), jnp.where(lane < right, tall, 0.0)], axis=1)


def light_kernel(info, probe, inner, rim, canvas):
    n = probe.shape[1]
    slots = info.shape[1]
    stripe, columns = inner.shape
    canvas[...] = jnp.zeros_like(canvas)
    power = probe[0] * probe[0] + probe[1] * probe[1]

    def one(slot, carry):
        at, down, right = spot(info, slot, columns, n)
        canvas[at] = canvas[at] + placed(power, down, right)
        return carry

    lax.fori_loop(0, jnp.minimum(info[2, 0], slots), one, 0)
    inner[...] = canvas[:stripe]
    rim[...] = canvas[stripe:]


def window_kernel(info, own, following, *rest):
    outs, ext = rest[:-1], rest[-1]
    cuts = len(outs)
    stripe, columns = own.shape[1:]
    pair, _, n, _ = outs[0].shape
    me = info[2, 1]
    ext[:, :stripe] = own[...]
    ext[:, stripe:] = following[...]
    for away in range(cuts):
        target = lax.rem(me + away, cuts)
        for which in range(pair):
            at, down, right = spot(info, target + which * cuts, columns, n)
            for part in range(2):
                outs[away][which, part] = cut_out(ext[(part, *at)], down, right)


def wave_kernel(cuts, info, probe, amplitude, tables, *rest):
    arrived, rest = rest[:cuts], rest[cuts:]
    terms, probe_out, rest = rest[:cuts], rest[cuts], rest[cuts + 1 :]
    patch, term, amp, sems = rest
    pair, _, n, _ = arrived[0].shape
    me = info[2, 1]
    live = info[2, 0]
    copies = [
        pltpu.make_async_copy(amplitude.at[me + which * cuts], amp.at[which], sems.at[which]) for which in range(pair)
    ]
    for copy in copies:
        copy.start()
    for away in range(cuts):
        patch[lax.rem(me + cuts - away, cuts)] = arrived[away][...]

    def patch_of(layer):
        return patch[layer, :, 0], patch[layer, :, 1]

    wave = tuple(jnp.broadcast_to(probe[part][None], (pair, n, n)) for part in range(2))
    incident = []
    for layer in range(cuts):
        incident.append(wave)
        wave = complex_mult(wave, patch_of(layer))
        if layer < cuts - 1:
            wave = both_sides(wave, tables, 0)
    far = both_sides(wave, tables, 2)
    for copy in copies:
        copy.wait()
    magnitude = jnp.sqrt(far[0] * far[0] + far[1] * far[1])
    slot = me + cuts * lax.broadcasted_iota(jnp.int32, (pair, n, n), 0)
    weight = (slot < live).astype(jnp.float32)
    factor = weight * (1.0 - amp[...] / jnp.maximum(magnitude, 1.0))
    back = both_sides((factor * far[0], factor * far[1]), tables, 3)
    for layer in range(cuts - 1, -1, -1):
        value = conj_mult(incident[layer], back)
        term[layer, :, 0] = value[0]
        term[layer, :, 1] = value[1]
        carry = conj_mult(patch_of(layer), back)
        if layer > 0:
            back = both_sides(carry, tables, 1)
    for part in range(2):
        probe_out[part] = jnp.sum(carry[part], axis=0)
    for away in range(cuts):
        terms[away][...] = term[lax.rem(me + away, cuts)]


def scatter_kernel(cuts, info, *rest):
    arrived, (inner, rim, canvas) = rest[:cuts], rest[cuts:]
    stripe, columns = inner.shape[1:]
    pair, _, n, _ = arrived[0].shape
    me = info[2, 1]
    canvas[...] = jnp.zeros_like(canvas)
    for away in range(cuts):
        source = lax.rem(me + cuts - away, cuts)
        for which in range(pair):
            at, down, right = spot(info, source + which * cuts, columns, n)
            for part in range(2):
                spread = placed(arrived[away][which, part], down, right)
                canvas[(part, *at)] = canvas[(part, *at)] + spread
    inner[...] = canvas[:, :stripe]
    rim[...] = canvas[:, stripe:]


def along(block, distance):
    devices = range(lax.axis_size("pos"))
    return lax.ppermute(block, "pos", [(i - distance, i) for i in devices if i - distance in devices])


def around(block, distance):
    count = lax.axis_size("cuts")
    return lax.ppermute(block, "cuts", [(i, (i + distance) % count) for i in range(count)])


def sum_over_pos(block):
    count = lax.axis_size("pos")
    step = 1
    while step < count:
        block = block + lax.ppermute(block, "pos", [(i, i ^ step) for i in range(count)])
        step *= 2
    return block


def local(specimen, probe, amplitude, offsets, live):
    n = probe.shape[1]
    stripe, columns = specimen.shape[2:]
    slots = amplitude.shape[0]
    across = lax.axis_size("pos")
    cuts = lax.axis_size("cuts")
    pair = slots // cuts
    me = lax.axis_index("cuts")
    own = specimen[:, 0]
    following = along(own, -1)
    row = offsets[0] - lax.axis_index("pos") * stripe
    extra = jnp.zeros((slots,), jnp.int32).at[0].set(live[0]).at[1].set(me)
    info = jnp.stack([row, offsets[1], extra])
    smem = pl.BlockSpec(memory_space=pltpu.SMEM)
    vmem = pl.BlockSpec(memory_space=pltpu.VMEM)
    hbm = pl.BlockSpec(memory_space=pl.ANY)
    tables = jnp.asarray(table_stack(n))

    light, light_rim = pl.pallas_call(
        light_kernel,
        out_shape=[jax.ShapeDtypeStruct((stripe, columns), jnp.float32)] * 2,
        in_specs=[smem, vmem],
        out_specs=[vmem] * 2,
        scratch_shapes=[pltpu.VMEM((stripe + n, columns), jnp.float32)],
        compiler_params=VMEM,
        name="light",
    )(info, probe)
    light_in = along(light_rim, 1)

    packet = jax.ShapeDtypeStruct((pair, 2, n, n), jnp.float32)
    windows = pl.pallas_call(
        window_kernel,
        out_shape=[packet] * cuts,
        in_specs=[smem, vmem, vmem],
        out_specs=[vmem] * cuts,
        scratch_shapes=[pltpu.VMEM((2, 2 * stripe, columns), jnp.float32)],
        compiler_params=VMEM,
        name="windows",
    )(info, own, following)
    arrived = [windows[0]] + [around(windows[away], away) for away in range(1, cuts)]

    *terms, probe_term = pl.pallas_call(
        functools.partial(wave_kernel, cuts),
        out_shape=[packet] * cuts + [jax.ShapeDtypeStruct((2, n, n), jnp.float32)],
        in_specs=[smem, vmem, hbm, vmem] + [vmem] * cuts,
        out_specs=[vmem] * (cuts + 1),
        scratch_shapes=[
            pltpu.VMEM((cuts, pair, 2, n, n), jnp.float32),
            pltpu.VMEM((cuts, pair, 2, n, n), jnp.float32),
            pltpu.VMEM((pair, n, n), jnp.float32),
            pltpu.SemaphoreType.DMA((pair,)),
        ],
        compiler_params=VMEM,
        name="waves",
    )(info, probe, amplitude, tables, *arrived)
    gathered = [terms[0]] + [around(terms[away], away) for away in range(1, cuts)]

    rows = n // cuts
    probe_part = lax.dynamic_slice_in_dim(probe_term, me * rows, rows, 1)
    for away in range(1, cuts):
        theirs = lax.dynamic_slice_in_dim(probe_term, (me + away) % cuts * rows, rows, 1)
        probe_part = probe_part + around(theirs, away)
    probe_grad = sum_over_pos(probe_part) / math.sqrt(slots * across)

    inner, rim = pl.pallas_call(
        functools.partial(scatter_kernel, cuts),
        out_shape=[jax.ShapeDtypeStruct((2, stripe, columns), jnp.float32)] * 2,
        in_specs=[smem] + [vmem] * cuts,
        out_specs=[vmem] * 2,
        scratch_shapes=[pltpu.VMEM((2, stripe + n, columns), jnp.float32)],
        compiler_params=VMEM,
        name="scatter",
    )(info, *gathered)
    rim_in = along(rim, 1)
    slice_grad = ((inner + rim_in) / (light + light_in + 1.0))[:, None]
    return slice_grad, probe_grad


def solution(mesh):
    in_specs = (P(None, "cuts", "pos", None), P(), P("pos", None, None), P(None, "pos"), P("pos"))
    out_specs = (P(None, "cuts", "pos", None), P(None, "cuts", None))
    return jax.shard_map(local, mesh=mesh, in_specs=in_specs, out_specs=out_specs, check_vma=False)
```

time: 890 us -> 122 us (0.14); the launches traced: 878 us -> 121 us
  blocking collectives: 492 us -> 0 us
  waiting for transfers between devices: 143 us -> 19.1 us
  matrix products: 68.3 us -> 0 us
  starting transfers between devices: 34.6 us -> 86.2 us
  local copies, waits for them, and re-layouts: 48.7 us -> 2.23 us
  other arithmetic: 44.3 us -> 2.4 us
  loops' own time: 31.5 us -> 0 us
  between operations: 15.8 us -> 1.63 us
  Pallas kernels: 0 us -> 9.83 us
    psum x1 -> x0, blocking collectives: 492 us -> none  [local(): probe_grad = lax.psum(probe_part, 'pos') / math.sqrt(slot_count * across)]
    ppermute x14 -> x19, waiting for transfers between devices: 117 us -> 19.1 us  [the longest x9 8.93 us: around(): lax.ppermute(block, 'cuts', [(i, (i + distance) % count) for i in range(c...]
    dot_general x64 -> x0, matrix products: 68.3 us -> none  [the longest x32 34.9 us: mat_right(): jnp.einsum('bmk,kn->bmn', batch, table, precision=lax.Precision.HIGHEST)]
    ppermute x14 -> x19, starting transfers between devices: 34.6 us -> 86.2 us  [the longest x7 37.5 us: sum_over_pos(): lax.ppermute(block, 'pos', [(i, i ^ step) for i in range(count)])]
    reduce_sum x2 -> x0, other arithmetic: 39 us -> none  [the longest x1 37.5 us: make_tables(): prop_imag = jnp.mean(jnp.sin(argument), axis=2)]
    another operation x2 -> x0, loops' own time: 31.5 us -> none  [the longest x1 31.3 us: scatter_add(): return lax.fori_loop(0, values.shape[0], add_one, canvas)]
    reduce_scatter x1 -> x0, waiting for transfers between devices: 25.6 us -> none  [local(): lax.psum_scatter(probe_term, 'cuts', scatter_dimension=1, tiled=True)]
    dynamic_update_slice x8 -> x0, local copies, waits for them, and re-layouts: 23.1 us -> none  [add_one(): lax.dynamic_update_slice(current_canvas, current + values[position], corner)]
  transfers between devices with their start and end apart: 15 -> 19, of which waited for: 13 -> 9; matrix products, arithmetic and copies ran while one was open for 5% -> 1% of each run, Pallas kernels for 0% -> 2%
where the time goes in v1:
time: 122 us; the launch traced here: 121 us
  starting transfers between devices  86.2 us (71%)
  waiting for transfers between devices  19.1 us (16%)
  Pallas kernels  9.83 us (8%)
  other arithmetic  2.4 us (2%)
  local copies, waits for them, and re-layouts  2.23 us (2%)
  between operations  1.63 us (1%)
    ppermute x7, starting transfers between devices, sum_over_pos(): lax.ppermute(block, 'pos', [(i, i ^ step) for i in range(count)])  37.5 us
    ppermute x9, starting transfers between devices, around(): lax.ppermute(block, 'cuts', [(i, (i + distance) % count) for i in range(c...  29 us
    ppermute x3, starting transfers between devices, along(): lax.ppermute(block, 'pos', [(i - distance, i) for i in devices if i - dis...  19.7 us
    ppermute x9, waiting for transfers between devices, around(): lax.ppermute(block, 'cuts', [(i, (i + distance) % count) for i in range(c...  8.93 us
    ppermute x7, waiting for transfers between devices, sum_over_pos(): lax.ppermute(block, 'pos', [(i, i ^ step) for i in range(count)])  8.86 us
    pallas_call x1, Pallas kernels, local(): pl.pallas_call(functools.partial(wave_kernel, cuts), out_shape=[packet] *...  6.19 us
  transfers between devices with their start and end apart: 19, of which 9 were waited for; matrix products, arithmetic and copies ran while one was open for 1% of the time, Pallas kernels for 2%

profile of v1, /device:TPU:1, one launch (start us, length us, event | category | flops | bytes accessed | tf_op | source)
XLA Modules:
  0.0 121.4 jit_solution(14382803416972861415)
XLA Ops:
  0.6 0.0 copy-start
  0.6 8.9 %collective-permute-start = (f32[2,128,512]{2,1,0:T(8,128)}, f32[2,128,512]{2,1,0:T(8,128)S(1)}, u32[]{:S(2)}, u32[]{:S(2)}) collective-permute-start(f32[2,128,512]{2,1,0:T(8,128)} %bitcast.8), channel_id=1, source_target_pairs={{4,0},{8,4},{12,8},{16,12},{20,16},{24,20},{28,24},{32,28},{36,32}... | collective-permute-start | bytes 1572872 | tf_op jit(solution)/shard_map/ppermute | solution.py:206
  10.2 0.1 scatter.12
  10.3 0.8 slice_subtract_fusion
  11.1 1.3 %collective-permute-done.following = f32[2,128,512]{2,1,0:T(8,128)S(1)} collective-permute-done((f32[2,128,512]{2,1,0:T(8,128)}, f32[2,128,512]{2,1,0:T(8,128)S(1)}, u32[]{:S(2)}, u32[]{:S(2)}) %collective-permute-start) | collective-permute-done | bytes 524320 | tf_op jit(solution)/shard_map/ppermute | solution.py:206
  12.4 0.0 copy-start.2
  12.4 1.0 copy-done.2
  13.5 0.0 copy-start.1
  13.5 1.3 %windows.1 = (f32[2,2,128,128]{3,2,1,0:T(8,128)S(1)}, f32[2,2,128,128]{3,2,1,0:T(8,128)S(1)}, f32[2,2,128,128]{3,2,1,0:T(8,128)S(1)}, f32[2,2,128,128]{3,2,1,0:T(8,128)S(1)}) custom-call(s32[3,8]{1,0:T(4,128)S(1)} %pad_add_fusion.info, f32[2,128,512]{2,1,0:T(8,128)S(1)} %bitcast.9, f32[2,128,512]{2,1,0:T(8,128)S(1)} %collective-permute-done.following), custom_call_target="tpu_custom_call" | custom-call | tf_op jit(solution)/shard_map/windows/pallas_call | solution.py:253
  14.8 3.1 %collective-permute-start.1 = (f32[2,2,128,128]{3,2,1,0:T(8,128)S(1)}, f32[2,2,128,128]{3,2,1,0:T(8,128)S(1)}, u32[]{:S(2)}, u32[]{:S(2)}) collective-permute-start(f32[2,2,128,128]{3,2,1,0:T(8,128)S(1)} %get-tuple-element.40), channel_id=1, source_target_pairs={{0,1},{1,2},{2,3},{3,0},{4,5},{5,6},{6,7},{7,4},{8,9},{9,10},{10,1... | collective-permute-start | bytes 786440 | tf_op jit(solution)/shard_map/ppermute | solution.py:211
  17.9 4.4 %collective-permute-start.2 = (f32[2,2,128,128]{3,2,1,0:T(8,128)S(1)}, f32[2,2,128,128]{3,2,1,0:T(8,128)S(1)}, u32[]{:S(2)}, u32[]{:S(2)}) collective-permute-start(f32[2,2,128,128]{3,2,1,0:T(8,128)S(1)} %get-tuple-element.41), channel_id=1, source_target_pairs={{0,2},{1,3},{2,0},{3,1},{4,6},{5,7},{6,4},{7,5},{8,10},{9,11},{10,... | collective-permute-start | bytes 786440 | tf_op jit(solution)/shard_map/ppermute | solution.py:211
  22.3 3.1 %collective-permute-start.3 = (f32[2,2,128,128]{3,2,1,0:T(8,128)S(1)}, f32[2,2,128,128]{3,2,1,0:T(8,128)S(1)}, u32[]{:S(2)}, u32[]{:S(2)}) collective-permute-start(f32[2,2,128,128]{3,2,1,0:T(8,128)S(1)} %get-tuple-element.42), channel_id=1, source_target_pairs={{0,3},{1,0},{2,1},{3,2},{4,7},{5,4},{6,5},{7,6},{8,11},{9,8},{10,9... | collective-permute-start | bytes 786440 | tf_op jit(solution)/shard_map/ppermute | solution.py:211
  25.4 5.8 %collective-permute-done.1.rest_1_ = f32[2,2,128,128]{3,2,1,0:T(8,128)S(1)} collective-permute-done((f32[2,2,128,128]{3,2,1,0:T(8,128)S(1)}, f32[2,2,128,128]{3,2,1,0:T(8,128)S(1)}, u32[]{:S(2)}, u32[]{:S(2)}) %collective-permute-start.1) | collective-permute-done | bytes 262176 | tf_op jit(solution)/shard_map/ppermute | solution.py:211
  31.2 0.0 collective-permute-done.2.rest_2_
  31.2 3.1 %collective-permute-done.3.rest_3_ = f32[2,2,128,128]{3,2,1,0:T(8,128)S(1)} collective-permute-done((f32[2,2,128,128]{3,2,1,0:T(8,128)S(1)}, f32[2,2,128,128]{3,2,1,0:T(8,128)S(1)}, u32[]{:S(2)}, u32[]{:S(2)}) %collective-permute-start.3) | collective-permute-done | bytes 262176 | tf_op jit(solution)/shard_map/ppermute | solution.py:211
  34.3 0.0 copy-done
  34.3 0.0 copy-done.1
  34.3 0.0 copy-start.3
  34.3 1.0 copy-done.3
  35.3 6.2 %waves.1 = (f32[2,2,128,128]{3,2,1,0:T(8,128)S(1)}, f32[2,2,128,128]{3,2,1,0:T(8,128)S(1)}, f32[2,2,128,128]{3,2,1,0:T(8,128)S(1)}, f32[2,2,128,128]{3,2,1,0:T(8,128)S(1)}, f32[2,128,128]{2,1,0:T(8,128)S(1)}) custom-call(s32[3,8]{1,0:T(4,128)S(1)} %pad_add_fusion.info, f32[2,128,128]{2,1,0:T(8,128)S(1)} %copy-done.1, f32[8,128,128]{2,1,0:T(8,128)S(1)} %copy-done.3, ...), custom_call_target="tpu_custom_call" | custom-call | tf_op jit(solution)/shard_map/waves/pallas_call | solution.py:264
  41.6 4.2 %collective-permute-start.11 = (f32[2,32,128]{2,1,0:T(8,128)S(1)}, f32[2,32,128]{2,1,0:T(8,128)S(1)}, u32[]{:S(2)}, u32[]{:S(2)}) collective-permute-start(f32[2,32,128]{2,1,0:T(8,128)S(1)} %get-tuple-element.55), channel_id=1, source_target_pairs={{0,3},{1,0},{2,1},{3,2},{4,7},{5,4},{6,5},{7,6},{8,11},{9,8},{10,9... | collective-permute-start | bytes 98312 | tf_op jit(solution)/shard_map/ppermute | solution.py:211
  45.8 1.9 %collective-permute-start.10 = (f32[2,32,128]{2,1,0:T(8,128)S(1)}, f32[2,32,128]{2,1,0:T(8,128)S(1)}, u32[]{:S(2)}, u32[]{:S(2)}) collective-permute-start(f32[2,32,128]{2,1,0:T(8,128)S(1)} %get-tuple-element.56), channel_id=1, source_target_pairs={{0,2},{1,3},{2,0},{3,1},{4,6},{5,7},{6,4},{7,5},{8,10},{9,11},{10,... | collective-permute-start | bytes 98312 | tf_op jit(solution)/shard_map/ppermute | solution.py:211
  47.7 2.5 %collective-permute-start.9 = (f32[2,32,128]{2,1,0:T(8,128)S(1)}, f32[2,32,128]{2,1,0:T(8,128)S(1)}, u32[]{:S(2)}, u32[]{:S(2)}) collective-permute-start(f32[2,32,128]{2,1,0:T(8,128)S(1)} %get-tuple-element.54), channel_id=1, source_target_pairs={{0,1},{1,2},{2,3},{3,0},{4,5},{5,6},{6,7},{7,4},{8,9},{9,10},{10,1... | collective-permute-start | bytes 98312 | tf_op jit(solution)/shard_map/ppermute | solution.py:211
  50.2 1.3 %light.1 = (f32[128,512]{1,0:T(8,128)S(1)}, f32[128,512]{1,0:T(8,128)S(1)}) custom-call(s32[3,8]{1,0:T(4,128)S(1)} %pad_add_fusion.info, f32[2,128,128]{2,1,0:T(8,128)S(1)} %copy-done.1), custom_call_target="tpu_custom_call" | custom-call | tf_op jit(solution)/shard_map/light/pallas_call | solution.py:241
  51.5 4.1 %collective-permute-start.8 = (f32[128,512]{1,0:T(8,128)S(1)}, f32[128,512]{1,0:T(8,128)S(1)}, u32[]{:S(2)}, u32[]{:S(2)}) collective-permute-start(f32[128,512]{1,0:T(8,128)S(1)} %get-tuple-element.50), channel_id=1, source_target_pairs={{0,4},{4,8},{8,12},{12,16},{16,20},{20,24},{24,28},{28,32},{32,36}... | collective-permute-start | bytes 786440 | tf_op jit(solution)/shard_map/ppermute | solution.py:206
  55.6 3.3 %collective-permute-start.4 = (f32[2,2,128,128]{3,2,1,0:T(8,128)S(1)}, f32[2,2,128,128]{3,2,1,0:T(8,128)S(1)}, u32[]{:S(2)}, u32[]{:S(2)}) collective-permute-start(f32[2,2,128,128]{3,2,1,0:T(8,128)S(1)} %get-tuple-element.44), channel_id=1, source_target_pairs={{0,1},{1,2},{2,3},{3,0},{4,5},{5,6},{6,7},{7,4},{8,9},{9,10},{10,1... | collective-permute-start | bytes 786440 | tf_op jit(solution)/shard_map/ppermute | solution.py:211
  59.0 0.0 collective-permute-done.11
  59.0 4.6 %collective-permute-start.5 = (f32[2,2,128,128]{3,2,1,0:T(8,128)S(1)}, f32[2,2,128,128]{3,2,1,0:T(8,128)S(1)}, u32[]{:S(2)}, u32[]{:S(2)}) collective-permute-start(f32[2,2,128,128]{3,2,1,0:T(8,128)S(1)} %get-tuple-element.45), channel_id=1, source_target_pairs={{0,2},{1,3},{2,0},{3,1},{4,6},{5,7},{6,4},{7,5},{8,10},{9,11},{10,... | collective-permute-start | bytes 786440 | tf_op jit(solution)/shard_map/ppermute | solution.py:211
  63.6 0.0 collective-permute-done.10
  63.6 1.9 %collective-permute-start.6 = (f32[2,2,128,128]{3,2,1,0:T(8,128)S(1)}, f32[2,2,128,128]{3,2,1,0:T(8,128)S(1)}, u32[]{:S(2)}, u32[]{:S(2)}) collective-permute-start(f32[2,2,128,128]{3,2,1,0:T(8,128)S(1)} %get-tuple-element.46), channel_id=1, source_target_pairs={{0,3},{1,0},{2,1},{3,2},{4,7},{5,4},{6,5},{7,6},{8,11},{9,8},{10,9... | collective-permute-start | bytes 786440 | tf_op jit(solution)/shard_map/ppermute | solution.py:211
  65.6 0.0 collective-permute-done.9
  65.6 1.9 %collective-permute-start.12 = (f32[2,32,128]{2,1,0:T(8,128)S(1)}, f32[2,32,128]{2,1,0:T(8,128)S(1)}, u32[]{:S(2)}, u32[]{:S(2)}) collective-permute-start(f32[2,32,128]{2,1,0:T(8,128)S(1)} %add_add_fusion.1), channel_id=1, source_target_pairs={{0,4},{4,0},{8,12},{12,8},{16,20},{20,16},{24,28},{28,24},{32,36},... | collective-permute-start | bytes 98312 | tf_op jit(solution)/shard_map/ppermute | solution.py:218
  67.5 1.2 collective-permute-done.12
  68.7 3.1 %collective-permute-start.13 = (f32[2,32,128]{2,1,0:T(8,128)S(1)}, f32[2,32,128]{2,1,0:T(8,128)S(1)}, u32[]{:S(2)}, u32[]{:S(2)}) collective-permute-start(f32[2,32,128]{2,1,0:T(8,128)S(1)} %add.96), channel_id=1, source_target_pairs={{0,8},{4,12},{8,0},{12,4},{16,24},{20,28},{24,16},{28,20},{32,40},... | collective-permute-start | bytes 98312 | tf_op jit(solution)/shard_map/ppermute | solution.py:218
  71.8 1.5 %collective-permute-done.13 = f32[2,32,128]{2,1,0:T(8,128)S(1)} collective-permute-done((f32[2,32,128]{2,1,0:T(8,128)S(1)}, f32[2,32,128]{2,1,0:T(8,128)S(1)}, u32[]{:S(2)}, u32[]{:S(2)}) %collective-permute-start.13) | collective-permute-done | bytes 32800 | tf_op jit(solution)/shard_map/ppermute | solution.py:218
  73.4 5.9 %collective-permute-start.14 = (f32[2,32,128]{2,1,0:T(8,128)S(1)}, f32[2,32,128]{2,1,0:T(8,128)S(1)}, u32[]{:S(2)}, u32[]{:S(2)}) collective-permute-start(f32[2,32,128]{2,1,0:T(8,128)S(1)} %add.97), channel_id=1, source_target_pairs={{0,16},{4,20},{8,24},{12,28},{16,0},{20,4},{24,8},{28,12},{32,48},... | collective-permute-start | bytes 98312 | tf_op jit(solution)/shard_map/ppermute | solution.py:218
  79.2 1.3 %collective-permute-done.14 = f32[2,32,128]{2,1,0:T(8,128)S(1)} collective-permute-done((f32[2,32,128]{2,1,0:T(8,128)S(1)}, f32[2,32,128]{2,1,0:T(8,128)S(1)}, u32[]{:S(2)}, u32[]{:S(2)}) %collective-permute-start.14) | collective-permute-done | bytes 32800 | tf_op jit(solution)/shard_map/ppermute | solution.py:218
  80.5 6.6 %collective-permute-start.15 = (f32[2,32,128]{2,1,0:T(8,128)S(1)}, f32[2,32,128]{2,1,0:T(8,128)S(1)}, u32[]{:S(2)}, u32[]{:S(2)}) collective-permute-start(f32[2,32,128]{2,1,0:T(8,128)S(1)} %add.98), channel_id=1, source_target_pairs={{0,32},{4,36},{8,40},{12,44},{16,48},{20,52},{24,56},{28,60},{32,0... | collective-permute-start | bytes 98312 | tf_op jit(solution)/shard_map/ppermute | solution.py:218
  87.1 2.0 %collective-permute-done.15 = f32[2,32,128]{2,1,0:T(8,128)S(1)} collective-permute-done((f32[2,32,128]{2,1,0:T(8,128)S(1)}, f32[2,32,128]{2,1,0:T(8,128)S(1)}, u32[]{:S(2)}, u32[]{:S(2)}) %collective-permute-start.15) | collective-permute-done | bytes 32800 | tf_op jit(solution)/shard_map/ppermute | solution.py:218
  89.1 3.7 %collective-permute-start.16 = (f32[2,32,128]{2,1,0:T(8,128)S(1)}, f32[2,32,128]{2,1,0:T(8,128)S(1)}, u32[]{:S(2)}, u32[]{:S(2)}) collective-permute-start(f32[2,32,128]{2,1,0:T(8,128)S(1)} %add.99), channel_id=1, source_target_pairs={{0,64},{4,68},{8,72},{12,76},{16,80},{20,84},{24,88},{28,92},{32,9... | collective-permute-start | bytes 98312 | tf_op jit(solution)/shard_map/ppermute | solution.py:218
  92.8 0.0 collective-permute-done.4.rest_1_
  92.8 0.0 collective-permute-done.5.rest_2_
  92.8 0.0 collective-permute-done.6.rest_3_
  92.8 1.0 scatter.14
  93.9 6.7 %collective-permute-start.7 = (f32[2,128,512]{2,1,0:T(8,128)S(1)}, f32[2,128,512]{2,1,0:T(8,128)S(1)}, u32[]{:S(2)}, u32[]{:S(2)}) collective-permute-start(f32[2,128,512]{2,1,0:T(8,128)S(1)} %get-tuple-element.48), channel_id=1, source_target_pairs={{0,4},{4,8},{8,12},{12,16},{16,20},{20,24},{24,28},{28,32},{32,36}... | collective-permute-start | bytes 1572872 | tf_op jit(solution)/shard_map/ppermute | solution.py:206
  100.6 0.0 collective-permute-done.16
  100.6 6.3 %collective-permute-start.17 = (f32[2,32,128]{2,1,0:T(8,128)S(1)}, f32[2,32,128]{2,1,0:T(8,128)S(1)}, u32[]{:S(2)}, u32[]{:S(2)}) collective-permute-start(f32[2,32,128]{2,1,0:T(8,128)S(1)} %add.100), channel_id=1, source_target_pairs={{0,128},{4,132},{8,136},{12,140},{16,144},{20,148},{24,152},{28,15... | collective-permute-start | bytes 98312 | tf_op jit(solution)/shard_map/ppermute | solution.py:218
  106.9 1.3 %collective-permute-done.17 = f32[2,32,128]{2,1,0:T(8,128)S(1)} collective-permute-done((f32[2,32,128]{2,1,0:T(8,128)S(1)}, f32[2,32,128]{2,1,0:T(8,128)S(1)}, u32[]{:S(2)}, u32[]{:S(2)}) %collective-permute-start.17) | collective-permute-done | bytes 32800 | tf_op jit(solution)/shard_map/ppermute | solution.py:218
  108.2 10.0 %collective-permute-start.18 = (f32[2,32,128]{2,1,0:T(8,128)S(1)}, f32[2,32,128]{2,1,0:T(8,128)S(1)}, u32[]{:S(2)}, u32[]{:S(2)}) collective-permute-start(f32[2,32,128]{2,1,0:T(8,128)S(1)} %add.101), channel_id=1, source_target_pairs={{0,256},{4,260},{8,264},{12,268},{16,272},{20,276},{24,280},{28,28... | collective-permute-start | bytes 98312 | tf_op jit(solution)/shard_map/ppermute | solution.py:218
  118.3 0.0 collective-permute-done.8
  118.3 1.6 %collective-permute-done.18 = f32[2,32,128]{2,1,0:T(8,128)S(1)} collective-permute-done((f32[2,32,128]{2,1,0:T(8,128)S(1)}, f32[2,32,128]{2,1,0:T(8,128)S(1)}, u32[]{:S(2)}, u32[]{:S(2)}) %collective-permute-start.18) | collective-permute-done | bytes 32800 | tf_op jit(solution)/shard_map/ppermute | solution.py:218
  119.9 0.6 add_multiply_fusion
  120.5 0.0 collective-permute-done.7
  120.5 0.9 divide_bitcast_fusion
  (11 shorter events, 0.1 us)
Async XLA Ops:
  0.6 33.7 %copy-start = (bf16[4,2,256,256]{3,2,1,0:T(8,128)(2,1)S(1)}, bf16[4,2,256,256]{3,2,1,0:T(8,128)(2,1)}, u32[]{:S(2)}) copy-start(bf16[4,2,256,256]{3,2,1,0:T(8,128)(2,1)} %constant.94.clone.tables) | copy-start | bytes 3145732
  0.6 11.8 %collective-permute-start = (f32[2,128,512]{2,1,0:T(8,128)}, f32[2,128,512]{2,1,0:T(8,128)S(1)}, u32[]{:S(2)}, u32[]{:S(2)}) collective-permute-start(f32[2,128,512]{2,1,0:T(8,128)} %bitcast.8), channel_id=1, source_target_pairs={{4,0},{8,4},{12,8},{16,12},{20,16},{24,20},{28,24},{32,28},{36,32}... | collective-permute-start | bytes 1572872 | tf_op jit(solution)/shard_map/ppermute | solution.py:206
  12.4 1.0 copy-start.2
  13.5 20.8 %copy-start.1 = (f32[2,128,128]{2,1,0:T(8,128)S(1)}, f32[2,128,128]{2,1,0:T(8,128)}, u32[]{:S(2)}) copy-start(f32[2,128,128]{2,1,0:T(8,128)} %probe.3) | copy-start | bytes 393220
  14.8 16.4 %collective-permute-start.1 = (f32[2,2,128,128]{3,2,1,0:T(8,128)S(1)}, f32[2,2,128,128]{3,2,1,0:T(8,128)S(1)}, u32[]{:S(2)}, u32[]{:S(2)}) collective-permute-start(f32[2,2,128,128]{3,2,1,0:T(8,128)S(1)} %get-tuple-element.40), channel_id=1, source_target_pairs={{0,1},{1,2},{2,3},{3,0},{4,5},{5,6},{6,7},{7,4},{8,9},{9,10},{10,1... | collective-permute-start | bytes 786440 | tf_op jit(solution)/shard_map/ppermute | solution.py:211
  17.9 13.3 %collective-permute-start.2 = (f32[2,2,128,128]{3,2,1,0:T(8,128)S(1)}, f32[2,2,128,128]{3,2,1,0:T(8,128)S(1)}, u32[]{:S(2)}, u32[]{:S(2)}) collective-permute-start(f32[2,2,128,128]{3,2,1,0:T(8,128)S(1)} %get-tuple-element.41), channel_id=1, source_target_pairs={{0,2},{1,3},{2,0},{3,1},{4,6},{5,7},{6,4},{7,5},{8,10},{9,11},{10,... | collective-permute-start | bytes 786440 | tf_op jit(solution)/shard_map/ppermute | solution.py:211
  22.3 12.0 %collective-permute-start.3 = (f32[2,2,128,128]{3,2,1,0:T(8,128)S(1)}, f32[2,2,128,128]{3,2,1,0:T(8,128)S(1)}, u32[]{:S(2)}, u32[]{:S(2)}) collective-permute-start(f32[2,2,128,128]{3,2,1,0:T(8,128)S(1)} %get-tuple-element.42), channel_id=1, source_target_pairs={{0,3},{1,0},{2,1},{3,2},{4,7},{5,4},{6,5},{7,6},{8,11},{9,8},{10,9... | collective-permute-start | bytes 786440 | tf_op jit(solution)/shard_map/ppermute | solution.py:211
  34.3 1.0 copy-start.3
  41.6 17.4 %collective-permute-start.11 = (f32[2,32,128]{2,1,0:T(8,128)S(1)}, f32[2,32,128]{2,1,0:T(8,128)S(1)}, u32[]{:S(2)}, u32[]{:S(2)}) collective-permute-start(f32[2,32,128]{2,1,0:T(8,128)S(1)} %get-tuple-element.55), channel_id=1, source_target_pairs={{0,3},{1,0},{2,1},{3,2},{4,7},{5,4},{6,5},{7,6},{8,11},{9,8},{10,9... | collective-permute-start | bytes 98312 | tf_op jit(solution)/shard_map/ppermute | solution.py:211
  45.8 17.9 %collective-permute-start.10 = (f32[2,32,128]{2,1,0:T(8,128)S(1)}, f32[2,32,128]{2,1,0:T(8,128)S(1)}, u32[]{:S(2)}, u32[]{:S(2)}) collective-permute-start(f32[2,32,128]{2,1,0:T(8,128)S(1)} %get-tuple-element.56), channel_id=1, source_target_pairs={{0,2},{1,3},{2,0},{3,1},{4,6},{5,7},{6,4},{7,5},{8,10},{9,11},{10,... | collective-permute-start | bytes 98312 | tf_op jit(solution)/shard_map/ppermute | solution.py:211
  47.7 17.9 %collective-permute-start.9 = (f32[2,32,128]{2,1,0:T(8,128)S(1)}, f32[2,32,128]{2,1,0:T(8,128)S(1)}, u32[]{:S(2)}, u32[]{:S(2)}) collective-permute-start(f32[2,32,128]{2,1,0:T(8,128)S(1)} %get-tuple-element.54), channel_id=1, source_target_pairs={{0,1},{1,2},{2,3},{3,0},{4,5},{5,6},{6,7},{7,4},{8,9},{9,10},{10,1... | collective-permute-start | bytes 98312 | tf_op jit(solution)/shard_map/ppermute | solution.py:211
  51.5 66.7 %collective-permute-start.8 = (f32[128,512]{1,0:T(8,128)S(1)}, f32[128,512]{1,0:T(8,128)S(1)}, u32[]{:S(2)}, u32[]{:S(2)}) collective-permute-start(f32[128,512]{1,0:T(8,128)S(1)} %get-tuple-element.50), channel_id=1, source_target_pairs={{0,4},{4,8},{8,12},{12,16},{16,20},{20,24},{24,28},{28,32},{32,36}... | collective-permute-start | bytes 786440 | tf_op jit(solution)/shard_map/ppermute | solution.py:206
  55.6 37.1 %collective-permute-start.4 = (f32[2,2,128,128]{3,2,1,0:T(8,128)S(1)}, f32[2,2,128,128]{3,2,1,0:T(8,128)S(1)}, u32[]{:S(2)}, u32[]{:S(2)}) collective-permute-start(f32[2,2,128,128]{3,2,1,0:T(8,128)S(1)} %get-tuple-element.44), channel_id=1, source_target_pairs={{0,1},{1,2},{2,3},{3,0},{4,5},{5,6},{6,7},{7,4},{8,9},{9,10},{10,1... | collective-permute-start | bytes 786440 | tf_op jit(solution)/shard_map/ppermute | solution.py:211
  59.0 33.8 %collective-permute-start.5 = (f32[2,2,128,128]{3,2,1,0:T(8,128)S(1)}, f32[2,2,128,128]{3,2,1,0:T(8,128)S(1)}, u32[]{:S(2)}, u32[]{:S(2)}) collective-permute-start(f32[2,2,128,128]{3,2,1,0:T(8,128)S(1)} %get-tuple-element.45), channel_id=1, source_target_pairs={{0,2},{1,3},{2,0},{3,1},{4,6},{5,7},{6,4},{7,5},{8,10},{9,11},{10,... | collective-permute-start | bytes 786440 | tf_op jit(solution)/shard_map/ppermute | solution.py:211
  63.6 29.2 %collective-permute-start.6 = (f32[2,2,128,128]{3,2,1,0:T(8,128)S(1)}, f32[2,2,128,128]{3,2,1,0:T(8,128)S(1)}, u32[]{:S(2)}, u32[]{:S(2)}) collective-permute-start(f32[2,2,128,128]{3,2,1,0:T(8,128)S(1)} %get-tuple-element.46), channel_id=1, source_target_pairs={{0,3},{1,0},{2,1},{3,2},{4,7},{5,4},{6,5},{7,6},{8,11},{9,8},{10,9... | collective-permute-start | bytes 786440 | tf_op jit(solution)/shard_map/ppermute | solution.py:211
  65.6 3.1 %collective-permute-start.12 = (f32[2,32,128]{2,1,0:T(8,128)S(1)}, f32[2,32,128]{2,1,0:T(8,128)S(1)}, u32[]{:S(2)}, u32[]{:S(2)}) collective-permute-start(f32[2,32,128]{2,1,0:T(8,128)S(1)} %add_add_fusion.1), channel_id=1, source_target_pairs={{0,4},{4,0},{8,12},{12,8},{16,20},{20,16},{24,28},{28,24},{32,36},... | collective-permute-start | bytes 98312 | tf_op jit(solution)/shard_map/ppermute | solution.py:218
  68.7 4.6 %collective-permute-start.13 = (f32[2,32,128]{2,1,0:T(8,128)S(1)}, f32[2,32,128]{2,1,0:T(8,128)S(1)}, u32[]{:S(2)}, u32[]{:S(2)}) collective-permute-start(f32[2,32,128]{2,1,0:T(8,128)S(1)} %add.96), channel_id=1, source_target_pairs={{0,8},{4,12},{8,0},{12,4},{16,24},{20,28},{24,16},{28,20},{32,40},... | collective-permute-start | bytes 98312 | tf_op jit(solution)/shard_map/ppermute | solution.py:218
  73.4 7.2 %collective-permute-start.14 = (f32[2,32,128]{2,1,0:T(8,128)S(1)}, f32[2,32,128]{2,1,0:T(8,128)S(1)}, u32[]{:S(2)}, u32[]{:S(2)}) collective-permute-start(f32[2,32,128]{2,1,0:T(8,128)S(1)} %add.97), channel_id=1, source_target_pairs={{0,16},{4,20},{8,24},{12,28},{16,0},{20,4},{24,8},{28,12},{32,48},... | collective-permute-start | bytes 98312 | tf_op jit(solution)/shard_map/ppermute | solution.py:218
  80.5 8.6 %collective-permute-start.15 = (f32[2,32,128]{2,1,0:T(8,128)S(1)}, f32[2,32,128]{2,1,0:T(8,128)S(1)}, u32[]{:S(2)}, u32[]{:S(2)}) collective-permute-start(f32[2,32,128]{2,1,0:T(8,128)S(1)} %add.98), channel_id=1, source_target_pairs={{0,32},{4,36},{8,40},{12,44},{16,48},{20,52},{24,56},{28,60},{32,0... | collective-permute-start | bytes 98312 | tf_op jit(solution)/shard_map/ppermute | solution.py:218
  89.1 11.5 %collective-permute-start.16 = (f32[2,32,128]{2,1,0:T(8,128)S(1)}, f32[2,32,128]{2,1,0:T(8,128)S(1)}, u32[]{:S(2)}, u32[]{:S(2)}) collective-permute-start(f32[2,32,128]{2,1,0:T(8,128)S(1)} %add.99), channel_id=1, source_target_pairs={{0,64},{4,68},{8,72},{12,76},{16,80},{20,84},{24,88},{28,92},{32,9... | collective-permute-start | bytes 98312 | tf_op jit(solution)/shard_map/ppermute | solution.py:218
  93.9 26.6 %collective-permute-start.7 = (f32[2,128,512]{2,1,0:T(8,128)S(1)}, f32[2,128,512]{2,1,0:T(8,128)S(1)}, u32[]{:S(2)}, u32[]{:S(2)}) collective-permute-start(f32[2,128,512]{2,1,0:T(8,128)S(1)} %get-tuple-element.48), channel_id=1, source_target_pairs={{0,4},{4,8},{8,12},{12,16},{16,20},{20,24},{24,28},{28,32},{32,36}... | collective-permute-start | bytes 1572872 | tf_op jit(solution)/shard_map/ppermute | solution.py:206
  100.6 7.6 %collective-permute-start.17 = (f32[2,32,128]{2,1,0:T(8,128)S(1)}, f32[2,32,128]{2,1,0:T(8,128)S(1)}, u32[]{:S(2)}, u32[]{:S(2)}) collective-permute-start(f32[2,32,128]{2,1,0:T(8,128)S(1)} %add.100), channel_id=1, source_target_pairs={{0,128},{4,132},{8,136},{12,140},{16,144},{20,148},{24,152},{28,15... | collective-permute-start | bytes 98312 | tf_op jit(solution)/shard_map/ppermute | solution.py:218
  108.2 11.7 %collective-permute-start.18 = (f32[2,32,128]{2,1,0:T(8,128)S(1)}, f32[2,32,128]{2,1,0:T(8,128)S(1)}, u32[]{:S(2)}, u32[]{:S(2)}) collective-permute-start(f32[2,32,128]{2,1,0:T(8,128)S(1)} %add.101), channel_id=1, source_target_pairs={{0,256},{4,260},{8,264},{12,268},{16,272},{20,276},{24,280},{28,28... | collective-permute-start | bytes 98312 | tf_op jit(solution)/shard_map/ppermute | solution.py:218

commit v2 on v1

v2 whole, which is shorter than its diff:
```python
import math

import jax
import jax.numpy as jnp
import numpy as np
from jax import lax
from jax.experimental import pallas as pl
from jax.experimental.pallas import tpu as pltpu
from jax.sharding import Mesh
from jax.sharding import PartitionSpec as P

FRESNEL = 0.7
POS = ("z", "y", "core")
VMEM = pltpu.CompilerParams(vmem_limit_bytes=48 * 1024 * 1024)


def make_tables(n):
    index = np.arange(n)
    four = np.exp(-2j * math.pi / n * (index[:, None] * index[None, :] % n)) / math.sqrt(n)
    signed = np.where(index < n // 2, index, index - n)
    spacing = (index[:, None] - index[None, :]) % n
    turns = spacing[:, :, None] * index[None, None, :] % n
    phase = FRESNEL * math.pi / n * (signed * signed)
    prop = np.mean(np.exp(1j * (phase[None, None, :] + 2.0 * math.pi / n * turns)), axis=2)
    return four, prop


def split_pair(table):
    whole = np.block([[table.real, table.imag], [-table.imag, table.real]]).astype(np.float32)
    lead = whole.astype(jnp.bfloat16)
    return np.stack([lead, (whole - lead.astype(np.float32)).astype(jnp.bfloat16)])


def table_stack(n):
    four, prop = make_tables(n)
    return np.stack([split_pair(prop), split_pair(prop.conj()), split_pair(four), split_pair(four.conj())])


def parts(x):
    lead = x.astype(jnp.bfloat16)
    return lead, (x - lead.astype(jnp.float32)).astype(jnp.bfloat16)


def dot(a, b):
    return jnp.dot(a, b, preferred_element_type=jnp.float32)


def both_sides(wave, tables, which):
    real, imag = wave
    count, n, _ = real.shape
    whole = jnp.concatenate([real.reshape(count * n, n), imag.reshape(count * n, n)], axis=1)
    lead, trail = parts(whole)
    right_lead, right_trail = tables[which, 0], tables[which, 1]
    mid = dot(lead, right_lead) + (dot(trail, right_lead) + dot(lead, right_trail))
    mid = jnp.concatenate(
        [
            jnp.concatenate([mid[p * n : (p + 1) * n, h * n : (h + 1) * n] for p in range(count)], axis=1)
            for h in range(2)
        ],
        axis=0,
    )
    lead, trail = parts(mid)
    left_lead, left_trail = tables[which ^ 1, 0], tables[which ^ 1, 1]
    out = dot(left_lead, lead) + (dot(left_lead, trail) + dot(left_trail, lead))
    real = jnp.stack([out[:n, p * n : (p + 1) * n] for p in range(count)])
    imag = jnp.stack([out[n:, p * n : (p + 1) * n] for p in range(count)])
    return real, imag


def complex_mult(a, b):
    return a[0] * b[0] - a[1] * b[1], a[0] * b[1] + a[1] * b[0]


def conj_mult(a, b):
    return a[0] * b[0] + a[1] * b[1], a[0] * b[1] - a[1] * b[0]


def spot(info, slot, columns, n):
    row = info[0, slot]
    col = info[1, slot]
    top = pl.multiple_of(row // 8 * 8, 8)
    band = pl.multiple_of(jnp.minimum(col // n * n, columns - 2 * n), n)
    return (pl.ds(top, n + 8), pl.ds(band, 2 * n)), row - top, col - band


def cut_out(box, down, right):
    n = box.shape[1] // 2
    turn = lax.rem(n - right, n)
    lane = lax.broadcasted_iota(jnp.int32, (n + 8, n), 1)
    wide = jnp.where(lane < n - right, pltpu.roll(box[:, :n], turn, axis=1), pltpu.roll(box[:, n:], turn, axis=1))
    groups = pltpu.roll(wide.reshape(n // 8 + 1, 8, n), lax.rem(8 - down, 8), axis=1)
    line = lax.broadcasted_iota(jnp.int32, (n // 8, 8, n), 1)
    return jnp.where(line < 8 - down, groups[:-1], groups[1:]).reshape(n, n)


def placed(value, down, right):
    n = value.shape[0]
    groups = pltpu.roll(value.reshape(n // 8, 8, n), down, axis=1)
    empty = jnp.zeros((1, 8, n), jnp.float32)
    line = lax.broadcasted_iota(jnp.int32, (n // 8 + 1, 8, n), 1)
    tall = jnp.where(
        line >= down, jnp.concatenate([groups, empty], axis=0), jnp.concatenate([empty, groups], axis=0)
    ).reshape(n + 8, n)
    tall = pltpu.roll(tall, lax.rem(right, n), axis=1)
    lane = lax.broadcasted_iota(jnp.int32, (n + 8, n), 1)
    return jnp.concatenate([jnp.where(lane >= right, tall, 0.0), jnp.where(lane < right, tall, 0.0)], axis=1)


def light_kernel(info, probe, own, inner, rim, copied, canvas, sem):
    copy = pltpu.make_async_copy(own, copied, sem)
    copy.start()
    n = probe.shape[1]
    stripe, columns = inner.shape
    canvas[...] = jnp.zeros_like(canvas)
    power = probe[0] * probe[0] + probe[1] * probe[1]

    def one(slot, carry):
        at, down, right = spot(info, slot, columns, n)
        canvas[at] = canvas[at] + placed(power, down, right)
        return carry

    lax.fori_loop(0, jnp.minimum(info[2, 0], info.shape[1]), one, 0)
    inner[...] = canvas[:stripe]
    rim[...] = canvas[stripe:]
    copy.wait()


def window_kernel(info, own, following, out, ext):
    cuts, pair, _, n, _ = out.shape
    stripe, columns = own.shape[1:]
    ext[:, :stripe] = own[...]
    ext[:, stripe:] = following[...]
    for target in range(cuts):
        for which in range(pair):
            at, down, right = spot(info, target + which * cuts, columns, n)
            for part in range(2):
                out[target, which, part] = cut_out(ext[(part, *at)], down, right)


def wave_kernel(info, probe, amplitude, tables, patch, terms, probe_out, amp, sems):
    cuts, pair, _, n, _ = patch.shape
    me = info[2, 1]
    live = info[2, 0]
    copies = [
        pltpu.make_async_copy(amplitude.at[me + which * cuts], amp.at[which], sems.at[which]) for which in range(pair)
    ]
    for copy in copies:
        copy.start()

    def patch_of(layer):
        return patch[layer, :, 0], patch[layer, :, 1]

    wave = tuple(jnp.broadcast_to(probe[part][None], (pair, n, n)) for part in range(2))
    incident = []
    for layer in range(cuts):
        incident.append(wave)
        wave = complex_mult(wave, patch_of(layer))
        if layer < cuts - 1:
            wave = both_sides(wave, tables, 0)
    far = both_sides(wave, tables, 2)
    for copy in copies:
        copy.wait()
    magnitude = jnp.sqrt(far[0] * far[0] + far[1] * far[1])
    slot = me + cuts * lax.broadcasted_iota(jnp.int32, (pair, n, n), 0)
    weight = (slot < live).astype(jnp.float32)
    factor = weight * (1.0 - amp[...] / jnp.maximum(magnitude, 1.0))
    back = both_sides((factor * far[0], factor * far[1]), tables, 3)
    for layer in range(cuts - 1, -1, -1):
        value = conj_mult(incident[layer], back)
        terms[layer, :, 0] = value[0]
        terms[layer, :, 1] = value[1]
        carry = conj_mult(patch_of(layer), back)
        if layer > 0:
            back = both_sides(carry, tables, 1)
    rows = n // cuts
    for part in range(2):
        total = jnp.sum(carry[part], axis=0)
        for piece in range(probe_out.shape[0]):
            at = piece % cuts * rows
            probe_out[piece, part * rows : (part + 1) * rows] = total[at : at + rows]


def scatter_kernel(info, arrived, light_rim, inner, rim, canvas):
    cuts, pair, _, n, _ = arrived.shape
    stripe, columns = inner.shape[1:]
    canvas[...] = jnp.zeros_like(canvas)
    for source in range(cuts):
        for which in range(pair):
            at, down, right = spot(info, source + which * cuts, columns, n)
            for part in range(2):
                spread = placed(arrived[source, which, part], down, right)
                canvas[(part, *at)] = canvas[(part, *at)] + spread
    inner[...] = canvas[:, :stripe]
    rim[:2] = canvas[:, stripe:]
    rim[2] = light_rim[...]


def along(block, distance):
    devices = range(lax.axis_size(POS))
    return lax.ppermute(block, POS, [(i - distance, i) for i in devices if i - distance in devices])


def swap(block, axes):
    return lax.all_to_all(block, axes, 0, 0)


def sum_over_grid(block, axes):
    count = lax.axis_size(axes)
    rows, columns = block.shape
    part = jnp.sum(swap(block.reshape(count, rows // count, columns), axes), axis=0)
    return swap(jnp.broadcast_to(part[None], (count, *part.shape)), axes).reshape(rows, columns)


def local(specimen, probe, amplitude, offsets, live):
    n = probe.shape[1]
    stripe, columns = specimen.shape[2:]
    slots = amplitude.shape[0]
    across = lax.axis_size(POS)
    cuts = lax.axis_size("cuts")
    pair = slots // cuts
    me = lax.axis_index("cuts")
    own = specimen[:, 0]
    following = along(own, -1)
    row = offsets[0] - lax.axis_index(POS) * stripe
    extra = jnp.zeros((slots,), jnp.int32).at[0].set(live[0]).at[1].set(me)
    info = jnp.stack([row, offsets[1], extra])
    smem = pl.BlockSpec(memory_space=pltpu.SMEM)
    vmem = pl.BlockSpec(memory_space=pltpu.VMEM)
    hbm = pl.BlockSpec(memory_space=pltpu.HBM)
    tables = jnp.asarray(table_stack(n))
    stripe_shape = jax.ShapeDtypeStruct((2, stripe, columns), jnp.float32)
    plane_shape = jax.ShapeDtypeStruct((stripe, columns), jnp.float32)
    packet = jax.ShapeDtypeStruct((cuts, pair, 2, n, n), jnp.float32)

    light, light_rim, own = pl.pallas_call(
        light_kernel,
        out_shape=[plane_shape, plane_shape, stripe_shape],
        in_specs=[smem, vmem, hbm],
        out_specs=[vmem] * 3,
        scratch_shapes=[pltpu.VMEM((stripe + n, columns), jnp.float32), pltpu.SemaphoreType.DMA],
        compiler_params=VMEM,
        name="light",
    )(info, probe, own)

    windows = pl.pallas_call(
        window_kernel,
        out_shape=packet,
        in_specs=[smem, vmem, vmem],
        out_specs=vmem,
        scratch_shapes=[pltpu.VMEM((2, 2 * stripe, columns), jnp.float32)],
        compiler_params=VMEM,
        name="windows",
    )(info, own, following)
    patches = swap(windows, "cuts")

    shares = 2 * cuts
    terms, probe_parts = pl.pallas_call(
        wave_kernel,
        out_shape=[packet, jax.ShapeDtypeStruct((shares, 2 * n // cuts, n), jnp.float32)],
        in_specs=[smem, vmem, hbm, vmem, vmem],
        out_specs=[vmem] * 2,
        scratch_shapes=[pltpu.VMEM((pair, n, n), jnp.float32), pltpu.SemaphoreType.DMA((pair,))],
        compiler_params=VMEM,
        name="waves",
    )(info, probe, amplitude, tables, patches)
    probe_part = jnp.sum(swap(probe_parts, ("core", "cuts")), axis=0)
    gathered = swap(terms, "cuts")

    inner, rim = pl.pallas_call(
        scatter_kernel,
        out_shape=[stripe_shape, jax.ShapeDtypeStruct((3, stripe, columns), jnp.float32)],
        in_specs=[smem, vmem, vmem],
        out_specs=[vmem] * 2,
        scratch_shapes=[pltpu.VMEM((2, stripe + n, columns), jnp.float32)],
        compiler_params=VMEM,
        name="scatter",
    )(info, gathered, light_rim)
    rim_in = along(rim, 1)
    slice_grad = ((inner + rim_in[:2]) / (light + rim_in[2] + 1.0))[:, None]
    probe_grad = sum_over_grid(probe_part, ("z", "y")).reshape(2, n // cuts, n) / math.sqrt(slots * across)
    return slice_grad, probe_grad


def solution(mesh):
    across, cuts = mesh.devices.shape
    y = min(8, across // 2)
    split = Mesh(mesh.devices.reshape(across // 2 // y, y, 2, cuts), ("z", "y", "core", "cuts"))
    in_specs = (P(None, "cuts", POS, None), P(), P(POS, None, None), P(None, POS), P(POS))
    out_specs = (P(None, "cuts", POS, None), P(None, "cuts", None))
    return jax.shard_map(local, mesh=split, in_specs=in_specs, out_specs=out_specs, check_vma=False)
```

time: 122 us -> 114 us (0.934)
  blocking collectives: 0 us -> 85.6 us
  starting transfers between devices: 86.2 us -> 12 us
  waiting for transfers between devices: 19.1 us -> 0.01 us
    all_to_all x0 -> x5, blocking collectives: none -> 85.6 us  [swap(): return lax.all_to_all(block, axes, 0, 0)]
    ppermute x19 -> x2, starting transfers between devices: 86.2 us -> 12 us  [along(): lax.ppermute(block, POS, [(i - distance, i) for i in devices if i - dista...]
    ppermute x19 -> x2, waiting for transfers between devices: 19.1 us -> 0.01 us  [along(): lax.ppermute(block, POS, [(i - distance, i) for i in devices if i - dista...]
    unnamed x8 -> x10, local copies, waits for them, and re-layouts: 2.09 us -> 2.51 us
  transfers between devices with their start and end apart: 19 -> 2, of which waited for: 9 -> 0; matrix products, arithmetic and copies ran while one was open for 1% -> 1% of each run, Pallas kernels for 2% -> 1%
where the time goes in v2:
time: 114 us; the launch traced here: 113 us
  blocking collectives  85.6 us (75%)
  starting transfers between devices  12 us (11%)
  Pallas kernels  9.82 us (9%)
  local copies, waits for them, and re-layouts  2.65 us (2%)
  other arithmetic  1.72 us (2%)
  between operations  1.4 us (1%)
    all_to_all x5, blocking collectives, swap(): return lax.all_to_all(block, axes, 0, 0)  85.6 us
    ppermute x2, starting transfers between devices, along(): lax.ppermute(block, POS, [(i - distance, i) for i in devices if i - dista...  12 us
    pallas_call x1, Pallas kernels, local(): pl.pallas_call(wave_kernel, out_shape=[packet, jax.ShapeDtypeStruct((shar...  6.09 us
    unnamed x10, local copies, waits for them, and re-layouts  2.51 us
  transfers between devices with their start and end apart: 2, of which 0 were waited for; matrix products, arithmetic and copies ran while one was open for 1% of the time, Pallas kernels for 1%

profile of v2, /device:TPU:1, one launch (start us, length us, event | category | flops | bytes accessed | tf_op | source)
XLA Modules:
  0.0 113.2 jit_solution(1273682967929835349)
XLA Ops:
  0.6 8.8 %collective-permute-start = (f32[2,128,512]{2,1,0:T(8,128)}, f32[2,128,512]{2,1,0:T(8,128)S(1)}, u32[]{:S(2)}, u32[]{:S(2)}) collective-permute-start(f32[2,128,512]{2,1,0:T(8,128)} %bitcast.16), channel_id=1, source_target_pairs={{4,0},{8,4},{12,8},{16,12},{20,16},{24,20},{28,24},{32,28},{36,32}... | collective-permute-start | bytes 1572872 | tf_op jit(solution)/shard_map/ppermute | solution.py:200
  10.1 0.0 copy-start.4
  10.1 0.1 scatter.12
  10.2 0.6 copy-done.4
  10.8 0.0 copy-start.1
  10.8 0.9 copy-done.1
  11.7 0.0 copy-start.2
  11.7 1.0 copy-done.2
  12.7 1.4 %light.1 = (f32[128,512]{1,0:T(8,128)S(1)}, f32[128,512]{1,0:T(8,128)S(1)}, f32[2,128,512]{2,1,0:T(8,128)S(1)}) custom-call(s32[3,8]{1,0:T(4,128)S(1)} %pad_add_fusion.info, f32[2,128,128]{2,1,0:T(8,128)S(1)} %copy-done.1, f32[2,128,512]{2,1,0:T(8,128)S(1)} %bitcast.17), custom_call_target="tpu_custom_call" | custom-call | tf_op jit(solution)/shard_map/light/pallas_call | solution.py:235
  14.1 0.0 collective-permute-done.following
  14.1 1.3 %windows.1 = f32[4,2,2,128,128]{4,3,2,1,0:T(8,128)S(1)} custom-call(s32[3,8]{1,0:T(4,128)S(1)} %pad_add_fusion.info, f32[2,128,512]{2,1,0:T(8,128)S(1)} %get-tuple-element.33.own, f32[2,128,512]{2,1,0:T(8,128)S(1)} %collective-permute-done.following), custom_call_target="tpu_custom_call" | custom-call | tf_op jit(solution)/shard_map/windows/pallas_call | solution.py:245
  15.4 0.0 copy-start
  15.4 0.0 copy-start.3
  15.5 18.1 %all_to_all.25.patch = f32[4,2,2,128,128]{4,3,2,1,0:T(8,128)S(1)} all-to-all(f32[4,2,2,128,128]{4,3,2,1,0:T(8,128)S(1)} %windows.1), channel_id=1, replica_groups=mesh['z'=8,'y'=8,'core'=2,'cuts'=4] {'cuts'}, dimensions={0} | all-to-all | bytes 2097152 | tf_op jit(solution)/shard_map/all_to_all | solution.py:204
  33.5 0.0 copy-done
  33.5 0.0 copy-done.3
  33.5 6.1 %waves.1 = (f32[4,2,2,128,128]{4,3,2,1,0:T(8,128)S(1)}, f32[8,64,128]{2,1,0:T(8,128)S(1)}) custom-call(s32[3,8]{1,0:T(4,128)S(1)} %pad_add_fusion.info, f32[2,128,128]{2,1,0:T(8,128)S(1)} %copy-done.1, f32[8,128,128]{2,1,0:T(8,128)S(1)} %copy-done.3, bf16[4,2,256,256]{3,2,1,0:T(8,128)(2,1)S(1)} %copy-done, f32[4,2,2,128,128]{4,3,2,1,0:T(8,128)S(1)} %all_to_all.25.patch), custom_call_target="tpu_custom_call" | custom-call | tf_op jit(solution)/shard_map/waves/pallas_call | solution.py:257
  39.6 17.2 %all_to_all.26.arrived = f32[4,2,2,128,128]{4,3,2,1,0:T(8,128)S(1)} all-to-all(f32[4,2,2,128,128]{4,3,2,1,0:T(8,128)S(1)} %get-tuple-element.34), channel_id=1, replica_groups=mesh['z'=8,'y'=8,'core'=2,'cuts'=4] {'cuts'}, dimensions={0} | all-to-all | bytes 2097152 | tf_op jit(solution)/shard_map/all_to_all | solution.py:204
  56.9 1.1 scatter.14
  58.0 3.2 %collective-permute-start.1 = (f32[3,128,512]{2,1,0:T(8,128)S(1)}, f32[3,128,512]{2,1,0:T(8,128)S(1)}, u32[]{:S(2)}, u32[]{:S(2)}) collective-permute-start(f32[3,128,512]{2,1,0:T(8,128)S(1)} %get-tuple-element.37), channel_id=1, source_target_pairs={{0,4},{4,8},{8,12},{12,16},{16,20},{20,24},{24,28},{28,32},{32,36}... | collective-permute-start | bytes 2359304 | tf_op jit(solution)/shard_map/ppermute | solution.py:200
  61.2 8.9 %all_to_all.27 = f32[8,64,128]{2,1,0:T(8,128)S(1)} all-to-all(f32[8,64,128]{2,1,0:T(8,128)S(1)} %get-tuple-element.39), channel_id=1, replica_groups=mesh['z'=8,'y'=8,'core'=2,'cuts'=4] {'core','cuts'}, dimensions={0} | all-to-all | bytes 524288 | tf_op jit(solution)/shard_map/all_to_all | solution.py:204
  70.1 26.7 %all_to_all.28 = f32[64,1,128]{2,1,0:T(1,128)S(1)} all-to-all(f32[64,1,128]{2,1,0:T(1,128)S(1)} %bitcast.18), channel_id=1, replica_groups=mesh['z'=8,'y'=8,'core'=2,'cuts'=4] {'z','y'}, dimensions={0} | all-to-all | bytes 65536 | tf_op jit(solution)/shard_map/all_to_all | solution.py:204
  96.8 0.1 reduce_sum.19
  96.9 14.6 %all_to_all.29 = f32[64,1,128]{2,1,0:T(1,128)S(1)} all-to-all(f32[64,1,128]{2,1,0:T(1,128)S(1)} %broadcast_in_dim.5), channel_id=1, replica_groups=mesh['z'=8,'y'=8,'core'=2,'cuts'=4] {'z','y'}, dimensions={0} | all-to-all | bytes 65536 | tf_op jit(solution)/shard_map/all_to_all | solution.py:204
  111.5 0.6 broadcast_multiply_fusion
  112.2 0.0 collective-permute-done.1
  112.2 0.9 fusion.1
  (6 shorter events, 0.1 us)
Async XLA Ops:
  0.6 13.5 %collective-permute-start = (f32[2,128,512]{2,1,0:T(8,128)}, f32[2,128,512]{2,1,0:T(8,128)S(1)}, u32[]{:S(2)}, u32[]{:S(2)}) collective-permute-start(f32[2,128,512]{2,1,0:T(8,128)} %bitcast.16), channel_id=1, source_target_pairs={{4,0},{8,4},{12,8},{16,12},{20,16},{24,20},{28,24},{32,28},{36,32}... | collective-permute-start | bytes 1572872 | tf_op jit(solution)/shard_map/ppermute | solution.py:200
  10.1 0.7 copy-start.4
  10.8 0.9 copy-start.1
  11.7 1.0 copy-start.2
  15.4 18.1 %copy-start = (bf16[4,2,256,256]{3,2,1,0:T(8,128)(2,1)S(1)}, bf16[4,2,256,256]{3,2,1,0:T(8,128)(2,1)}, u32[]{:S(2)}) copy-start(bf16[4,2,256,256]{3,2,1,0:T(8,128)(2,1)} %constant.81.clone.tables) | copy-start | bytes 3145732
  15.4 18.1 %copy-start.3 = (f32[8,128,128]{2,1,0:T(8,128)S(1)}, f32[8,128,128]{2,1,0:T(8,128)}, u32[]{:S(2)}) copy-start(f32[8,128,128]{2,1,0:T(8,128)} %amplitude.1) | copy-start | bytes 1572868
  58.0 54.2 %collective-permute-start.1 = (f32[3,128,512]{2,1,0:T(8,128)S(1)}, f32[3,128,512]{2,1,0:T(8,128)S(1)}, u32[]{:S(2)}, u32[]{:S(2)}) collective-permute-start(f32[3,128,512]{2,1,0:T(8,128)S(1)} %get-tuple-element.37), channel_id=1, source_target_pairs={{0,4},{4,8},{8,12},{12,16},{16,20},{20,24},{24,28},{28,32},{32,36}... | collective-permute-start | bytes 2359304 | tf_op jit(solution)/shard_map/ppermute | solution.py:200

commit v3 on v2

--- a/solution.py
+++ b/solution.py
@@ -137,8 +137,9 @@
                 out[target, which, part] = cut_out(ext[(part, *at)], down, right)
 
 
-def wave_kernel(info, probe, amplitude, tables, patch, terms, probe_out, amp, sems):
+def wave_kernel(info, probe, amplitude, tables, patch, *rest):
     cuts, pair, _, n, _ = patch.shape
+    sent, (probe_out, terms, amp, sems) = rest[:cuts], rest[cuts:]
     me = info[2, 1]
     live = info[2, 0]
     copies = [
@@ -172,6 +173,8 @@
         carry = conj_mult(patch_of(layer), back)
         if layer > 0:
             back = both_sides(carry, tables, 1)
+    for away in range(cuts):
+        sent[away][...] = terms[lax.rem(me + away, cuts)]
     rows = n // cuts
     for part in range(2):
         total = jnp.sum(carry[part], axis=0)
@@ -180,15 +183,19 @@
             probe_out[piece, part * rows : (part + 1) * rows] = total[at : at + rows]
 
 
-def scatter_kernel(info, arrived, light_rim, inner, rim, canvas):
-    cuts, pair, _, n, _ = arrived.shape
+def scatter_kernel(info, light_rim, *rest):
+    arrived, (inner, rim, canvas) = rest[:-3], rest[-3:]
+    cuts = len(arrived)
+    pair, _, n, _ = arrived[0].shape
     stripe, columns = inner.shape[1:]
+    me = info[2, 1]
     canvas[...] = jnp.zeros_like(canvas)
-    for source in range(cuts):
+    for away in range(cuts):
+        source = lax.rem(me + cuts - away, cuts)
         for which in range(pair):
             at, down, right = spot(info, source + which * cuts, columns, n)
             for part in range(2):
-                spread = placed(arrived[source, which, part], down, right)
+                spread = placed(arrived[away][which, part], down, right)
                 canvas[(part, *at)] = canvas[(part, *at)] + spread
     inner[...] = canvas[:, :stripe]
     rim[:2] = canvas[:, stripe:]
@@ -200,15 +207,28 @@
     return lax.ppermute(block, POS, [(i - distance, i) for i in devices if i - distance in devices])
 
 
+def around(block, distance):
+    count = lax.axis_size("cuts")
+    return lax.ppermute(block, "cuts", [(i, (i + distance) % count) for i in range(count)])
+
+
 def swap(block, axes):
     return lax.all_to_all(block, axes, 0, 0)
 
 
-def sum_over_grid(block, axes):
+def summed_rows(block, axes):
     count = lax.axis_size(axes)
     rows, columns = block.shape
-    part = jnp.sum(swap(block.reshape(count, rows // count, columns), axes), axis=0)
-    return swap(jnp.broadcast_to(part[None], (count, *part.shape)), axes).reshape(rows, columns)
+    return jnp.sum(swap(block.reshape(count, rows // count, columns), axes), axis=0)
+
+
+def all_rows(part, axes):
+    count = lax.axis_size(axes)
+    return swap(jnp.broadcast_to(part[None], (count, *part.shape)), axes)
+
+
+def after(block, *first):
+    return lax.optimization_barrier((block, *first))[0]
 
 
 def local(specimen, probe, amplitude, offsets, live):
@@ -254,30 +274,38 @@
     patches = swap(windows, "cuts")
 
     shares = 2 * cuts
-    terms, probe_parts = pl.pallas_call(
+    packet = jax.ShapeDtypeStruct((pair, 2, n, n), jnp.float32)
+    *terms, probe_parts = pl.pallas_call(
         wave_kernel,
-        out_shape=[packet, jax.ShapeDtypeStruct((shares, 2 * n // cuts, n), jnp.float32)],
+        out_shape=[packet] * cuts + [jax.ShapeDtypeStruct((shares, 2 * n // cuts, n), jnp.float32)],
         in_specs=[smem, vmem, hbm, vmem, vmem],
-        out_specs=[vmem] * 2,
-        scratch_shapes=[pltpu.VMEM((pair, n, n), jnp.float32), pltpu.SemaphoreType.DMA((pair,))],
+        out_specs=[vmem] * (cuts + 1),
+        scratch_shapes=[
+            pltpu.VMEM((cuts, pair, 2, n, n), jnp.float32),
+            pltpu.VMEM((pair, n, n), jnp.float32),
+            pltpu.SemaphoreType.DMA((pair,)),
+        ],
         compiler_params=VMEM,
         name="waves",
     )(info, probe, amplitude, tables, patches)
     probe_part = jnp.sum(swap(probe_parts, ("core", "cuts")), axis=0)
-    gathered = swap(terms, "cuts")
+    terms = lax.optimization_barrier((*terms, probe_part))[:cuts]
+    gathered = [terms[0]] + [around(terms[away], away) for away in range(1, cuts)]
+
+    probe_rows = summed_rows(probe_part, ("z", "y"))
 
     inner, rim = pl.pallas_call(
         scatter_kernel,
         out_shape=[stripe_shape, jax.ShapeDtypeStruct((3, stripe, columns), jnp.float32)],
-        in_specs=[smem, vmem, vmem],
+        in_specs=[smem] + [vmem] * (cuts + 1),
         out_specs=[vmem] * 2,
         scratch_shapes=[pltpu.VMEM((2, stripe + n, columns), jnp.float32)],
         compiler_params=VMEM,
         name="scatter",
-    )(info, gathered, light_rim)
+    )(after(info, probe_rows), light_rim, *gathered)
     rim_in = along(rim, 1)
     slice_grad = ((inner + rim_in[:2]) / (light + rim_in[2] + 1.0))[:, None]
-    probe_grad = sum_over_grid(probe_part, ("z", "y")).reshape(2, n // cuts, n) / math.sqrt(slots * across)
+    probe_grad = all_rows(after(probe_rows, rim), ("z", "y")).reshape(2, n // cuts, n) / math.sqrt(slots * across)
     return slice_grad, probe_grad
 
 

time: 114 us -> 108 us (0.947)
  blocking collectives: 85.6 us -> 70 us
  starting transfers between devices: 12 us -> 22 us
    all_to_all x5 -> x4, blocking collectives: 85.6 us -> 70 us  [swap(): return lax.all_to_all(block, axes, 0, 0)]
    ppermute x0 -> x3, starting transfers between devices: none -> 8.71 us  [around(): lax.ppermute(block, 'cuts', [(i, (i + distance) % count) for i in range(c...]
    ppermute x2, starting transfers between devices: 12 us -> 13.3 us  [along(): lax.ppermute(block, POS, [(i - distance, i) for i in devices if i - dista...]
  transfers between devices with their start and end apart: 2 -> 5, of which waited for: 0 -> 0; matrix products, arithmetic and copies ran while one was open for 1% -> 1% of each run, Pallas kernels for 1% -> 1%
where the time goes in v3:
time: 108 us; the launch traced here: 107 us
  blocking collectives  70 us (65%)
  starting transfers between devices  22 us (20%)
  Pallas kernels  9.43 us (9%)
  local copies, waits for them, and re-layouts  2.65 us (2%)
  other arithmetic  1.72 us (2%)
  between operations  1.44 us (1%)
    all_to_all x4, blocking collectives, swap(): return lax.all_to_all(block, axes, 0, 0)  70 us
    ppermute x2, starting transfers between devices, along(): lax.ppermute(block, POS, [(i - distance, i) for i in devices if i - dista...  13.3 us
    ppermute x3, starting transfers between devices, around(): lax.ppermute(block, 'cuts', [(i, (i + distance) % count) for i in range(c...  8.71 us
    pallas_call x1, Pallas kernels, local(): pl.pallas_call(wave_kernel, out_shape=[packet] * cuts + [jax.ShapeDtypeSt...  6.22 us
    unnamed x10, local copies, waits for them, and re-layouts  2.51 us
  transfers between devices with their start and end apart: 5, of which 0 were waited for; matrix products, arithmetic and copies ran while one was open for 1% of the time, Pallas kernels for 1%

profile of v3, /device:TPU:1, one launch (start us, length us, event | category | flops | bytes accessed | tf_op | source)
XLA Modules:
  0.0 107.3 jit_solution(10257370969037493591)
XLA Ops:
  0.6 8.8 %collective-permute-start = (f32[2,128,512]{2,1,0:T(8,128)}, f32[2,128,512]{2,1,0:T(8,128)S(1)}, u32[]{:S(2)}, u32[]{:S(2)}) collective-permute-start(f32[2,128,512]{2,1,0:T(8,128)} %bitcast.18), channel_id=1, source_target_pairs={{4,0},{8,4},{12,8},{16,12},{20,16},{24,20},{28,24},{32,28},{36,32}... | collective-permute-start | bytes 1572872 | tf_op jit(solution)/shard_map/ppermute | solution.py:207
  10.1 0.0 copy-start.4
  10.1 0.1 scatter.12
  10.2 0.6 copy-done.4
  10.8 0.0 copy-start.1
  10.8 0.9 copy-done.1
  11.7 0.0 copy-start.2
  11.7 1.0 copy-done.2
  12.7 0.9 light.1
  13.6 0.0 collective-permute-done.following
  13.6 1.3 %windows.1 = f32[4,2,2,128,128]{4,3,2,1,0:T(8,128)S(1)} custom-call(s32[3,8]{1,0:T(4,128)S(1)} %pad_add_fusion.info, f32[2,128,512]{2,1,0:T(8,128)S(1)} %get-tuple-element.42.own, f32[2,128,512]{2,1,0:T(8,128)S(1)} %collective-permute-done.following), custom_call_target="tpu_custom_call" | custom-call | tf_op jit(solution)/shard_map/windows/pallas_call | solution.py:265
  14.9 0.0 copy-start
  14.9 0.0 copy-start.3
  15.0 17.8 %all_to_all.20.patch = f32[4,2,2,128,128]{4,3,2,1,0:T(8,128)S(1)} all-to-all(f32[4,2,2,128,128]{4,3,2,1,0:T(8,128)S(1)} %windows.1), channel_id=1, replica_groups=mesh['z'=8,'y'=8,'core'=2,'cuts'=4] {'cuts'}, dimensions={0} | all-to-all | bytes 2097152 | tf_op jit(solution)/shard_map/all_to_all | solution.py:216
  32.8 0.0 copy-done
  32.8 0.0 copy-done.3
  32.8 6.2 %waves.1 = (f32[2,2,128,128]{3,2,1,0:T(8,128)S(1)}, f32[2,2,128,128]{3,2,1,0:T(8,128)S(1)}, f32[2,2,128,128]{3,2,1,0:T(8,128)S(1)}, f32[2,2,128,128]{3,2,1,0:T(8,128)S(1)}, f32[8,64,128]{2,1,0:T(8,128)S(1)}) custom-call(s32[3,8]{1,0:T(4,128)S(1)} %pad_add_fusion.info, f32[2,128,128]{2,1,0:T(8,128)S(1)} %copy-done.1, f32[8,128,128]{2,1,0:T(8,128)S(1)} %copy-done.3, ...), custom_call_target="tpu_custom_call" | custom-call | tf_op jit(solution)/shard_map/waves/pallas_call | solution.py:278
  39.0 9.4 %all_to_all.21 = f32[8,64,128]{2,1,0:T(8,128)S(1)} all-to-all(f32[8,64,128]{2,1,0:T(8,128)S(1)} %get-tuple-element.43), channel_id=1, replica_groups=mesh['z'=8,'y'=8,'core'=2,'cuts'=4] {'core','cuts'}, dimensions={0} | all-to-all | bytes 524288 | tf_op jit(solution)/shard_map/all_to_all | solution.py:216
  48.4 2.5 %collective-permute-start.1 = (f32[2,2,128,128]{3,2,1,0:T(8,128)S(1)}, f32[2,2,128,128]{3,2,1,0:T(8,128)S(1)}, u32[]{:S(2)}, u32[]{:S(2)}) collective-permute-start(f32[2,2,128,128]{3,2,1,0:T(8,128)S(1)} %get-tuple-element.51), channel_id=1, source_target_pairs={{0,1},{1,2},{2,3},{3,0},{4,5},{5,6},{6,7},{7,4},{8,9},{9,10},{10,1... | collective-permute-start | bytes 786440 | tf_op jit(solution)/shard_map/ppermute | solution.py:212
  50.9 3.3 %collective-permute-start.2 = (f32[2,2,128,128]{3,2,1,0:T(8,128)S(1)}, f32[2,2,128,128]{3,2,1,0:T(8,128)S(1)}, u32[]{:S(2)}, u32[]{:S(2)}) collective-permute-start(f32[2,2,128,128]{3,2,1,0:T(8,128)S(1)} %get-tuple-element.52), channel_id=1, source_target_pairs={{0,2},{1,3},{2,0},{3,1},{4,6},{5,7},{6,4},{7,5},{8,10},{9,11},{10,... | collective-permute-start | bytes 786440 | tf_op jit(solution)/shard_map/ppermute | solution.py:212
  54.3 2.9 %collective-permute-start.3 = (f32[2,2,128,128]{3,2,1,0:T(8,128)S(1)}, f32[2,2,128,128]{3,2,1,0:T(8,128)S(1)}, u32[]{:S(2)}, u32[]{:S(2)}) collective-permute-start(f32[2,2,128,128]{3,2,1,0:T(8,128)S(1)} %get-tuple-element.53), channel_id=1, source_target_pairs={{0,3},{1,0},{2,1},{3,2},{4,7},{5,4},{6,5},{7,6},{8,11},{9,8},{10,9... | collective-permute-start | bytes 786440 | tf_op jit(solution)/shard_map/ppermute | solution.py:212
  57.1 26.6 %all_to_all.22 = f32[64,1,128]{2,1,0:T(1,128)S(1)} all-to-all(f32[64,1,128]{2,1,0:T(1,128)S(1)} %bitcast.20), channel_id=1, replica_groups=mesh['z'=8,'y'=8,'core'=2,'cuts'=4] {'z','y'}, dimensions={0} | all-to-all | bytes 65536 | tf_op jit(solution)/shard_map/all_to_all | solution.py:216
  83.7 0.1 reduce_sum.21
  83.8 0.0 collective-permute-done.1.rest_1_
  83.8 0.0 collective-permute-done.2.rest_2_
  83.8 0.0 collective-permute-done.3.rest_3_
  83.8 1.0 scatter.14
  84.9 4.5 %collective-permute-start.4 = (f32[3,128,512]{2,1,0:T(8,128)S(1)}, f32[3,128,512]{2,1,0:T(8,128)S(1)}, u32[]{:S(2)}, u32[]{:S(2)}) collective-permute-start(f32[3,128,512]{2,1,0:T(8,128)S(1)} %get-tuple-element.55), channel_id=1, source_target_pairs={{0,4},{4,8},{8,12},{12,16},{16,20},{20,24},{24,28},{28,32},{32,36}... | collective-permute-start | bytes 2359304 | tf_op jit(solution)/shard_map/ppermute | solution.py:207
  89.4 16.2 %all_to_all.23 = f32[64,1,128]{2,1,0:T(1,128)S(1)} all-to-all(f32[64,1,128]{2,1,0:T(1,128)S(1)} %broadcast_in_dim.14), channel_id=1, replica_groups=mesh['z'=8,'y'=8,'core'=2,'cuts'=4] {'z','y'}, dimensions={0} | all-to-all | bytes 65536 | tf_op jit(solution)/shard_map/all_to_all | solution.py:216
  105.7 0.6 broadcast_multiply_fusion
  106.3 0.0 collective-permute-done.4
  106.4 0.9 fusion.1
  (6 shorter events, 0.1 us)
Async XLA Ops:
  0.6 13.0 %collective-permute-start = (f32[2,128,512]{2,1,0:T(8,128)}, f32[2,128,512]{2,1,0:T(8,128)S(1)}, u32[]{:S(2)}, u32[]{:S(2)}) collective-permute-start(f32[2,128,512]{2,1,0:T(8,128)} %bitcast.18), channel_id=1, source_target_pairs={{4,0},{8,4},{12,8},{16,12},{20,16},{24,20},{28,24},{32,28},{36,32}... | collective-permute-start | bytes 1572872 | tf_op jit(solution)/shard_map/ppermute | solution.py:207
  10.1 0.7 copy-start.4
  10.8 0.9 copy-start.1
  11.7 1.0 copy-start.2
  14.9 17.9 %copy-start = (bf16[4,2,256,256]{3,2,1,0:T(8,128)(2,1)S(1)}, bf16[4,2,256,256]{3,2,1,0:T(8,128)(2,1)}, u32[]{:S(2)}) copy-start(bf16[4,2,256,256]{3,2,1,0:T(8,128)(2,1)} %constant.81.clone.tables) | copy-start | bytes 3145732
  14.9 17.9 %copy-start.3 = (f32[8,128,128]{2,1,0:T(8,128)S(1)}, f32[8,128,128]{2,1,0:T(8,128)}, u32[]{:S(2)}) copy-start(f32[8,128,128]{2,1,0:T(8,128)} %amplitude.1) | copy-start | bytes 1572868
  48.4 35.4 %collective-permute-start.1 = (f32[2,2,128,128]{3,2,1,0:T(8,128)S(1)}, f32[2,2,128,128]{3,2,1,0:T(8,128)S(1)}, u32[]{:S(2)}, u32[]{:S(2)}) collective-permute-start(f32[2,2,128,128]{3,2,1,0:T(8,128)S(1)} %get-tuple-element.51), channel_id=1, source_target_pairs={{0,1},{1,2},{2,3},{3,0},{4,5},{5,6},{6,7},{7,4},{8,9},{9,10},{10,1... | collective-permute-start | bytes 786440 | tf_op jit(solution)/shard_map/ppermute | solution.py:212
  50.9 32.9 %collective-permute-start.2 = (f32[2,2,128,128]{3,2,1,0:T(8,128)S(1)}, f32[2,2,128,128]{3,2,1,0:T(8,128)S(1)}, u32[]{:S(2)}, u32[]{:S(2)}) collective-permute-start(f32[2,2,128,128]{3,2,1,0:T(8,128)S(1)} %get-tuple-element.52), channel_id=1, source_target_pairs={{0,2},{1,3},{2,0},{3,1},{4,6},{5,7},{6,4},{7,5},{8,10},{9,11},{10,... | collective-permute-start | bytes 786440 | tf_op jit(solution)/shard_map/ppermute | solution.py:212
  54.3 29.6 %collective-permute-start.3 = (f32[2,2,128,128]{3,2,1,0:T(8,128)S(1)}, f32[2,2,128,128]{3,2,1,0:T(8,128)S(1)}, u32[]{:S(2)}, u32[]{:S(2)}) collective-permute-start(f32[2,2,128,128]{3,2,1,0:T(8,128)S(1)} %get-tuple-element.53), channel_id=1, source_target_pairs={{0,3},{1,0},{2,1},{3,2},{4,7},{5,4},{6,5},{7,6},{8,11},{9,8},{10,9... | collective-permute-start | bytes 786440 | tf_op jit(solution)/shard_map/ppermute | solution.py:212
  84.9 21.5 %collective-permute-start.4 = (f32[3,128,512]{2,1,0:T(8,128)S(1)}, f32[3,128,512]{2,1,0:T(8,128)S(1)}, u32[]{:S(2)}, u32[]{:S(2)}) collective-permute-start(f32[3,128,512]{2,1,0:T(8,128)S(1)} %get-tuple-element.55), channel_id=1, source_target_pairs={{0,4},{4,8},{8,12},{12,16},{16,20},{20,24},{24,28},{28,32},{32,36}... | collective-permute-start | bytes 2359304 | tf_op jit(solution)/shard_map/ppermute | solution.py:207

commit v4 on v3

--- a/solution.py
+++ b/solution.py
@@ -1,3 +1,4 @@
+import functools
 import math
 
 import jax
@@ -11,7 +12,7 @@
 
 FRESNEL = 0.7
 POS = ("z", "y", "core")
-VMEM = pltpu.CompilerParams(vmem_limit_bytes=48 * 1024 * 1024)
+VMEM = pltpu.CompilerParams(vmem_limit_bytes=16 * 1024 * 1024)
 
 
 def make_tables(n):
@@ -47,24 +48,19 @@
 
 def both_sides(wave, tables, which):
     real, imag = wave
-    count, n, _ = real.shape
-    whole = jnp.concatenate([real.reshape(count * n, n), imag.reshape(count * n, n)], axis=1)
-    lead, trail = parts(whole)
+    n = real.shape[1]
     right_lead, right_trail = tables[which, 0], tables[which, 1]
-    mid = dot(lead, right_lead) + (dot(trail, right_lead) + dot(lead, right_trail))
-    mid = jnp.concatenate(
-        [
-            jnp.concatenate([mid[p * n : (p + 1) * n, h * n : (h + 1) * n] for p in range(count)], axis=1)
-            for h in range(2)
-        ],
-        axis=0,
-    )
-    lead, trail = parts(mid)
     left_lead, left_trail = tables[which ^ 1, 0], tables[which ^ 1, 1]
-    out = dot(left_lead, lead) + (dot(left_lead, trail) + dot(left_trail, lead))
-    real = jnp.stack([out[:n, p * n : (p + 1) * n] for p in range(count)])
-    imag = jnp.stack([out[n:, p * n : (p + 1) * n] for p in range(count)])
-    return real, imag
+    halves = []
+    for p in range(real.shape[0]):
+        lead, trail = parts(jnp.concatenate([real[p], imag[p]], axis=1))
+        mid = dot(lead, right_lead) + (dot(trail, right_lead) + dot(lead, right_trail))
+        halves.append(parts(jnp.concatenate([mid[:, :n], mid[:, n:]], axis=0)))
+    outs = []
+    for lead, trail in halves:
+        both = dot(left_lead, jnp.concatenate([lead, trail], axis=1))
+        outs.append(both[:, :n] + (both[:, n:] + dot(left_trail, lead)))
+    return jnp.stack([out[:n] for out in outs]), jnp.stack([out[n:] for out in outs])
 
 
 def complex_mult(a, b):
@@ -106,23 +102,30 @@
     return jnp.concatenate([jnp.where(lane >= right, tall, 0.0), jnp.where(lane < right, tall, 0.0)], axis=1)
 
 
-def light_kernel(info, probe, own, inner, rim, copied, canvas, sem):
-    copy = pltpu.make_async_copy(own, copied, sem)
-    copy.start()
+def stage_kernel(own, probe, own_copy, probe_copy):
+    own_copy[...] = own[...]
+    probe_copy[...] = probe[...]
+
+
+def light_kernel(info, former, probe, light, canvas):
     n = probe.shape[1]
-    stripe, columns = inner.shape
-    canvas[...] = jnp.zeros_like(canvas)
+    stripe, columns = light.shape
     power = probe[0] * probe[0] + probe[1] * probe[1]
 
-    def one(slot, carry):
-        at, down, right = spot(info, slot, columns, n)
-        canvas[at] = canvas[at] + placed(power, down, right)
-        return carry
-
-    lax.fori_loop(0, jnp.minimum(info[2, 0], info.shape[1]), one, 0)
-    inner[...] = canvas[:stripe]
-    rim[...] = canvas[stripe:]
-    copy.wait()
+    def fill(source):
+        canvas[...] = jnp.zeros_like(canvas)
+
+        def one(slot, carry):
+            at, down, right = spot(source, slot, columns, n)
+            canvas[at] = canvas[at] + placed(power, down, right)
+            return carry
+
+        lax.fori_loop(0, jnp.minimum(source[2, 0], source.shape[1]), one, 0)
+
+    fill(former)
+    light[...] = canvas[stripe:]
+    fill(info)
+    light[...] += canvas[:stripe]
 
 
 def window_kernel(info, own, following, out, ext):
@@ -137,7 +140,7 @@
                 out[target, which, part] = cut_out(ext[(part, *at)], down, right)
 
 
-def wave_kernel(info, probe, amplitude, tables, patch, *rest):
+def wave_kernel(scale, info, probe, amplitude, tables, patch, *rest):
     cuts, pair, _, n, _ = patch.shape
     sent, (probe_out, terms, amp, sems) = rest[:cuts], rest[cuts:]
     me = info[2, 1]
@@ -176,14 +179,15 @@
     for away in range(cuts):
         sent[away][...] = terms[lax.rem(me + away, cuts)]
     rows = n // cuts
-    for part in range(2):
-        total = jnp.sum(carry[part], axis=0)
-        for piece in range(probe_out.shape[0]):
-            at = piece % cuts * rows
-            probe_out[piece, part * rows : (part + 1) * rows] = total[at : at + rows]
-
-
-def scatter_kernel(info, light_rim, *rest):
+    share = probe_out.shape[1]
+    total = [jnp.sum(carry[part], axis=0) * scale for part in range(2)]
+    for cut in range(cuts):
+        block = jnp.concatenate([total[part][cut * rows : (cut + 1) * rows] for part in range(2)], axis=0)
+        for group in range(2 * rows // share):
+            probe_out[group * cuts + cut] = block[group * share : (group + 1) * share]
+
+
+def scatter_kernel(info, *rest):
     arrived, (inner, rim, canvas) = rest[:-3], rest[-3:]
     cuts = len(arrived)
     pair, _, n, _ = arrived[0].shape
@@ -198,8 +202,14 @@
                 spread = placed(arrived[away][which, part], down, right)
                 canvas[(part, *at)] = canvas[(part, *at)] + spread
     inner[...] = canvas[:, :stripe]
-    rim[:2] = canvas[:, stripe:]
-    rim[2] = light_rim[...]
+    rim[...] = canvas[:, stripe:]
+
+
+def final_kernel(inner, rim, light, rows, slice_grad, probe_grad):
+    whole = light[...] + 1.0
+    for part in range(2):
+        slice_grad[part, 0] = (inner[part] + rim[part]) / whole
+    probe_grad[...] = rows[...].reshape(probe_grad.shape)
 
 
 def along(block, distance):
@@ -216,15 +226,8 @@
     return lax.all_to_all(block, axes, 0, 0)
 
 
-def summed_rows(block, axes):
-    count = lax.axis_size(axes)
-    rows, columns = block.shape
-    return jnp.sum(swap(block.reshape(count, rows // count, columns), axes), axis=0)
-
-
-def all_rows(part, axes):
-    count = lax.axis_size(axes)
-    return swap(jnp.broadcast_to(part[None], (count, *part.shape)), axes)
+def copies(block, axes):
+    return swap(jnp.broadcast_to(block[None], (lax.axis_size(axes), *block.shape)), axes)
 
 
 def after(block, *first):
@@ -252,15 +255,23 @@
     plane_shape = jax.ShapeDtypeStruct((stripe, columns), jnp.float32)
     packet = jax.ShapeDtypeStruct((cuts, pair, 2, n, n), jnp.float32)
 
-    light, light_rim, own = pl.pallas_call(
+    own, probe = pl.pallas_call(
+        stage_kernel,
+        out_shape=[stripe_shape, jax.ShapeDtypeStruct(probe.shape, jnp.float32)],
+        in_specs=[vmem] * 2,
+        out_specs=[vmem] * 2,
+        compiler_params=VMEM,
+        name="stage",
+    )(own, probe)
+    light = pl.pallas_call(
         light_kernel,
-        out_shape=[plane_shape, plane_shape, stripe_shape],
-        in_specs=[smem, vmem, hbm],
-        out_specs=[vmem] * 3,
-        scratch_shapes=[pltpu.VMEM((stripe + n, columns), jnp.float32), pltpu.SemaphoreType.DMA],
+        out_shape=plane_shape,
+        in_specs=[smem, smem, vmem],
+        out_specs=vmem,
+        scratch_shapes=[pltpu.VMEM((stripe + n, columns), jnp.float32)],
         compiler_params=VMEM,
         name="light",
-    )(info, probe, own)
+    )(info, along(info, 1), probe)
 
     windows = pl.pallas_call(
         window_kernel,
@@ -270,14 +281,14 @@
         scratch_shapes=[pltpu.VMEM((2, 2 * stripe, columns), jnp.float32)],
         compiler_params=VMEM,
         name="windows",
-    )(info, own, following)
+    )(after(info, light), own, following)
     patches = swap(windows, "cuts")
 
-    shares = 2 * cuts
+    shares = lax.axis_size(("z", "cuts"))
     packet = jax.ShapeDtypeStruct((pair, 2, n, n), jnp.float32)
     *terms, probe_parts = pl.pallas_call(
-        wave_kernel,
-        out_shape=[packet] * cuts + [jax.ShapeDtypeStruct((shares, 2 * n // cuts, n), jnp.float32)],
+        functools.partial(wave_kernel, 1.0 / math.sqrt(slots * across)),
+        out_shape=[packet] * cuts + [jax.ShapeDtypeStruct((shares, 2 * n // shares, n), jnp.float32)],
         in_specs=[smem, vmem, hbm, vmem, vmem],
         out_specs=[vmem] * (cuts + 1),
         scratch_shapes=[
@@ -288,24 +299,32 @@
         compiler_params=VMEM,
         name="waves",
     )(info, probe, amplitude, tables, patches)
-    probe_part = jnp.sum(swap(probe_parts, ("core", "cuts")), axis=0)
-    terms = lax.optimization_barrier((*terms, probe_part))[:cuts]
+    probe_rows = jnp.sum(swap(probe_parts, ("z", "cuts")), axis=0)
     gathered = [terms[0]] + [around(terms[away], away) for away in range(1, cuts)]
-
-    probe_rows = summed_rows(probe_part, ("z", "y"))
+    probe_rows = jnp.sum(copies(probe_rows, ("y", "core")), axis=0)
 
     inner, rim = pl.pallas_call(
         scatter_kernel,
-        out_shape=[stripe_shape, jax.ShapeDtypeStruct((3, stripe, columns), jnp.float32)],
-        in_specs=[smem] + [vmem] * (cuts + 1),
+        out_shape=[stripe_shape] * 2,
+        in_specs=[smem] + [vmem] * cuts,
         out_specs=[vmem] * 2,
         scratch_shapes=[pltpu.VMEM((2, stripe + n, columns), jnp.float32)],
         compiler_params=VMEM,
         name="scatter",
-    )(after(info, probe_rows), light_rim, *gathered)
+    )(after(info, probe_rows), *gathered)
     rim_in = along(rim, 1)
-    slice_grad = ((inner + rim_in[:2]) / (light + rim_in[2] + 1.0))[:, None]
-    probe_grad = all_rows(after(probe_rows, rim), ("z", "y")).reshape(2, n // cuts, n) / math.sqrt(slots * across)
+    probe_rows = copies(after(probe_rows, rim), "z")
+    slice_grad, probe_grad = pl.pallas_call(
+        final_kernel,
+        out_shape=[
+            jax.ShapeDtypeStruct((2, 1, stripe, columns), jnp.float32),
+            jax.ShapeDtypeStruct((2, n // cuts, n), jnp.float32),
+        ],
+        in_specs=[vmem] * 4,
+        out_specs=[vmem] * 2,
+        compiler_params=VMEM,
+        name="final",
+    )(inner, rim_in, light, probe_rows)
     return slice_grad, probe_grad
 
 

time: 108 us -> 95.6 us (0.89)
  blocking collectives: 70 us -> 53.2 us
  starting transfers between devices: 22 us -> 27.9 us
  other arithmetic: 1.72 us -> 0.07 us
    all_to_all x4 -> x3, blocking collectives: 70 us -> 53.2 us  [swap(): return lax.all_to_all(block, axes, 0, 0)]
    all_to_all x0 -> x1, starting transfers between devices: none -> 4.4 us  [swap(): return lax.all_to_all(block, axes, 0, 0)]
    ppermute x3, starting transfers between devices: 8.71 us -> 10.5 us  [around(): lax.ppermute(block, 'cuts', [(i, (i + distance) % count) for i in range(c...]
    pallas_call x3 -> x5, Pallas kernels: 8.15 us -> 8.6 us  [the longest x1 5.18 us: local(): pl.pallas_call(functools.partial(wave_kernel, 1.0 / math.sqrt(slots * acr...]
    ppermute x2 -> x3, starting transfers between devices: 13.3 us -> 13 us  [along(): lax.ppermute(block, POS, [(i - distance, i) for i in devices if i - dista...]
  transfers between devices with their start and end apart: 5 -> 7, of which waited for: 0 -> 0; matrix products, arithmetic and copies ran while one was open for 1% -> 0% of each run, Pallas kernels for 1% -> 2%
where the time goes in v4:
time: 95.6 us; the launch traced here: 95.1 us
  blocking collectives  53.2 us (56%)
  starting transfers between devices  27.9 us (29%)
  Pallas kernels  9.87 us (10%)
  local copies, waits for them, and re-layouts  2.64 us (3%)
  between operations  1.47 us (2%)
    all_to_all x3, blocking collectives, swap(): return lax.all_to_all(block, axes, 0, 0)  53.2 us
    ppermute x3, starting transfers between devices, along(): lax.ppermute(block, POS, [(i - distance, i) for i in devices if i - dista...  13 us
    ppermute x3, starting transfers between devices, around(): lax.ppermute(block, 'cuts', [(i, (i + distance) % count) for i in range(c...  10.5 us
    pallas_call x1, Pallas kernels, local(): pl.pallas_call(functools.partial(wave_kernel, 1.0 / math.sqrt(slots * acr...  5.18 us
    all_to_all x1, starting transfers between devices, swap(): return lax.all_to_all(block, axes, 0, 0)  4.4 us
    unnamed x10, local copies, waits for them, and re-layouts  2.52 us
  transfers between devices with their start and end apart: 7, of which 0 were waited for; matrix products, arithmetic and copies ran while one was open for 0% of the time, Pallas kernels for 2%

profile of v4, /device:TPU:1, one launch (start us, length us, event | category | flops | bytes accessed | tf_op | source)
XLA Modules:
  0.0 95.1 jit_solution(5591635440414184683)
XLA Ops:
  0.6 8.8 %collective-permute-start.1 = (f32[2,128,512]{2,1,0:T(8,128)}, f32[2,128,512]{2,1,0:T(8,128)S(1)}, u32[]{:S(2)}, u32[]{:S(2)}) collective-permute-start(f32[2,128,512]{2,1,0:T(8,128)} %bitcast.4), channel_id=1, source_target_pairs={{4,0},{8,4},{12,8},{16,12},{20,16},{24,20},{28,24},{32,28},{36,32}... | collective-permute-start | bytes 1572872 | tf_op jit(solution)/shard_map/ppermute | solution.py:217
  10.1 0.0 copy-start.4
  10.1 0.1 scatter.12
  10.2 0.6 copy-done.4
  10.8 1.9 %collective-permute-start = (s32[3,8]{1,0:T(4,128)S(1)}, s32[3,8]{1,0:T(4,128)S(1)}, u32[]{:S(2)}, u32[]{:S(2)}) collective-permute-start(s32[3,8]{1,0:T(4,128)S(1)} %pad_add_fusion.info), channel_id=1, source_target_pairs={{0,4},{4,8},{8,12},{12,16},{16,20},{20,24},{24,28},{28,32},{32,36}... | collective-permute-start | bytes 296 | tf_op jit(solution)/shard_map/ppermute | solution.py:217
  12.7 0.0 copy-start.1
  12.7 1.0 %copy-done.1 = f32[2,1,128,512]{3,2,1,0:T(8,128)S(1)} copy-done((f32[2,1,128,512]{3,2,1,0:T(8,128)S(1)}, f32[2,1,128,512]{3,2,1,0:T(8,128)}, u32[]{:S(2)}) %copy-start.1) | copy-done | bytes 524312
  13.8 0.0 copy-start.3
  13.8 0.9 copy-done.3
  14.7 0.0 collective-permute-done.former
  14.7 1.4 %light.1 = f32[128,512]{1,0:T(8,128)S(1)} custom-call(s32[3,8]{1,0:T(4,128)S(1)} %pad_add_fusion.info, s32[3,8]{1,0:T(4,128)S(1)} %collective-permute-done.former, f32[2,128,128]{2,1,0:T(8,128)S(1)} %get-tuple-element.38.probe), custom_call_target="tpu_custom_call" | custom-call | tf_op jit(solution)/shard_map/light/pallas_call | solution.py:266
  16.2 0.0 collective-permute-done.1.following
  16.2 1.3 %windows.1 = f32[4,2,2,128,128]{4,3,2,1,0:T(8,128)S(1)} custom-call(s32[3,8]{1,0:T(4,128)S(1)} %pad_add_fusion.info, f32[2,128,512]{2,1,0:T(8,128)S(1)} %get-tuple-element.40.own, f32[2,128,512]{2,1,0:T(8,128)S(1)} %collective-permute-done.1.following), custom_call_target="tpu_custom_call" | custom-call | tf_op jit(solution)/shard_map/windows/pallas_call | solution.py:276
  17.4 0.0 copy-start
  17.5 0.0 copy-start.2
  17.5 17.5 %all_to_all.20.patch = f32[4,2,2,128,128]{4,3,2,1,0:T(8,128)S(1)} all-to-all(f32[4,2,2,128,128]{4,3,2,1,0:T(8,128)S(1)} %windows.1), channel_id=1, replica_groups=mesh['z'=8,'y'=8,'core'=2,'cuts'=4] {'cuts'}, dimensions={0} | all-to-all | bytes 2097152 | tf_op jit(solution)/shard_map/all_to_all | solution.py:226
  35.0 0.0 copy-done
  35.0 0.0 copy-done.2
  35.0 5.2 %waves.1 = (f32[2,2,128,128]{3,2,1,0:T(8,128)S(1)}, f32[2,2,128,128]{3,2,1,0:T(8,128)S(1)}, f32[2,2,128,128]{3,2,1,0:T(8,128)S(1)}, f32[2,2,128,128]{3,2,1,0:T(8,128)S(1)}, f32[32,8,128]{2,1,0:T(8,128)}) custom-call(s32[3,8]{1,0:T(4,128)S(1)} %pad_add_fusion.info, f32[2,128,128]{2,1,0:T(8,128)S(1)} %get-tuple-element.38.probe, f32[8,128,128]{2,1,0:T(8,128)S(1)} %copy-done.2, ...), custom_call_target="tpu_custom_call" | custom-call | tf_op jit(solution)/shard_map/waves/pallas_call | solution.py:289
  40.2 4.4 %all-to-all-start.1 = ((f32[32,8,128]{2,1,0:T(8,128)}), f32[32,8,128]{2,1,0:T(8,128)S(1)}, u32[]{:S(2)}, u32[]{:S(2)}) async-start(f32[32,8,128]{2,1,0:T(8,128)} %get-tuple-element.41), calls=%async_computation.1 | async-start | bytes 262144 | tf_op jit(solution)/shard_map/all_to_all | solution.py:226
  44.6 3.1 %collective-permute-start.2 = (f32[2,2,128,128]{3,2,1,0:T(8,128)S(1)}, f32[2,2,128,128]{3,2,1,0:T(8,128)S(1)}, u32[]{:S(2)}, u32[]{:S(2)}) collective-permute-start(f32[2,2,128,128]{3,2,1,0:T(8,128)S(1)} %get-tuple-element.44), channel_id=1, source_target_pairs={{0,1},{1,2},{2,3},{3,0},{4,5},{5,6},{6,7},{7,4},{8,9},{9,10},{10,1... | collective-permute-start | bytes 786440 | tf_op jit(solution)/shard_map/ppermute | solution.py:222
  47.7 4.3 %collective-permute-start.3 = (f32[2,2,128,128]{3,2,1,0:T(8,128)S(1)}, f32[2,2,128,128]{3,2,1,0:T(8,128)S(1)}, u32[]{:S(2)}, u32[]{:S(2)}) collective-permute-start(f32[2,2,128,128]{3,2,1,0:T(8,128)S(1)} %get-tuple-element.45), channel_id=1, source_target_pairs={{0,2},{1,3},{2,0},{3,1},{4,6},{5,7},{6,4},{7,5},{8,10},{9,11},{10,... | collective-permute-start | bytes 786440 | tf_op jit(solution)/shard_map/ppermute | solution.py:222
  52.0 3.1 %collective-permute-start.4 = (f32[2,2,128,128]{3,2,1,0:T(8,128)S(1)}, f32[2,2,128,128]{3,2,1,0:T(8,128)S(1)}, u32[]{:S(2)}, u32[]{:S(2)}) collective-permute-start(f32[2,2,128,128]{3,2,1,0:T(8,128)S(1)} %get-tuple-element.46), channel_id=1, source_target_pairs={{0,3},{1,0},{2,1},{3,2},{4,7},{5,4},{6,5},{7,6},{8,11},{9,8},{10,9... | collective-permute-start | bytes 786440 | tf_op jit(solution)/shard_map/ppermute | solution.py:222
  55.1 0.0 all-to-all-done.1
  55.2 21.5 %all_to_all.21 = f32[16,8,128]{2,1,0:T(8,128)S(1)} all-to-all(f32[16,8,128]{2,1,0:T(8,128)S(1)} %broadcast_in_dim.4), channel_id=1, replica_groups=mesh['z'=8,'y'=8,'core'=2,'cuts'=4] {'y','core'}, dimensions={0} | all-to-all | bytes 131072 | tf_op jit(solution)/shard_map/all_to_all | solution.py:226
  76.7 0.0 collective-permute-done.2.rest_1_
  76.7 0.0 collective-permute-done.3.rest_2_
  76.7 0.0 collective-permute-done.4.rest_3_
  76.8 1.0 %scatter.14 = (f32[2,128,512]{2,1,0:T(8,128)S(1)}, f32[2,128,512]{2,1,0:T(8,128)S(1)}) custom-call(s32[3,8]{1,0:T(4,128)S(1)} %pad_add_fusion.info, f32[2,2,128,128]{3,2,1,0:T(8,128)S(1)} %get-tuple-element.43.rest_0_, f32[2,2,128,128]{3,2,1,0:T(8,128)S(1)} %collective-permute-done.2.rest_1_, f32[2,2,128,128]{3,2,1,0:T(8,128)S(1)} %collective-permute-done.3.rest_2_, ...), custom_call_target="tpu_custom_call" | custom-call | tf_op jit(solution)/shard_map/scatter/pallas_call | solution.py:306
  77.8 2.3 %collective-permute-start.5 = (f32[2,128,512]{2,1,0:T(8,128)S(1)}, f32[2,128,512]{2,1,0:T(8,128)S(1)}, u32[]{:S(2)}, u32[]{:S(2)}) collective-permute-start(f32[2,128,512]{2,1,0:T(8,128)S(1)} %get-tuple-element.48), channel_id=1, source_target_pairs={{0,4},{4,8},{8,12},{12,16},{16,20},{20,24},{24,28},{28,32},{32,36}... | collective-permute-start | bytes 1572872 | tf_op jit(solution)/shard_map/ppermute | solution.py:217
  80.1 14.1 %all_to_all.22.rows = f32[8,8,128]{2,1,0:T(8,128)S(1)} all-to-all(f32[8,8,128]{2,1,0:T(8,128)S(1)} %broadcast_in_dim.5), channel_id=1, replica_groups=mesh['z'=8,'y'=8,'core'=2,'cuts'=4] {'z'}, dimensions={0} | all-to-all | bytes 65536 | tf_op jit(solution)/shard_map/all_to_all | solution.py:226
  94.2 0.0 collective-permute-done.5.rim
  94.2 0.9 final.1
  (8 shorter events, 0.1 us)
Async XLA Ops:
  0.6 15.5 %collective-permute-start.1 = (f32[2,128,512]{2,1,0:T(8,128)}, f32[2,128,512]{2,1,0:T(8,128)S(1)}, u32[]{:S(2)}, u32[]{:S(2)}) collective-permute-start(f32[2,128,512]{2,1,0:T(8,128)} %bitcast.4), channel_id=1, source_target_pairs={{4,0},{8,4},{12,8},{16,12},{20,16},{24,20},{28,24},{32,28},{36,32}... | collective-permute-start | bytes 1572872 | tf_op jit(solution)/shard_map/ppermute | solution.py:217
  10.1 0.7 copy-start.4
  10.8 3.9 %collective-permute-start = (s32[3,8]{1,0:T(4,128)S(1)}, s32[3,8]{1,0:T(4,128)S(1)}, u32[]{:S(2)}, u32[]{:S(2)}) collective-permute-start(s32[3,8]{1,0:T(4,128)S(1)} %pad_add_fusion.info), channel_id=1, source_target_pairs={{0,4},{4,8},{8,12},{12,16},{16,20},{20,24},{24,28},{28,32},{32,36}... | collective-permute-start | bytes 296 | tf_op jit(solution)/shard_map/ppermute | solution.py:217
  12.7 1.0 %copy-start.1 = (f32[2,1,128,512]{3,2,1,0:T(8,128)S(1)}, f32[2,1,128,512]{3,2,1,0:T(8,128)}, u32[]{:S(2)}) copy-start(f32[2,1,128,512]{3,2,1,0:T(8,128)} %param.10) | copy-start | bytes 1572868
  13.8 0.9 copy-start.3
  17.4 17.5 %copy-start = (bf16[4,2,256,256]{3,2,1,0:T(8,128)(2,1)S(1)}, bf16[4,2,256,256]{3,2,1,0:T(8,128)(2,1)}, u32[]{:S(2)}) copy-start(bf16[4,2,256,256]{3,2,1,0:T(8,128)(2,1)} %constant.76.clone.tables) | copy-start | bytes 3145732
  17.5 17.5 %copy-start.2 = (f32[8,128,128]{2,1,0:T(8,128)S(1)}, f32[8,128,128]{2,1,0:T(8,128)}, u32[]{:S(2)}) copy-start(f32[8,128,128]{2,1,0:T(8,128)} %amplitude.1) | copy-start | bytes 1572868
  40.2 15.0 %all-to-all-start.1 = ((f32[32,8,128]{2,1,0:T(8,128)}), f32[32,8,128]{2,1,0:T(8,128)S(1)}, u32[]{:S(2)}, u32[]{:S(2)}) async-start(f32[32,8,128]{2,1,0:T(8,128)} %get-tuple-element.41), calls=%async_computation.1 | async-start | bytes 262144 | tf_op jit(solution)/shard_map/all_to_all | solution.py:226
  44.6 32.2 %collective-permute-start.2 = (f32[2,2,128,128]{3,2,1,0:T(8,128)S(1)}, f32[2,2,128,128]{3,2,1,0:T(8,128)S(1)}, u32[]{:S(2)}, u32[]{:S(2)}) collective-permute-start(f32[2,2,128,128]{3,2,1,0:T(8,128)S(1)} %get-tuple-element.44), channel_id=1, source_target_pairs={{0,1},{1,2},{2,3},{3,0},{4,5},{5,6},{6,7},{7,4},{8,9},{9,10},{10,1... | collective-permute-start | bytes 786440 | tf_op jit(solution)/shard_map/ppermute | solution.py:222
  47.7 29.0 %collective-permute-start.3 = (f32[2,2,128,128]{3,2,1,0:T(8,128)S(1)}, f32[2,2,128,128]{3,2,1,0:T(8,128)S(1)}, u32[]{:S(2)}, u32[]{:S(2)}) collective-permute-start(f32[2,2,128,128]{3,2,1,0:T(8,128)S(1)} %get-tuple-element.45), channel_id=1, source_target_pairs={{0,2},{1,3},{2,0},{3,1},{4,6},{5,7},{6,4},{7,5},{8,10},{9,11},{10,... | collective-permute-start | bytes 786440 | tf_op jit(solution)/shard_map/ppermute | solution.py:222
  52.0 24.7 %collective-permute-start.4 = (f32[2,2,128,128]{3,2,1,0:T(8,128)S(1)}, f32[2,2,128,128]{3,2,1,0:T(8,128)S(1)}, u32[]{:S(2)}, u32[]{:S(2)}) collective-permute-start(f32[2,2,128,128]{3,2,1,0:T(8,128)S(1)} %get-tuple-element.46), channel_id=1, source_target_pairs={{0,3},{1,0},{2,1},{3,2},{4,7},{5,4},{6,5},{7,6},{8,11},{9,8},{10,9... | collective-permute-start | bytes 786440 | tf_op jit(solution)/shard_map/ppermute | solution.py:222
  77.8 16.4 %collective-permute-start.5 = (f32[2,128,512]{2,1,0:T(8,128)S(1)}, f32[2,128,512]{2,1,0:T(8,128)S(1)}, u32[]{:S(2)}, u32[]{:S(2)}) collective-permute-start(f32[2,128,512]{2,1,0:T(8,128)S(1)} %get-tuple-element.48), channel_id=1, source_target_pairs={{0,4},{4,8},{8,12},{12,16},{16,20},{20,24},{24,28},{28,32},{32,36}... | collective-permute-start | bytes 1572872 | tf_op jit(solution)/shard_map/ppermute | solution.py:217

commit v5 on v4

--- a/solution.py
+++ b/solution.py
@@ -255,6 +255,7 @@
     plane_shape = jax.ShapeDtypeStruct((stripe, columns), jnp.float32)
     packet = jax.ShapeDtypeStruct((cuts, pair, 2, n, n), jnp.float32)
 
+    former = along(info, 1)
     own, probe = pl.pallas_call(
         stage_kernel,
         out_shape=[stripe_shape, jax.ShapeDtypeStruct(probe.shape, jnp.float32)],
@@ -263,16 +264,6 @@
         compiler_params=VMEM,
         name="stage",
     )(own, probe)
-    light = pl.pallas_call(
-        light_kernel,
-        out_shape=plane_shape,
-        in_specs=[smem, smem, vmem],
-        out_specs=vmem,
-        scratch_shapes=[pltpu.VMEM((stripe + n, columns), jnp.float32)],
-        compiler_params=VMEM,
-        name="light",
-    )(info, along(info, 1), probe)
-
     windows = pl.pallas_call(
         window_kernel,
         out_shape=packet,
@@ -281,7 +272,7 @@
         scratch_shapes=[pltpu.VMEM((2, 2 * stripe, columns), jnp.float32)],
         compiler_params=VMEM,
         name="windows",
-    )(after(info, light), own, following)
+    )(info, own, following)
     patches = swap(windows, "cuts")
 
     shares = lax.axis_size(("z", "cuts"))
@@ -300,6 +291,16 @@
         name="waves",
     )(info, probe, amplitude, tables, patches)
     probe_rows = jnp.sum(swap(probe_parts, ("z", "cuts")), axis=0)
+    later = after(info, probe_rows)
+    light = pl.pallas_call(
+        light_kernel,
+        out_shape=plane_shape,
+        in_specs=[smem, smem, vmem],
+        out_specs=vmem,
+        scratch_shapes=[pltpu.VMEM((stripe + n, columns), jnp.float32)],
+        compiler_params=VMEM,
+        name="light",
+    )(later, former, probe)
     gathered = [terms[0]] + [around(terms[away], away) for away in range(1, cuts)]
     probe_rows = jnp.sum(copies(probe_rows, ("y", "core")), axis=0)
 
@@ -311,7 +312,7 @@
         scratch_shapes=[pltpu.VMEM((2, stripe + n, columns), jnp.float32)],
         compiler_params=VMEM,
         name="scatter",
-    )(after(info, probe_rows), *gathered)
+    )(after(info, probe_rows, light), *gathered)
     rim_in = along(rim, 1)
     probe_rows = copies(after(probe_rows, rim), "z")
     slice_grad, probe_grad = pl.pallas_call(

time: 95.6 us -> 95.9 us (level)
  blocking collectives: 53.2 us -> 32.1 us
  starting transfers between devices: 27.9 us -> 45.7 us
  waiting for transfers between devices: 0.02 us -> 2.46 us
    all_to_all x3 -> x2, blocking collectives: 53.2 us -> 32.1 us  [swap(): return lax.all_to_all(block, axes, 0, 0)]
    all_to_all x1 -> x2, starting transfers between devices: 4.4 us -> 20.5 us  [swap(): return lax.all_to_all(block, axes, 0, 0)]
    ppermute x3, starting transfers between devices: 13 us -> 14.7 us  [along(): lax.ppermute(block, POS, [(i - distance, i) for i in devices if i - dista...]
    all_to_all x1 -> x2, waiting for transfers between devices: 0.01 us -> 1.74 us  [swap(): return lax.all_to_all(block, axes, 0, 0)]
  transfers between devices with their start and end apart: 7 -> 8, of which waited for: 0 -> 2; matrix products, arithmetic and copies ran while one was open for 0% -> 1% of each run, Pallas kernels for 2% -> 2%
where the time goes in v5:
time: 95.9 us; the launch traced here: 95.3 us
  starting transfers between devices  45.7 us (48%)
  blocking collectives  32.1 us (33%)
  Pallas kernels  10.3 us (11%)
  local copies, waits for them, and re-layouts  3.27 us (3%)
  waiting for transfers between devices  2.46 us (3%)
  between operations  1.48 us (2%)
    all_to_all x2, blocking collectives, swap(): return lax.all_to_all(block, axes, 0, 0)  32.1 us
    all_to_all x2, starting transfers between devices, swap(): return lax.all_to_all(block, axes, 0, 0)  20.5 us
    ppermute x3, starting transfers between devices, along(): lax.ppermute(block, POS, [(i - distance, i) for i in devices if i - dista...  14.7 us
    ppermute x3, starting transfers between devices, around(): lax.ppermute(block, 'cuts', [(i, (i + distance) % count) for i in range(c...  10.5 us
    pallas_call x1, Pallas kernels, local(): pl.pallas_call(functools.partial(wave_kernel, 1.0 / math.sqrt(slots * acr...  5.2 us
    unnamed x10, local copies, waits for them, and re-layouts  2.51 us
  transfers between devices with their start and end apart: 8, of which 2 were waited for; matrix products, arithmetic and copies ran while one was open for 1% of the time, Pallas kernels for 2%

profile of v5, /device:TPU:1, one launch (start us, length us, event | category | flops | bytes accessed | tf_op | source)
XLA Modules:
  0.0 95.3 jit_solution(962088032073758084)
XLA Ops:
  0.6 8.8 %collective-permute-start = (f32[2,128,512]{2,1,0:T(8,128)}, f32[2,128,512]{2,1,0:T(8,128)S(1)}, u32[]{:S(2)}, u32[]{:S(2)}) collective-permute-start(f32[2,128,512]{2,1,0:T(8,128)} %bitcast.4), channel_id=1, source_target_pairs={{4,0},{8,4},{12,8},{16,12},{20,16},{24,20},{28,24},{32,28},{36,32}... | collective-permute-start | bytes 1572872 | tf_op jit(solution)/shard_map/ppermute | solution.py:217
  10.1 0.0 copy-start.1
  10.1 1.0 %copy-done.1 = f32[2,1,128,512]{3,2,1,0:T(8,128)S(1)} copy-done((f32[2,1,128,512]{3,2,1,0:T(8,128)S(1)}, f32[2,1,128,512]{3,2,1,0:T(8,128)}, u32[]{:S(2)}) %copy-start.1) | copy-done | bytes 524312
  11.1 0.0 copy-start.3
  11.1 0.9 copy-done.3
  12.1 0.0 copy-start.4
  12.1 0.1 scatter.12
  12.2 0.6 copy-done.4
  12.8 0.0 collective-permute-done.following
  12.8 1.3 %windows.1 = f32[4,2,2,128,128]{4,3,2,1,0:T(8,128)S(1)} custom-call(s32[3,8]{1,0:T(4,128)S(1)} %pad_add_fusion.info, f32[2,128,512]{2,1,0:T(8,128)S(1)} %get-tuple-element.39.own, f32[2,128,512]{2,1,0:T(8,128)S(1)} %collective-permute-done.following), custom_call_target="tpu_custom_call" | custom-call | tf_op jit(solution)/shard_map/windows/pallas_call | solution.py:267
  14.1 0.0 copy-start
  14.1 0.0 copy-start.2
  14.1 17.8 %all_to_all.20.patch = f32[4,2,2,128,128]{4,3,2,1,0:T(8,128)S(1)} all-to-all(f32[4,2,2,128,128]{4,3,2,1,0:T(8,128)S(1)} %windows.1), channel_id=1, replica_groups=mesh['z'=8,'y'=8,'core'=2,'cuts'=4] {'cuts'}, dimensions={0} | all-to-all | bytes 2097152 | tf_op jit(solution)/shard_map/all_to_all | solution.py:226
  31.9 0.0 copy-done
  31.9 0.0 copy-done.2
  31.9 5.2 %waves.1 = (f32[2,2,128,128]{3,2,1,0:T(8,128)S(1)}, f32[2,2,128,128]{3,2,1,0:T(8,128)S(1)}, f32[2,2,128,128]{3,2,1,0:T(8,128)S(1)}, f32[2,2,128,128]{3,2,1,0:T(8,128)S(1)}, f32[32,8,128]{2,1,0:T(8,128)}) custom-call(s32[3,8]{1,0:T(4,128)S(1)} %pad_add_fusion.info, f32[2,128,128]{2,1,0:T(8,128)S(1)} %get-tuple-element.38.probe, f32[8,128,128]{2,1,0:T(8,128)S(1)} %copy-done.2, ...), custom_call_target="tpu_custom_call" | custom-call | tf_op jit(solution)/shard_map/waves/pallas_call | solution.py:280
  37.1 10.8 %all-to-all-start.1 = ((f32[32,8,128]{2,1,0:T(8,128)}), f32[32,8,128]{2,1,0:T(8,128)S(1)}, u32[]{:S(2)}, u32[]{:S(2)}) async-start(f32[32,8,128]{2,1,0:T(8,128)} %get-tuple-element.40), calls=%async_computation.1 | async-start | bytes 262144 | tf_op jit(solution)/shard_map/all_to_all | solution.py:226
  47.9 3.1 %collective-permute-start.2 = (f32[2,2,128,128]{3,2,1,0:T(8,128)S(1)}, f32[2,2,128,128]{3,2,1,0:T(8,128)S(1)}, u32[]{:S(2)}, u32[]{:S(2)}) collective-permute-start(f32[2,2,128,128]{3,2,1,0:T(8,128)S(1)} %get-tuple-element.44), channel_id=1, source_target_pairs={{0,1},{1,2},{2,3},{3,0},{4,5},{5,6},{6,7},{7,4},{8,9},{9,10},{10,1... | collective-permute-start | bytes 786440 | tf_op jit(solution)/shard_map/ppermute | solution.py:222
  51.0 4.3 %collective-permute-start.3 = (f32[2,2,128,128]{3,2,1,0:T(8,128)S(1)}, f32[2,2,128,128]{3,2,1,0:T(8,128)S(1)}, u32[]{:S(2)}, u32[]{:S(2)}) collective-permute-start(f32[2,2,128,128]{3,2,1,0:T(8,128)S(1)} %get-tuple-element.45), channel_id=1, source_target_pairs={{0,2},{1,3},{2,0},{3,1},{4,6},{5,7},{6,4},{7,5},{8,10},{9,11},{10,... | collective-permute-start | bytes 786440 | tf_op jit(solution)/shard_map/ppermute | solution.py:222
  55.3 3.1 %collective-permute-start.4 = (f32[2,2,128,128]{3,2,1,0:T(8,128)S(1)}, f32[2,2,128,128]{3,2,1,0:T(8,128)S(1)}, u32[]{:S(2)}, u32[]{:S(2)}) collective-permute-start(f32[2,2,128,128]{3,2,1,0:T(8,128)S(1)} %get-tuple-element.46), channel_id=1, source_target_pairs={{0,3},{1,0},{2,1},{3,2},{4,7},{5,4},{6,5},{7,6},{8,11},{9,8},{10,9... | collective-permute-start | bytes 786440 | tf_op jit(solution)/shard_map/ppermute | solution.py:222
  58.4 0.0 all-to-all-done.1
  58.5 0.6 broadcast_in_dim.4
  59.1 9.7 %all-to-all-start.2 = ((f32[16,8,128]{2,1,0:T(8,128)}), f32[16,8,128]{2,1,0:T(8,128)S(1)}, u32[]{:S(2)}, u32[]{:S(2)}) async-start(f32[16,8,128]{2,1,0:T(8,128)} %broadcast_in_dim.4), calls=%async_computation.2 | async-start | bytes 131072 | tf_op jit(solution)/shard_map/all_to_all | solution.py:226
  68.8 3.5 %collective-permute-start.1 = (s32[3,8]{1,0:T(4,128)S(1)}, s32[3,8]{1,0:T(4,128)S(1)}, u32[]{:S(2)}, u32[]{:S(2)}) collective-permute-start(s32[3,8]{1,0:T(4,128)S(1)} %pad_add_fusion.info), channel_id=1, source_target_pairs={{0,4},{4,8},{8,12},{12,16},{16,20},{20,24},{24,28},{28,32},{32,36}... | collective-permute-start | bytes 296 | tf_op jit(solution)/shard_map/ppermute | solution.py:217
  72.4 0.7 collective-permute-done.1.former
  73.1 1.8 %light.1 = f32[128,512]{1,0:T(8,128)S(1)} custom-call(s32[3,8]{1,0:T(4,128)S(1)} %pad_add_fusion.info, s32[3,8]{1,0:T(4,128)S(1)} %collective-permute-done.1.former, f32[2,128,128]{2,1,0:T(8,128)S(1)} %get-tuple-element.38.probe), custom_call_target="tpu_custom_call" | custom-call | tf_op jit(solution)/shard_map/light/pallas_call | solution.py:295
  74.9 1.7 %all-to-all-done.2 = f32[16,8,128]{2,1,0:T(8,128)S(1)} async-done(((f32[16,8,128]{2,1,0:T(8,128)}), f32[16,8,128]{2,1,0:T(8,128)S(1)}, u32[]{:S(2)}, u32[]{:S(2)}) %all-to-all-start.2) | async-done | bytes 65568 | tf_op jit(solution)/shard_map/all_to_all | solution.py:226
  76.6 0.0 collective-permute-done.2.rest_1_
  76.6 0.0 collective-permute-done.3.rest_2_
  76.7 0.0 collective-permute-done.4.rest_3_
  76.7 1.0 %scatter.14 = (f32[2,128,512]{2,1,0:T(8,128)S(1)}, f32[2,128,512]{2,1,0:T(8,128)S(1)}) custom-call(s32[3,8]{1,0:T(4,128)S(1)} %pad_add_fusion.info, f32[2,2,128,128]{3,2,1,0:T(8,128)S(1)} %get-tuple-element.43.rest_0_, f32[2,2,128,128]{3,2,1,0:T(8,128)S(1)} %collective-permute-done.2.rest_1_, f32[2,2,128,128]{3,2,1,0:T(8,128)S(1)} %collective-permute-done.3.rest_2_, ...), custom_call_target="tpu_custom_call" | custom-call | tf_op jit(solution)/shard_map/scatter/pallas_call | solution.py:307
  77.7 2.4 %collective-permute-start.5 = (f32[2,128,512]{2,1,0:T(8,128)S(1)}, f32[2,128,512]{2,1,0:T(8,128)S(1)}, u32[]{:S(2)}, u32[]{:S(2)}) collective-permute-start(f32[2,128,512]{2,1,0:T(8,128)S(1)} %get-tuple-element.48), channel_id=1, source_target_pairs={{0,4},{4,8},{8,12},{12,16},{16,20},{20,24},{24,28},{28,32},{32,36}... | collective-permute-start | bytes 1572872 | tf_op jit(solution)/shard_map/ppermute | solution.py:217
  80.1 14.3 %all_to_all.21.rows = f32[8,8,128]{2,1,0:T(8,128)S(1)} all-to-all(f32[8,8,128]{2,1,0:T(8,128)S(1)} %broadcast_in_dim.5), channel_id=1, replica_groups=mesh['z'=8,'y'=8,'core'=2,'cuts'=4] {'z'}, dimensions={0} | all-to-all | bytes 65536 | tf_op jit(solution)/shard_map/all_to_all | solution.py:226
  94.4 0.0 collective-permute-done.5.rim
  94.4 0.9 final.1
  (7 shorter events, 0.1 us)
Async XLA Ops:
  0.6 12.2 %collective-permute-start = (f32[2,128,512]{2,1,0:T(8,128)}, f32[2,128,512]{2,1,0:T(8,128)S(1)}, u32[]{:S(2)}, u32[]{:S(2)}) collective-permute-start(f32[2,128,512]{2,1,0:T(8,128)} %bitcast.4), channel_id=1, source_target_pairs={{4,0},{8,4},{12,8},{16,12},{20,16},{24,20},{28,24},{32,28},{36,32}... | collective-permute-start | bytes 1572872 | tf_op jit(solution)/shard_map/ppermute | solution.py:217
  10.1 1.0 %copy-start.1 = (f32[2,1,128,512]{3,2,1,0:T(8,128)S(1)}, f32[2,1,128,512]{3,2,1,0:T(8,128)}, u32[]{:S(2)}) copy-start(f32[2,1,128,512]{3,2,1,0:T(8,128)} %param.10) | copy-start | bytes 1572868
  11.1 0.9 copy-start.3
  12.1 0.7 copy-start.4
  14.1 17.8 %copy-start = (bf16[4,2,256,256]{3,2,1,0:T(8,128)(2,1)S(1)}, bf16[4,2,256,256]{3,2,1,0:T(8,128)(2,1)}, u32[]{:S(2)}) copy-start(bf16[4,2,256,256]{3,2,1,0:T(8,128)(2,1)} %constant.76.clone.tables) | copy-start | bytes 3145732
  14.1 17.8 %copy-start.2 = (f32[8,128,128]{2,1,0:T(8,128)S(1)}, f32[8,128,128]{2,1,0:T(8,128)}, u32[]{:S(2)}) copy-start(f32[8,128,128]{2,1,0:T(8,128)} %amplitude.1) | copy-start | bytes 1572868
  37.1 21.3 %all-to-all-start.1 = ((f32[32,8,128]{2,1,0:T(8,128)}), f32[32,8,128]{2,1,0:T(8,128)S(1)}, u32[]{:S(2)}, u32[]{:S(2)}) async-start(f32[32,8,128]{2,1,0:T(8,128)} %get-tuple-element.40), calls=%async_computation.1 | async-start | bytes 262144 | tf_op jit(solution)/shard_map/all_to_all | solution.py:226
  47.9 28.8 %collective-permute-start.2 = (f32[2,2,128,128]{3,2,1,0:T(8,128)S(1)}, f32[2,2,128,128]{3,2,1,0:T(8,128)S(1)}, u32[]{:S(2)}, u32[]{:S(2)}) collective-permute-start(f32[2,2,128,128]{3,2,1,0:T(8,128)S(1)} %get-tuple-element.44), channel_id=1, source_target_pairs={{0,1},{1,2},{2,3},{3,0},{4,5},{5,6},{6,7},{7,4},{8,9},{9,10},{10,1... | collective-permute-start | bytes 786440 | tf_op jit(solution)/shard_map/ppermute | solution.py:222
  51.0 25.6 %collective-permute-start.3 = (f32[2,2,128,128]{3,2,1,0:T(8,128)S(1)}, f32[2,2,128,128]{3,2,1,0:T(8,128)S(1)}, u32[]{:S(2)}, u32[]{:S(2)}) collective-permute-start(f32[2,2,128,128]{3,2,1,0:T(8,128)S(1)} %get-tuple-element.45), channel_id=1, source_target_pairs={{0,2},{1,3},{2,0},{3,1},{4,6},{5,7},{6,4},{7,5},{8,10},{9,11},{10,... | collective-permute-start | bytes 786440 | tf_op jit(solution)/shard_map/ppermute | solution.py:222
  55.3 21.3 %collective-permute-start.4 = (f32[2,2,128,128]{3,2,1,0:T(8,128)S(1)}, f32[2,2,128,128]{3,2,1,0:T(8,128)S(1)}, u32[]{:S(2)}, u32[]{:S(2)}) collective-permute-start(f32[2,2,128,128]{3,2,1,0:T(8,128)S(1)} %get-tuple-element.46), channel_id=1, source_target_pairs={{0,3},{1,0},{2,1},{3,2},{4,7},{5,4},{6,5},{7,6},{8,11},{9,8},{10,9... | collective-permute-start | bytes 786440 | tf_op jit(solution)/shard_map/ppermute | solution.py:222
  59.1 17.5 %all-to-all-start.2 = ((f32[16,8,128]{2,1,0:T(8,128)}), f32[16,8,128]{2,1,0:T(8,128)S(1)}, u32[]{:S(2)}, u32[]{:S(2)}) async-start(f32[16,8,128]{2,1,0:T(8,128)} %broadcast_in_dim.4), calls=%async_computation.2 | async-start | bytes 131072 | tf_op jit(solution)/shard_map/all_to_all | solution.py:226
  68.8 4.2 %collective-permute-start.1 = (s32[3,8]{1,0:T(4,128)S(1)}, s32[3,8]{1,0:T(4,128)S(1)}, u32[]{:S(2)}, u32[]{:S(2)}) collective-permute-start(s32[3,8]{1,0:T(4,128)S(1)} %pad_add_fusion.info), channel_id=1, source_target_pairs={{0,4},{4,8},{8,12},{12,16},{16,20},{20,24},{24,28},{28,32},{32,36}... | collective-permute-start | bytes 296 | tf_op jit(solution)/shard_map/ppermute | solution.py:217
  77.7 16.7 %collective-permute-start.5 = (f32[2,128,512]{2,1,0:T(8,128)S(1)}, f32[2,128,512]{2,1,0:T(8,128)S(1)}, u32[]{:S(2)}, u32[]{:S(2)}) collective-permute-start(f32[2,128,512]{2,1,0:T(8,128)S(1)} %get-tuple-element.48), channel_id=1, source_target_pairs={{0,4},{4,8},{8,12},{12,16},{16,20},{20,24},{24,28},{28,32},{32,36}... | collective-permute-start | bytes 1572872 | tf_op jit(solution)/shard_map/ppermute | solution.py:217

commit v6 on v5

--- a/solution.py
+++ b/solution.py
@@ -205,6 +205,10 @@
     rim[...] = canvas[:, stripe:]
 
 
+def total_kernel(rows, out):
+    out[...] = jnp.broadcast_to(jnp.sum(rows[...], axis=0)[None], out.shape)
+
+
 def final_kernel(inner, rim, light, rows, slice_grad, probe_grad):
     whole = light[...] + 1.0
     for part in range(2):
@@ -272,7 +276,7 @@
         scratch_shapes=[pltpu.VMEM((2, 2 * stripe, columns), jnp.float32)],
         compiler_params=VMEM,
         name="windows",
-    )(info, own, following)
+    )(after(info, former), own, following)
     patches = swap(windows, "cuts")
 
     shares = lax.axis_size(("z", "cuts"))
@@ -291,6 +295,7 @@
         name="waves",
     )(info, probe, amplitude, tables, patches)
     probe_rows = jnp.sum(swap(probe_parts, ("z", "cuts")), axis=0)
+    gathered = [terms[0]] + [around(terms[away], away) for away in range(1, cuts)]
     later = after(info, probe_rows)
     light = pl.pallas_call(
         light_kernel,
@@ -301,8 +306,16 @@
         compiler_params=VMEM,
         name="light",
     )(later, former, probe)
-    gathered = [terms[0]] + [around(terms[away], away) for away in range(1, cuts)]
-    probe_rows = jnp.sum(copies(probe_rows, ("y", "core")), axis=0)
+    layers = lax.axis_size("z")
+    probe_rows = pl.pallas_call(
+        total_kernel,
+        out_shape=jax.ShapeDtypeStruct((layers, *probe_rows.shape), jnp.float32),
+        in_specs=[vmem],
+        out_specs=vmem,
+        compiler_params=VMEM,
+        cost_estimate=pl.CostEstimate(flops=10**11, bytes_accessed=10**8, transcendentals=0),
+        name="total",
+    )(after(copies(probe_rows, ("y", "core")), light))
 
     inner, rim = pl.pallas_call(
         scatter_kernel,
@@ -312,9 +325,9 @@
         scratch_shapes=[pltpu.VMEM((2, stripe + n, columns), jnp.float32)],
         compiler_params=VMEM,
         name="scatter",
-    )(after(info, probe_rows, light), *gathered)
+    )(later, *gathered)
     rim_in = along(rim, 1)
-    probe_rows = copies(after(probe_rows, rim), "z")
+    probe_rows = swap(probe_rows, "z")
     slice_grad, probe_grad = pl.pallas_call(
         final_kernel,
         out_shape=[

time: 95.9 us -> 91.8 us (0.957)
  blocking collectives: 32.1 us -> 30.3 us
  waiting for transfers between devices: 2.46 us -> 0.98 us
  starting transfers between devices: 45.7 us -> 44.5 us
    all_to_all x2, blocking collectives: 32.1 us -> 30.3 us  [swap(): return lax.all_to_all(block, axes, 0, 0)]
  transfers between devices with their start and end apart: 8 -> 8, of which waited for: 2 -> 1; matrix products, arithmetic and copies ran while one was open for 1% -> 1% of each run, Pallas kernels for 2% -> 4%
where the time goes in v6:
time: 91.8 us; the launch traced here: 91.2 us
  starting transfers between devices  44.5 us (48%)
  blocking collectives  30.3 us (33%)
  Pallas kernels  10.7 us (12%)
  local copies, waits for them, and re-layouts  3.27 us (4%)
  between operations  1.47 us (2%)
  waiting for transfers between devices  0.98 us (1%)
    all_to_all x2, blocking collectives, swap(): return lax.all_to_all(block, axes, 0, 0)  30.3 us
    all_to_all x2, starting transfers between devices, swap(): return lax.all_to_all(block, axes, 0, 0)  19.7 us
    ppermute x3, starting transfers between devices, along(): lax.ppermute(block, POS, [(i - distance, i) for i in devices if i - dista...  14.2 us
    ppermute x3, starting transfers between devices, around(): lax.ppermute(block, 'cuts', [(i, (i + distance) % count) for i in range(c...  10.5 us
    pallas_call x1, Pallas kernels, local(): pl.pallas_call(functools.partial(wave_kernel, 1.0 / math.sqrt(slots * acr...  5.19 us
    unnamed x10, local copies, waits for them, and re-layouts  2.51 us
    pallas_call x1, Pallas kernels, local(): pl.pallas_call(light_kernel, out_shape=plane_shape, in_specs=[smem, smem,...  2.21 us
  transfers between devices with their start and end apart: 8, of which 1 were waited for; matrix products, arithmetic and copies ran while one was open for 1% of the time, Pallas kernels for 4%

profile of v6, /device:TPU:1, one launch (start us, length us, event | category | flops | bytes accessed | tf_op | source)
XLA Modules:
  0.0 91.2 jit_solution(8243786374156477780)
XLA Ops:
  0.6 8.8 %collective-permute-start.1 = (f32[2,128,512]{2,1,0:T(8,128)}, f32[2,128,512]{2,1,0:T(8,128)S(1)}, u32[]{:S(2)}, u32[]{:S(2)}) collective-permute-start(f32[2,128,512]{2,1,0:T(8,128)} %bitcast.4), channel_id=1, source_target_pairs={{4,0},{8,4},{12,8},{16,12},{20,16},{24,20},{28,24},{32,28},{36,32}... | collective-permute-start | bytes 1572872 | tf_op jit(solution)/shard_map/ppermute | solution.py:221
  10.1 0.0 copy-start.4
  10.1 0.1 scatter.12
  10.2 0.6 copy-done.4
  10.8 1.9 %collective-permute-start = (s32[3,8]{1,0:T(4,128)S(1)}, s32[3,8]{1,0:T(4,128)S(1)}, u32[]{:S(2)}, u32[]{:S(2)}) collective-permute-start(s32[3,8]{1,0:T(4,128)S(1)} %pad_add_fusion.info), channel_id=1, source_target_pairs={{0,4},{4,8},{8,12},{12,16},{16,20},{20,24},{24,28},{28,32},{32,36}... | collective-permute-start | bytes 296 | tf_op jit(solution)/shard_map/ppermute | solution.py:221
  12.7 0.0 copy-start.1
  12.7 1.0 %copy-done.1 = f32[2,1,128,512]{3,2,1,0:T(8,128)S(1)} copy-done((f32[2,1,128,512]{3,2,1,0:T(8,128)S(1)}, f32[2,1,128,512]{3,2,1,0:T(8,128)}, u32[]{:S(2)}) %copy-start.1) | copy-done | bytes 524312
  13.8 0.0 copy-start.3
  13.8 0.9 copy-done.3
  14.7 0.0 collective-permute-done.former
  14.7 0.0 collective-permute-done.1.following
  14.7 1.3 %windows.1 = f32[4,2,2,128,128]{4,3,2,1,0:T(8,128)S(1)} custom-call(s32[3,8]{1,0:T(4,128)S(1)} %pad_add_fusion.info, f32[2,128,512]{2,1,0:T(8,128)S(1)} %get-tuple-element.40.own, f32[2,128,512]{2,1,0:T(8,128)S(1)} %collective-permute-done.1.following), custom_call_target="tpu_custom_call" | custom-call | tf_op jit(solution)/shard_map/windows/pallas_call | solution.py:271
  16.0 0.0 copy-start
  16.0 0.0 copy-start.2
  16.0 17.3 %all_to_all.20.patch = f32[4,2,2,128,128]{4,3,2,1,0:T(8,128)S(1)} all-to-all(f32[4,2,2,128,128]{4,3,2,1,0:T(8,128)S(1)} %windows.1), channel_id=1, replica_groups=mesh['z'=8,'y'=8,'core'=2,'cuts'=4] {'cuts'}, dimensions={0} | all-to-all | bytes 2097152 | tf_op jit(solution)/shard_map/all_to_all | solution.py:230
  33.3 0.0 copy-done
  33.3 0.0 copy-done.2
  33.3 5.2 %waves.1 = (f32[2,2,128,128]{3,2,1,0:T(8,128)S(1)}, f32[2,2,128,128]{3,2,1,0:T(8,128)S(1)}, f32[2,2,128,128]{3,2,1,0:T(8,128)S(1)}, f32[2,2,128,128]{3,2,1,0:T(8,128)S(1)}, f32[32,8,128]{2,1,0:T(8,128)}) custom-call(s32[3,8]{1,0:T(4,128)S(1)} %pad_add_fusion.info, f32[2,128,128]{2,1,0:T(8,128)S(1)} %get-tuple-element.38.probe, f32[8,128,128]{2,1,0:T(8,128)S(1)} %copy-done.2, ...), custom_call_target="tpu_custom_call" | custom-call | tf_op jit(solution)/shard_map/waves/pallas_call | solution.py:284
  38.5 7.1 %all-to-all-start.1 = ((f32[32,8,128]{2,1,0:T(8,128)}), f32[32,8,128]{2,1,0:T(8,128)S(1)}, u32[]{:S(2)}, u32[]{:S(2)}) async-start(f32[32,8,128]{2,1,0:T(8,128)} %get-tuple-element.41), calls=%async_computation.1 | async-start | bytes 262144 | tf_op jit(solution)/shard_map/all_to_all | solution.py:230
  45.6 3.1 %collective-permute-start.2 = (f32[2,2,128,128]{3,2,1,0:T(8,128)S(1)}, f32[2,2,128,128]{3,2,1,0:T(8,128)S(1)}, u32[]{:S(2)}, u32[]{:S(2)}) collective-permute-start(f32[2,2,128,128]{3,2,1,0:T(8,128)S(1)} %get-tuple-element.44), channel_id=1, source_target_pairs={{0,1},{1,2},{2,3},{3,0},{4,5},{5,6},{6,7},{7,4},{8,9},{9,10},{10,1... | collective-permute-start | bytes 786440 | tf_op jit(solution)/shard_map/ppermute | solution.py:226
  48.7 4.3 %collective-permute-start.3 = (f32[2,2,128,128]{3,2,1,0:T(8,128)S(1)}, f32[2,2,128,128]{3,2,1,0:T(8,128)S(1)}, u32[]{:S(2)}, u32[]{:S(2)}) collective-permute-start(f32[2,2,128,128]{3,2,1,0:T(8,128)S(1)} %get-tuple-element.45), channel_id=1, source_target_pairs={{0,2},{1,3},{2,0},{3,1},{4,6},{5,7},{6,4},{7,5},{8,10},{9,11},{10,... | collective-permute-start | bytes 786440 | tf_op jit(solution)/shard_map/ppermute | solution.py:226
  53.1 3.1 %collective-permute-start.4 = (f32[2,2,128,128]{3,2,1,0:T(8,128)S(1)}, f32[2,2,128,128]{3,2,1,0:T(8,128)S(1)}, u32[]{:S(2)}, u32[]{:S(2)}) collective-permute-start(f32[2,2,128,128]{3,2,1,0:T(8,128)S(1)} %get-tuple-element.46), channel_id=1, source_target_pairs={{0,3},{1,0},{2,1},{3,2},{4,7},{5,4},{6,5},{7,6},{8,11},{9,8},{10,9... | collective-permute-start | bytes 786440 | tf_op jit(solution)/shard_map/ppermute | solution.py:226
  56.2 0.0 all-to-all-done.1
  56.2 0.6 broadcast_in_dim.2
  56.8 12.6 %all-to-all-start.2 = ((f32[16,8,128]{2,1,0:T(8,128)}), f32[16,8,128]{2,1,0:T(8,128)S(1)}, u32[]{:S(2)}, u32[]{:S(2)}) async-start(f32[16,8,128]{2,1,0:T(8,128)} %broadcast_in_dim.2), calls=%async_computation.2 | async-start | bytes 131072 | tf_op jit(solution)/shard_map/all_to_all | solution.py:230
  69.5 2.2 %light.1 = f32[128,512]{1,0:T(8,128)S(1)} custom-call(s32[3,8]{1,0:T(4,128)S(1)} %pad_add_fusion.info, s32[3,8]{1,0:T(4,128)S(1)} %collective-permute-done.former, f32[2,128,128]{2,1,0:T(8,128)S(1)} %get-tuple-element.38.probe), custom_call_target="tpu_custom_call" | custom-call | tf_op jit(solution)/shard_map/light/pallas_call | solution.py:300
  71.7 0.0 collective-permute-done.2.rest_1_
  71.7 0.0 collective-permute-done.3.rest_2_
  71.7 0.0 collective-permute-done.4.rest_3_
  71.7 1.0 %scatter.14 = (f32[2,128,512]{2,1,0:T(8,128)S(1)}, f32[2,128,512]{2,1,0:T(8,128)S(1)}) custom-call(s32[3,8]{1,0:T(4,128)S(1)} %pad_add_fusion.info, f32[2,2,128,128]{3,2,1,0:T(8,128)S(1)} %get-tuple-element.43.rest_0_, f32[2,2,128,128]{3,2,1,0:T(8,128)S(1)} %collective-permute-done.2.rest_1_, f32[2,2,128,128]{3,2,1,0:T(8,128)S(1)} %collective-permute-done.3.rest_2_, ...), custom_call_target="tpu_custom_call" | custom-call | tf_op jit(solution)/shard_map/scatter/pallas_call | solution.py:320
  72.8 3.5 %collective-permute-start.5 = (f32[2,128,512]{2,1,0:T(8,128)S(1)}, f32[2,128,512]{2,1,0:T(8,128)S(1)}, u32[]{:S(2)}, u32[]{:S(2)}) collective-permute-start(f32[2,128,512]{2,1,0:T(8,128)S(1)} %get-tuple-element.48), channel_id=1, source_target_pairs={{0,4},{4,8},{8,12},{12,16},{16,20},{20,24},{24,28},{28,32},{32,36}... | collective-permute-start | bytes 1572872 | tf_op jit(solution)/shard_map/ppermute | solution.py:221
  76.3 1.0 %all-to-all-done.2.rows = f32[16,8,128]{2,1,0:T(8,128)S(1)} async-done(((f32[16,8,128]{2,1,0:T(8,128)}), f32[16,8,128]{2,1,0:T(8,128)S(1)}, u32[]{:S(2)}, u32[]{:S(2)}) %all-to-all-start.2) | async-done | bytes 65568 | tf_op jit(solution)/shard_map/all_to_all | solution.py:230
  77.3 13.0 %all_to_all.21.rows = f32[8,8,128]{2,1,0:T(8,128)S(1)} all-to-all(f32[8,8,128]{2,1,0:T(8,128)S(1)} %total.1), channel_id=1, replica_groups=mesh['z'=8,'y'=8,'core'=2,'cuts'=4] {'z'}, dimensions={0} | all-to-all | bytes 65536 | tf_op jit(solution)/shard_map/all_to_all | solution.py:230
  90.4 0.0 collective-permute-done.5.rim
  90.4 0.9 final.1
  (6 shorter events, 0.1 us)
Async XLA Ops:
  0.6 14.1 %collective-permute-start.1 = (f32[2,128,512]{2,1,0:T(8,128)}, f32[2,128,512]{2,1,0:T(8,128)S(1)}, u32[]{:S(2)}, u32[]{:S(2)}) collective-permute-start(f32[2,128,512]{2,1,0:T(8,128)} %bitcast.4), channel_id=1, source_target_pairs={{4,0},{8,4},{12,8},{16,12},{20,16},{24,20},{28,24},{32,28},{36,32}... | collective-permute-start | bytes 1572872 | tf_op jit(solution)/shard_map/ppermute | solution.py:221
  10.1 0.7 copy-start.4
  10.8 3.9 %collective-permute-start = (s32[3,8]{1,0:T(4,128)S(1)}, s32[3,8]{1,0:T(4,128)S(1)}, u32[]{:S(2)}, u32[]{:S(2)}) collective-permute-start(s32[3,8]{1,0:T(4,128)S(1)} %pad_add_fusion.info), channel_id=1, source_target_pairs={{0,4},{4,8},{8,12},{12,16},{16,20},{20,24},{24,28},{28,32},{32,36}... | collective-permute-start | bytes 296 | tf_op jit(solution)/shard_map/ppermute | solution.py:221
  12.7 1.0 %copy-start.1 = (f32[2,1,128,512]{3,2,1,0:T(8,128)S(1)}, f32[2,1,128,512]{3,2,1,0:T(8,128)}, u32[]{:S(2)}) copy-start(f32[2,1,128,512]{3,2,1,0:T(8,128)} %param.10) | copy-start | bytes 1572868
  13.8 0.9 copy-start.3
  16.0 17.3 %copy-start = (bf16[4,2,256,256]{3,2,1,0:T(8,128)(2,1)S(1)}, bf16[4,2,256,256]{3,2,1,0:T(8,128)(2,1)}, u32[]{:S(2)}) copy-start(bf16[4,2,256,256]{3,2,1,0:T(8,128)(2,1)} %constant.76.clone.tables) | copy-start | bytes 3145732
  16.0 17.3 %copy-start.2 = (f32[8,128,128]{2,1,0:T(8,128)S(1)}, f32[8,128,128]{2,1,0:T(8,128)}, u32[]{:S(2)}) copy-start(f32[8,128,128]{2,1,0:T(8,128)} %amplitude.1) | copy-start | bytes 1572868
  38.5 17.6 %all-to-all-start.1 = ((f32[32,8,128]{2,1,0:T(8,128)}), f32[32,8,128]{2,1,0:T(8,128)S(1)}, u32[]{:S(2)}, u32[]{:S(2)}) async-start(f32[32,8,128]{2,1,0:T(8,128)} %get-tuple-element.41), calls=%async_computation.1 | async-start | bytes 262144 | tf_op jit(solution)/shard_map/all_to_all | solution.py:230
  45.6 26.1 %collective-permute-start.2 = (f32[2,2,128,128]{3,2,1,0:T(8,128)S(1)}, f32[2,2,128,128]{3,2,1,0:T(8,128)S(1)}, u32[]{:S(2)}, u32[]{:S(2)}) collective-permute-start(f32[2,2,128,128]{3,2,1,0:T(8,128)S(1)} %get-tuple-element.44), channel_id=1, source_target_pairs={{0,1},{1,2},{2,3},{3,0},{4,5},{5,6},{6,7},{7,4},{8,9},{9,10},{10,1... | collective-permute-start | bytes 786440 | tf_op jit(solution)/shard_map/ppermute | solution.py:226
  48.7 23.0 %collective-permute-start.3 = (f32[2,2,128,128]{3,2,1,0:T(8,128)S(1)}, f32[2,2,128,128]{3,2,1,0:T(8,128)S(1)}, u32[]{:S(2)}, u32[]{:S(2)}) collective-permute-start(f32[2,2,128,128]{3,2,1,0:T(8,128)S(1)} %get-tuple-element.45), channel_id=1, source_target_pairs={{0,2},{1,3},{2,0},{3,1},{4,6},{5,7},{6,4},{7,5},{8,10},{9,11},{10,... | collective-permute-start | bytes 786440 | tf_op jit(solution)/shard_map/ppermute | solution.py:226
  53.1 18.7 %collective-permute-start.4 = (f32[2,2,128,128]{3,2,1,0:T(8,128)S(1)}, f32[2,2,128,128]{3,2,1,0:T(8,128)S(1)}, u32[]{:S(2)}, u32[]{:S(2)}) collective-permute-start(f32[2,2,128,128]{3,2,1,0:T(8,128)S(1)} %get-tuple-element.46), channel_id=1, source_target_pairs={{0,3},{1,0},{2,1},{3,2},{4,7},{5,4},{6,5},{7,6},{8,11},{9,8},{10,9... | collective-permute-start | bytes 786440 | tf_op jit(solution)/shard_map/ppermute | solution.py:226
  56.8 20.4 %all-to-all-start.2 = ((f32[16,8,128]{2,1,0:T(8,128)}), f32[16,8,128]{2,1,0:T(8,128)S(1)}, u32[]{:S(2)}, u32[]{:S(2)}) async-start(f32[16,8,128]{2,1,0:T(8,128)} %broadcast_in_dim.2), calls=%async_computation.2 | async-start | bytes 131072 | tf_op jit(solution)/shard_map/all_to_all | solution.py:230
  72.8 17.6 %collective-permute-start.5 = (f32[2,128,512]{2,1,0:T(8,128)S(1)}, f32[2,128,512]{2,1,0:T(8,128)S(1)}, u32[]{:S(2)}, u32[]{:S(2)}) collective-permute-start(f32[2,128,512]{2,1,0:T(8,128)S(1)} %get-tuple-element.48), channel_id=1, source_target_pairs={{0,4},{4,8},{8,12},{12,16},{16,20},{20,24},{24,28},{28,32},{32,36}... | collective-permute-start | bytes 1572872 | tf_op jit(solution)/shard_map/ppermute | solution.py:221

commit v7 on v6

--- a/solution.py
+++ b/solution.py
@@ -71,9 +71,19 @@
     return a[0] * b[0] + a[1] * b[1], a[0] * b[1] - a[1] * b[0]
 
 
-def spot(info, slot, columns, n):
-    row = info[0, slot]
-    col = info[1, slot]
+def scalars(info):
+    values = info[...]
+    return [[values[line, slot] for slot in range(values.shape[1])] for line in range(values.shape[0])]
+
+
+def choose(values, index):
+    chosen = values[0]
+    for position in range(1, len(values)):
+        chosen = jnp.where(index == position, values[position], chosen)
+    return chosen
+
+
+def spot(row, col, columns, n):
     top = pl.multiple_of(row // 8 * 8, 8)
     band = pl.multiple_of(jnp.minimum(col // n * n, columns - 2 * n), n)
     return (pl.ds(top, n + 8), pl.ds(band, 2 * n)), row - top, col - band
@@ -113,14 +123,14 @@
     power = probe[0] * probe[0] + probe[1] * probe[1]
 
     def fill(source):
+        rows, cols, (live, *_) = scalars(source)
         canvas[...] = jnp.zeros_like(canvas)
-
-        def one(slot, carry):
-            at, down, right = spot(source, slot, columns, n)
-            canvas[at] = canvas[at] + placed(power, down, right)
-            return carry
-
-        lax.fori_loop(0, jnp.minimum(source[2, 0], source.shape[1]), one, 0)
+        for slot in range(len(rows)):
+
+            @pl.when(slot < live)
+            def _():
+                at, down, right = spot(rows[slot], cols[slot], columns, n)
+                canvas[at] = canvas[at] + placed(power, down, right)
 
     fill(former)
     light[...] = canvas[stripe:]
@@ -131,11 +141,13 @@
 def window_kernel(info, own, following, out, ext):
     cuts, pair, _, n, _ = out.shape
     stripe, columns = own.shape[1:]
+    rows, cols, _ = scalars(info)
     ext[:, :stripe] = own[...]
     ext[:, stripe:] = following[...]
     for target in range(cuts):
         for which in range(pair):
-            at, down, right = spot(info, target + which * cuts, columns, n)
+            slot = target + which * cuts
+            at, down, right = spot(rows[slot], cols[slot], columns, n)
             for part in range(2):
                 out[target, which, part] = cut_out(ext[(part, *at)], down, right)
 
@@ -143,8 +155,7 @@
 def wave_kernel(scale, info, probe, amplitude, tables, patch, *rest):
     cuts, pair, _, n, _ = patch.shape
     sent, (probe_out, terms, amp, sems) = rest[:cuts], rest[cuts:]
-    me = info[2, 1]
-    live = info[2, 0]
+    _, _, (live, me, *_) = scalars(info)
     copies = [
         pltpu.make_async_copy(amplitude.at[me + which * cuts], amp.at[which], sems.at[which]) for which in range(pair)
     ]
@@ -192,12 +203,13 @@
     cuts = len(arrived)
     pair, _, n, _ = arrived[0].shape
     stripe, columns = inner.shape[1:]
-    me = info[2, 1]
+    rows, cols, (_, me, *_) = scalars(info)
     canvas[...] = jnp.zeros_like(canvas)
     for away in range(cuts):
         source = lax.rem(me + cuts - away, cuts)
         for which in range(pair):
-            at, down, right = spot(info, source + which * cuts, columns, n)
+            mine = slice(which * cuts, (which + 1) * cuts)
+            at, down, right = spot(choose(rows[mine], source), choose(cols[mine], source), columns, n)
             for part in range(2):
                 spread = placed(arrived[away][which, part], down, right)
                 canvas[(part, *at)] = canvas[(part, *at)] + spread
@@ -228,10 +240,6 @@
 
 def swap(block, axes):
     return lax.all_to_all(block, axes, 0, 0)
-
-
-def copies(block, axes):
-    return swap(jnp.broadcast_to(block[None], (lax.axis_size(axes), *block.shape)), axes)
 
 
 def after(block, *first):
@@ -251,7 +259,6 @@
     row = offsets[0] - lax.axis_index(POS) * stripe
     extra = jnp.zeros((slots,), jnp.int32).at[0].set(live[0]).at[1].set(me)
     info = jnp.stack([row, offsets[1], extra])
-    smem = pl.BlockSpec(memory_space=pltpu.SMEM)
     vmem = pl.BlockSpec(memory_space=pltpu.VMEM)
     hbm = pl.BlockSpec(memory_space=pltpu.HBM)
     tables = jnp.asarray(table_stack(n))
@@ -271,7 +278,7 @@
     windows = pl.pallas_call(
         window_kernel,
         out_shape=packet,
-        in_specs=[smem, vmem, vmem],
+        in_specs=[vmem] * 3,
         out_specs=vmem,
         scratch_shapes=[pltpu.VMEM((2, 2 * stripe, columns), jnp.float32)],
         compiler_params=VMEM,
@@ -284,7 +291,7 @@
     *terms, probe_parts = pl.pallas_call(
         functools.partial(wave_kernel, 1.0 / math.sqrt(slots * across)),
         out_shape=[packet] * cuts + [jax.ShapeDtypeStruct((shares, 2 * n // shares, n), jnp.float32)],
-        in_specs=[smem, vmem, hbm, vmem, vmem],
+        in_specs=[vmem, vmem, hbm, vmem, vmem],
         out_specs=[vmem] * (cuts + 1),
         scratch_shapes=[
             pltpu.VMEM((cuts, pair, 2, n, n), jnp.float32),
@@ -294,33 +301,36 @@
         compiler_params=VMEM,
         name="waves",
     )(info, probe, amplitude, tables, patches)
-    probe_rows = jnp.sum(swap(probe_parts, ("z", "cuts")), axis=0)
+    def total(rows, axes, **kwargs):
+        return pl.pallas_call(
+            total_kernel,
+            out_shape=jax.ShapeDtypeStruct((lax.axis_size(axes), *rows.shape[1:]), jnp.float32),
+            in_specs=[vmem],
+            out_specs=vmem,
+            compiler_params=VMEM,
+            name="total",
+            **kwargs,
+        )(rows)
+
+    probe_rows = total(swap(probe_parts, ("z", "cuts")), ("y", "core"))
     gathered = [terms[0]] + [around(terms[away], away) for away in range(1, cuts)]
     later = after(info, probe_rows)
     light = pl.pallas_call(
         light_kernel,
         out_shape=plane_shape,
-        in_specs=[smem, smem, vmem],
+        in_specs=[vmem] * 3,
         out_specs=vmem,
         scratch_shapes=[pltpu.VMEM((stripe + n, columns), jnp.float32)],
         compiler_params=VMEM,
         name="light",
     )(later, former, probe)
-    layers = lax.axis_size("z")
-    probe_rows = pl.pallas_call(
-        total_kernel,
-        out_shape=jax.ShapeDtypeStruct((layers, *probe_rows.shape), jnp.float32),
-        in_specs=[vmem],
-        out_specs=vmem,
-        compiler_params=VMEM,
-        cost_estimate=pl.CostEstimate(flops=10**11, bytes_accessed=10**8, transcendentals=0),
-        name="total",
-    )(after(copies(probe_rows, ("y", "core")), light))
+    estimate = pl.CostEstimate(flops=10**11, bytes_accessed=10**8, transcendentals=0)
+    probe_rows = total(after(swap(probe_rows, ("y", "core")), light), "z", cost_estimate=estimate)
 
     inner, rim = pl.pallas_call(
         scatter_kernel,
         out_shape=[stripe_shape] * 2,
-        in_specs=[smem] + [vmem] * cuts,
+        in_specs=[vmem] * (cuts + 1),
         out_specs=[vmem] * 2,
         scratch_shapes=[pltpu.VMEM((2, stripe + n, columns), jnp.float32)],
         compiler_params=VMEM,

time: 91.8 us -> 90.8 us (0.989)
  Pallas kernels: 10.7 us -> 8.6 us
  waiting for transfers between devices: 0.98 us -> 2.59 us
    all_to_all x2, waiting for transfers between devices: 0.96 us -> 2.58 us  [swap(): return lax.all_to_all(block, axes, 0, 0)]
    pallas_call x4 -> x5, Pallas kernels: 4.55 us -> 2.96 us  [the longest x1 0.81 us: local(): pl.pallas_call(window_kernel, out_shape=packet, in_specs=[vmem] * 3, out_...]
  transfers between devices with their start and end apart: 8 -> 8, of which waited for: 1 -> 1; matrix products, arithmetic and copies ran while one was open for 1% -> 0% of each run, Pallas kernels for 4% -> 2%
where the time goes in v7:
time: 90.8 us; the launch traced here: 90.3 us
  starting transfers between devices  44.7 us (49%)
  blocking collectives  30.3 us (33%)
  Pallas kernels  8.6 us (9%)
  local copies, waits for them, and re-layouts  2.63 us (3%)
  waiting for transfers between devices  2.59 us (3%)
  between operations  1.46 us (2%)
    all_to_all x2, blocking collectives, swap(): return lax.all_to_all(block, axes, 0, 0)  30.3 us
    all_to_all x2, starting transfers between devices, swap(): return lax.all_to_all(block, axes, 0, 0)  19.7 us
    ppermute x3, starting transfers between devices, along(): lax.ppermute(block, POS, [(i - distance, i) for i in devices if i - dista...  14.4 us
    ppermute x3, starting transfers between devices, around(): lax.ppermute(block, 'cuts', [(i, (i + distance) % count) for i in range(c...  10.5 us
    pallas_call x1, Pallas kernels, local(): pl.pallas_call(functools.partial(wave_kernel, 1.0 / math.sqrt(slots * acr...  4.72 us
    all_to_all x2, waiting for transfers between devices, swap(): return lax.all_to_all(block, axes, 0, 0)  2.58 us
    unnamed x10, local copies, waits for them, and re-layouts  2.51 us
  transfers between devices with their start and end apart: 8, of which 1 were waited for; matrix products, arithmetic and copies ran while one was open for 0% of the time, Pallas kernels for 2%

profile of v7, /device:TPU:1, one launch (start us, length us, event | category | flops | bytes accessed | tf_op | source)
XLA Modules:
  0.0 90.3 jit_solution(11853669124559358319)
XLA Ops:
  0.6 8.8 %collective-permute-start.1 = (f32[2,128,512]{2,1,0:T(8,128)}, f32[2,128,512]{2,1,0:T(8,128)S(1)}, u32[]{:S(2)}, u32[]{:S(2)}) collective-permute-start(f32[2,128,512]{2,1,0:T(8,128)} %bitcast.4), channel_id=1, source_target_pairs={{4,0},{8,4},{12,8},{16,12},{20,16},{24,20},{28,24},{32,28},{36,32}... | collective-permute-start | bytes 1572872 | tf_op jit(solution)/shard_map/ppermute | solution.py:233
  10.1 0.0 copy-start.4
  10.1 0.1 scatter.12
  10.2 0.6 copy-done.4
  10.8 1.9 %collective-permute-start = (s32[3,8]{1,0:T(4,128)S(1)}, s32[3,8]{1,0:T(4,128)S(1)}, u32[]{:S(2)}, u32[]{:S(2)}) collective-permute-start(s32[3,8]{1,0:T(4,128)S(1)} %pad_add_fusion.info), channel_id=1, source_target_pairs={{0,4},{4,8},{8,12},{12,16},{16,20},{20,24},{24,28},{28,32},{32,36}... | collective-permute-start | bytes 296 | tf_op jit(solution)/shard_map/ppermute | solution.py:233
  12.7 0.0 copy-start.1
  12.7 1.0 %copy-done.1 = f32[2,1,128,512]{3,2,1,0:T(8,128)S(1)} copy-done((f32[2,1,128,512]{3,2,1,0:T(8,128)S(1)}, f32[2,1,128,512]{3,2,1,0:T(8,128)}, u32[]{:S(2)}) %copy-start.1) | copy-done | bytes 524312
  13.8 0.0 copy-start.3
  13.8 0.9 copy-done.3
  14.7 0.0 collective-permute-done.former
  14.7 0.0 collective-permute-done.1.following
  14.7 0.8 windows.1
  15.6 0.0 copy-start
  15.6 0.0 copy-start.2
  15.6 17.3 %all_to_all.20.patch = f32[4,2,2,128,128]{4,3,2,1,0:T(8,128)S(1)} all-to-all(f32[4,2,2,128,128]{4,3,2,1,0:T(8,128)S(1)} %windows.1), channel_id=1, replica_groups=mesh['z'=8,'y'=8,'core'=2,'cuts'=4] {'cuts'}, dimensions={0} | all-to-all | bytes 2097152 | tf_op jit(solution)/shard_map/all_to_all | solution.py:242
  32.8 0.0 copy-done
  32.8 0.0 copy-done.2
  32.9 4.7 %waves.1 = (f32[2,2,128,128]{3,2,1,0:T(8,128)S(1)}, f32[2,2,128,128]{3,2,1,0:T(8,128)S(1)}, f32[2,2,128,128]{3,2,1,0:T(8,128)S(1)}, f32[2,2,128,128]{3,2,1,0:T(8,128)S(1)}, f32[32,8,128]{2,1,0:T(8,128)}) custom-call(s32[3,8]{1,0:T(4,128)S(1)} %pad_add_fusion.info, f32[2,128,128]{2,1,0:T(8,128)S(1)} %get-tuple-element.38.probe, f32[8,128,128]{2,1,0:T(8,128)S(1)} %copy-done.2, ...), custom_call_target="tpu_custom_call" | custom-call | tf_op jit(solution)/shard_map/waves/pallas_call | solution.py:291
  37.6 7.1 %all-to-all-start.1 = ((f32[32,8,128]{2,1,0:T(8,128)}), f32[32,8,128]{2,1,0:T(8,128)S(1)}, u32[]{:S(2)}, u32[]{:S(2)}) async-start(f32[32,8,128]{2,1,0:T(8,128)} %get-tuple-element.41), calls=%async_computation.1 | async-start | bytes 262144 | tf_op jit(solution)/shard_map/all_to_all | solution.py:242
  44.7 3.1 %collective-permute-start.2 = (f32[2,2,128,128]{3,2,1,0:T(8,128)S(1)}, f32[2,2,128,128]{3,2,1,0:T(8,128)S(1)}, u32[]{:S(2)}, u32[]{:S(2)}) collective-permute-start(f32[2,2,128,128]{3,2,1,0:T(8,128)S(1)} %get-tuple-element.44), channel_id=1, source_target_pairs={{0,1},{1,2},{2,3},{3,0},{4,5},{5,6},{6,7},{7,4},{8,9},{9,10},{10,1... | collective-permute-start | bytes 786440 | tf_op jit(solution)/shard_map/ppermute | solution.py:238
  47.8 4.3 %collective-permute-start.3 = (f32[2,2,128,128]{3,2,1,0:T(8,128)S(1)}, f32[2,2,128,128]{3,2,1,0:T(8,128)S(1)}, u32[]{:S(2)}, u32[]{:S(2)}) collective-permute-start(f32[2,2,128,128]{3,2,1,0:T(8,128)S(1)} %get-tuple-element.45), channel_id=1, source_target_pairs={{0,2},{1,3},{2,0},{3,1},{4,6},{5,7},{6,4},{7,5},{8,10},{9,11},{10,... | collective-permute-start | bytes 786440 | tf_op jit(solution)/shard_map/ppermute | solution.py:238
  52.1 3.1 %collective-permute-start.4 = (f32[2,2,128,128]{3,2,1,0:T(8,128)S(1)}, f32[2,2,128,128]{3,2,1,0:T(8,128)S(1)}, u32[]{:S(2)}, u32[]{:S(2)}) collective-permute-start(f32[2,2,128,128]{3,2,1,0:T(8,128)S(1)} %get-tuple-element.46), channel_id=1, source_target_pairs={{0,3},{1,0},{2,1},{3,2},{4,7},{5,4},{6,5},{7,6},{8,11},{9,8},{10,9... | collective-permute-start | bytes 786440 | tf_op jit(solution)/shard_map/ppermute | solution.py:238
  55.2 0.0 all-to-all-done.1.rows
  55.2 0.7 total.2
  55.9 12.6 %all-to-all-start.2 = ((f32[16,8,128]{2,1,0:T(8,128)}), f32[16,8,128]{2,1,0:T(8,128)S(1)}, u32[]{:S(2)}, u32[]{:S(2)}) async-start(f32[16,8,128]{2,1,0:T(8,128)} %total.2), calls=%async_computation.2 | async-start | bytes 131072 | tf_op jit(solution)/shard_map/all_to_all | solution.py:242
  68.5 0.8 light.1
  69.4 0.0 collective-permute-done.2.rest_1_
  69.4 0.0 collective-permute-done.3.rest_2_
  69.4 0.0 collective-permute-done.4.rest_3_
  69.4 0.7 scatter.14
  70.0 3.7 %collective-permute-start.5 = (f32[2,128,512]{2,1,0:T(8,128)S(1)}, f32[2,128,512]{2,1,0:T(8,128)S(1)}, u32[]{:S(2)}, u32[]{:S(2)}) collective-permute-start(f32[2,128,512]{2,1,0:T(8,128)S(1)} %get-tuple-element.48), channel_id=1, source_target_pairs={{0,4},{4,8},{8,12},{12,16},{16,20},{20,24},{24,28},{28,32},{32,36}... | collective-permute-start | bytes 1572872 | tf_op jit(solution)/shard_map/ppermute | solution.py:233
  73.8 2.6 %all-to-all-done.2.rows = f32[16,8,128]{2,1,0:T(8,128)S(1)} async-done(((f32[16,8,128]{2,1,0:T(8,128)}), f32[16,8,128]{2,1,0:T(8,128)S(1)}, u32[]{:S(2)}, u32[]{:S(2)}) %all-to-all-start.2) | async-done | bytes 65568 | tf_op jit(solution)/shard_map/all_to_all | solution.py:242
  76.4 13.0 %all_to_all.21.rows = f32[8,8,128]{2,1,0:T(8,128)S(1)} all-to-all(f32[8,8,128]{2,1,0:T(8,128)S(1)} %total.3), channel_id=1, replica_groups=mesh['z'=8,'y'=8,'core'=2,'cuts'=4] {'z'}, dimensions={0} | all-to-all | bytes 65536 | tf_op jit(solution)/shard_map/all_to_all | solution.py:242
  89.4 0.0 collective-permute-done.5.rim
  89.4 0.9 final.1
  (5 shorter events, 0.1 us)
Async XLA Ops:
  0.6 14.1 %collective-permute-start.1 = (f32[2,128,512]{2,1,0:T(8,128)}, f32[2,128,512]{2,1,0:T(8,128)S(1)}, u32[]{:S(2)}, u32[]{:S(2)}) collective-permute-start(f32[2,128,512]{2,1,0:T(8,128)} %bitcast.4), channel_id=1, source_target_pairs={{4,0},{8,4},{12,8},{16,12},{20,16},{24,20},{28,24},{32,28},{36,32}... | collective-permute-start | bytes 1572872 | tf_op jit(solution)/shard_map/ppermute | solution.py:233
  10.1 0.7 copy-start.4
  10.8 3.9 %collective-permute-start = (s32[3,8]{1,0:T(4,128)S(1)}, s32[3,8]{1,0:T(4,128)S(1)}, u32[]{:S(2)}, u32[]{:S(2)}) collective-permute-start(s32[3,8]{1,0:T(4,128)S(1)} %pad_add_fusion.info), channel_id=1, source_target_pairs={{0,4},{4,8},{8,12},{12,16},{16,20},{20,24},{24,28},{28,32},{32,36}... | collective-permute-start | bytes 296 | tf_op jit(solution)/shard_map/ppermute | solution.py:233
  12.7 1.0 %copy-start.1 = (f32[2,1,128,512]{3,2,1,0:T(8,128)S(1)}, f32[2,1,128,512]{3,2,1,0:T(8,128)}, u32[]{:S(2)}) copy-start(f32[2,1,128,512]{3,2,1,0:T(8,128)} %param.10) | copy-start | bytes 1572868
  13.8 0.9 %copy-start.3 = (f32[2,128,128]{2,1,0:T(8,128)S(1)}, f32[2,128,128]{2,1,0:T(8,128)}, u32[]{:S(2)}) copy-start(f32[2,128,128]{2,1,0:T(8,128)} %probe.1) | copy-start | bytes 393220
  15.6 17.3 %copy-start = (bf16[4,2,256,256]{3,2,1,0:T(8,128)(2,1)S(1)}, bf16[4,2,256,256]{3,2,1,0:T(8,128)(2,1)}, u32[]{:S(2)}) copy-start(bf16[4,2,256,256]{3,2,1,0:T(8,128)(2,1)} %constant.74.clone.tables) | copy-start | bytes 3145732
  15.6 17.3 %copy-start.2 = (f32[8,128,128]{2,1,0:T(8,128)S(1)}, f32[8,128,128]{2,1,0:T(8,128)}, u32[]{:S(2)}) copy-start(f32[8,128,128]{2,1,0:T(8,128)} %amplitude.1) | copy-start | bytes 1572868
  37.6 17.6 %all-to-all-start.1 = ((f32[32,8,128]{2,1,0:T(8,128)}), f32[32,8,128]{2,1,0:T(8,128)S(1)}, u32[]{:S(2)}, u32[]{:S(2)}) async-start(f32[32,8,128]{2,1,0:T(8,128)} %get-tuple-element.41), calls=%async_computation.1 | async-start | bytes 262144 | tf_op jit(solution)/shard_map/all_to_all | solution.py:242
  44.7 24.7 %collective-permute-start.2 = (f32[2,2,128,128]{3,2,1,0:T(8,128)S(1)}, f32[2,2,128,128]{3,2,1,0:T(8,128)S(1)}, u32[]{:S(2)}, u32[]{:S(2)}) collective-permute-start(f32[2,2,128,128]{3,2,1,0:T(8,128)S(1)} %get-tuple-element.44), channel_id=1, source_target_pairs={{0,1},{1,2},{2,3},{3,0},{4,5},{5,6},{6,7},{7,4},{8,9},{9,10},{10,1... | collective-permute-start | bytes 786440 | tf_op jit(solution)/shard_map/ppermute | solution.py:238
  47.8 21.6 %collective-permute-start.3 = (f32[2,2,128,128]{3,2,1,0:T(8,128)S(1)}, f32[2,2,128,128]{3,2,1,0:T(8,128)S(1)}, u32[]{:S(2)}, u32[]{:S(2)}) collective-permute-start(f32[2,2,128,128]{3,2,1,0:T(8,128)S(1)} %get-tuple-element.45), channel_id=1, source_target_pairs={{0,2},{1,3},{2,0},{3,1},{4,6},{5,7},{6,4},{7,5},{8,10},{9,11},{10,... | collective-permute-start | bytes 786440 | tf_op jit(solution)/shard_map/ppermute | solution.py:238
  52.1 17.3 %collective-permute-start.4 = (f32[2,2,128,128]{3,2,1,0:T(8,128)S(1)}, f32[2,2,128,128]{3,2,1,0:T(8,128)S(1)}, u32[]{:S(2)}, u32[]{:S(2)}) collective-permute-start(f32[2,2,128,128]{3,2,1,0:T(8,128)S(1)} %get-tuple-element.46), channel_id=1, source_target_pairs={{0,3},{1,0},{2,1},{3,2},{4,7},{5,4},{6,5},{7,6},{8,11},{9,8},{10,9... | collective-permute-start | bytes 786440 | tf_op jit(solution)/shard_map/ppermute | solution.py:238
  55.9 20.4 %all-to-all-start.2 = ((f32[16,8,128]{2,1,0:T(8,128)}), f32[16,8,128]{2,1,0:T(8,128)S(1)}, u32[]{:S(2)}, u32[]{:S(2)}) async-start(f32[16,8,128]{2,1,0:T(8,128)} %total.2), calls=%async_computation.2 | async-start | bytes 131072 | tf_op jit(solution)/shard_map/all_to_all | solution.py:242
  70.0 19.4 %collective-permute-start.5 = (f32[2,128,512]{2,1,0:T(8,128)S(1)}, f32[2,128,512]{2,1,0:T(8,128)S(1)}, u32[]{:S(2)}, u32[]{:S(2)}) collective-permute-start(f32[2,128,512]{2,1,0:T(8,128)S(1)} %get-tuple-element.48), channel_id=1, source_target_pairs={{0,4},{4,8},{8,12},{12,16},{16,20},{20,24},{24,28},{28,32},{32,36}... | collective-permute-start | bytes 1572872 | tf_op jit(solution)/shard_map/ppermute | solution.py:233

commit v8 on v7

--- a/solution.py
+++ b/solution.py
@@ -275,6 +275,16 @@
         compiler_params=VMEM,
         name="stage",
     )(own, probe)
+    light = pl.pallas_call(
+        light_kernel,
+        out_shape=plane_shape,
+        in_specs=[vmem] * 3,
+        out_specs=vmem,
+        scratch_shapes=[pltpu.VMEM((stripe + n, columns), jnp.float32)],
+        compiler_params=VMEM,
+        name="light",
+    )(info, former, probe)
+
     windows = pl.pallas_call(
         window_kernel,
         out_shape=packet,
@@ -283,7 +293,7 @@
         scratch_shapes=[pltpu.VMEM((2, 2 * stripe, columns), jnp.float32)],
         compiler_params=VMEM,
         name="windows",
-    )(after(info, former), own, following)
+    )(after(info, light), own, following)
     patches = swap(windows, "cuts")
 
     shares = lax.axis_size(("z", "cuts"))
@@ -315,17 +325,8 @@
     probe_rows = total(swap(probe_parts, ("z", "cuts")), ("y", "core"))
     gathered = [terms[0]] + [around(terms[away], away) for away in range(1, cuts)]
     later = after(info, probe_rows)
-    light = pl.pallas_call(
-        light_kernel,
-        out_shape=plane_shape,
-        in_specs=[vmem] * 3,
-        out_specs=vmem,
-        scratch_shapes=[pltpu.VMEM((stripe + n, columns), jnp.float32)],
-        compiler_params=VMEM,
-        name="light",
-    )(later, former, probe)
     estimate = pl.CostEstimate(flops=10**11, bytes_accessed=10**8, transcendentals=0)
-    probe_rows = total(after(swap(probe_rows, ("y", "core")), light), "z", cost_estimate=estimate)
+    probe_rows = total(swap(probe_rows, ("y", "core")), "z", cost_estimate=estimate)
 
     inner, rim = pl.pallas_call(
         scatter_kernel,

time: 90.8 us -> 90.8 us (level)
  starting transfers between devices: 44.7 us -> 43.3 us
  waiting for transfers between devices: 2.59 us -> 3.58 us
    all_to_all x2, starting transfers between devices: 19.7 us -> 18.5 us  [swap(): return lax.all_to_all(block, axes, 0, 0)]
    all_to_all x2, waiting for transfers between devices: 2.58 us -> 3.57 us  [swap(): return lax.all_to_all(block, axes, 0, 0)]
  transfers between devices with their start and end apart: 8 -> 8, of which waited for: 1 -> 1; matrix products, arithmetic and copies ran while one was open for 0% -> 0% of each run, Pallas kernels for 2% -> 3%
where the time goes in v8:
time: 90.8 us; the launch traced here: 90.3 us
  starting transfers between devices  43.3 us (48%)
  blocking collectives  30.5 us (34%)
  Pallas kernels  8.78 us (10%)
  waiting for transfers between devices  3.58 us (4%)
  local copies, waits for them, and re-layouts  2.63 us (3%)
  between operations  1.46 us (2%)
    all_to_all x2, blocking collectives, swap(): return lax.all_to_all(block, axes, 0, 0)  30.5 us
    all_to_all x2, starting transfers between devices, swap(): return lax.all_to_all(block, axes, 0, 0)  18.5 us
    ppermute x3, starting transfers between devices, along(): lax.ppermute(block, POS, [(i - distance, i) for i in devices if i - dista...  14.3 us
    ppermute x3, starting transfers between devices, around(): lax.ppermute(block, 'cuts', [(i, (i + distance) % count) for i in range(c...  10.5 us
    pallas_call x1, Pallas kernels, local(): pl.pallas_call(functools.partial(wave_kernel, 1.0 / math.sqrt(slots * acr...  4.72 us
    all_to_all x2, waiting for transfers between devices, swap(): return lax.all_to_all(block, axes, 0, 0)  3.57 us
    unnamed x10, local copies, waits for them, and re-layouts  2.52 us
  transfers between devices with their start and end apart: 8, of which 1 were waited for; matrix products, arithmetic and copies ran while one was open for 0% of the time, Pallas kernels for 3%

profile of v8, /device:TPU:1, one launch (start us, length us, event | category | flops | bytes accessed | tf_op | source)
XLA Modules:
  0.0 90.3 jit_solution(16391823870932555922)
XLA Ops:
  0.6 8.8 %collective-permute-start.1 = (f32[2,128,512]{2,1,0:T(8,128)}, f32[2,128,512]{2,1,0:T(8,128)S(1)}, u32[]{:S(2)}, u32[]{:S(2)}) collective-permute-start(f32[2,128,512]{2,1,0:T(8,128)} %bitcast.4), channel_id=1, source_target_pairs={{4,0},{8,4},{12,8},{16,12},{20,16},{24,20},{28,24},{32,28},{36,32}... | collective-permute-start | bytes 1572872 | tf_op jit(solution)/shard_map/ppermute | solution.py:233
  10.1 0.0 copy-start.4
  10.1 0.1 scatter.12
  10.2 0.6 copy-done.4
  10.8 1.9 %collective-permute-start = (s32[3,8]{1,0:T(4,128)S(1)}, s32[3,8]{1,0:T(4,128)S(1)}, u32[]{:S(2)}, u32[]{:S(2)}) collective-permute-start(s32[3,8]{1,0:T(4,128)S(1)} %pad_add_fusion.info), channel_id=1, source_target_pairs={{0,4},{4,8},{8,12},{12,16},{16,20},{20,24},{24,28},{28,32},{32,36}... | collective-permute-start | bytes 296 | tf_op jit(solution)/shard_map/ppermute | solution.py:233
  12.7 0.0 copy-start.1
  12.7 1.0 %copy-done.1 = f32[2,1,128,512]{3,2,1,0:T(8,128)S(1)} copy-done((f32[2,1,128,512]{3,2,1,0:T(8,128)S(1)}, f32[2,1,128,512]{3,2,1,0:T(8,128)}, u32[]{:S(2)}) %copy-start.1) | copy-done | bytes 524312
  13.8 0.0 copy-start.3
  13.8 0.9 copy-done.3
  14.7 0.0 collective-permute-done.former
  14.7 1.0 %light.1 = f32[128,512]{1,0:T(8,128)S(1)} custom-call(s32[3,8]{1,0:T(4,128)S(1)} %pad_add_fusion.info, s32[3,8]{1,0:T(4,128)S(1)} %collective-permute-done.former, f32[2,128,128]{2,1,0:T(8,128)S(1)} %get-tuple-element.37.probe), custom_call_target="tpu_custom_call" | custom-call | tf_op jit(solution)/shard_map/light/pallas_call | solution.py:278
  15.7 0.0 collective-permute-done.1.following
  15.7 0.8 windows.1
  16.6 0.0 copy-start
  16.6 0.0 copy-start.2
  16.6 17.5 %all_to_all.20.patch = f32[4,2,2,128,128]{4,3,2,1,0:T(8,128)S(1)} all-to-all(f32[4,2,2,128,128]{4,3,2,1,0:T(8,128)S(1)} %windows.1), channel_id=1, replica_groups=mesh['z'=8,'y'=8,'core'=2,'cuts'=4] {'cuts'}, dimensions={0} | all-to-all | bytes 2097152 | tf_op jit(solution)/shard_map/all_to_all | solution.py:242
  34.1 0.0 copy-done
  34.1 0.0 copy-done.2
  34.1 4.7 %waves.1 = (f32[2,2,128,128]{3,2,1,0:T(8,128)S(1)}, f32[2,2,128,128]{3,2,1,0:T(8,128)S(1)}, f32[2,2,128,128]{3,2,1,0:T(8,128)S(1)}, f32[2,2,128,128]{3,2,1,0:T(8,128)S(1)}, f32[32,8,128]{2,1,0:T(8,128)}) custom-call(s32[3,8]{1,0:T(4,128)S(1)} %pad_add_fusion.info, f32[2,128,128]{2,1,0:T(8,128)S(1)} %get-tuple-element.37.probe, f32[8,128,128]{2,1,0:T(8,128)S(1)} %copy-done.2, ...), custom_call_target="tpu_custom_call" | custom-call | tf_op jit(solution)/shard_map/waves/pallas_call | solution.py:301
  38.8 4.8 %all-to-all-start.1 = ((f32[32,8,128]{2,1,0:T(8,128)}), f32[32,8,128]{2,1,0:T(8,128)S(1)}, u32[]{:S(2)}, u32[]{:S(2)}) async-start(f32[32,8,128]{2,1,0:T(8,128)} %get-tuple-element.40), calls=%async_computation.1 | async-start | bytes 262144 | tf_op jit(solution)/shard_map/all_to_all | solution.py:242
  43.5 3.1 %collective-permute-start.2 = (f32[2,2,128,128]{3,2,1,0:T(8,128)S(1)}, f32[2,2,128,128]{3,2,1,0:T(8,128)S(1)}, u32[]{:S(2)}, u32[]{:S(2)}) collective-permute-start(f32[2,2,128,128]{3,2,1,0:T(8,128)S(1)} %get-tuple-element.43), channel_id=1, source_target_pairs={{0,1},{1,2},{2,3},{3,0},{4,5},{5,6},{6,7},{7,4},{8,9},{9,10},{10,1... | collective-permute-start | bytes 786440 | tf_op jit(solution)/shard_map/ppermute | solution.py:238
  46.7 4.3 %collective-permute-start.3 = (f32[2,2,128,128]{3,2,1,0:T(8,128)S(1)}, f32[2,2,128,128]{3,2,1,0:T(8,128)S(1)}, u32[]{:S(2)}, u32[]{:S(2)}) collective-permute-start(f32[2,2,128,128]{3,2,1,0:T(8,128)S(1)} %get-tuple-element.44), channel_id=1, source_target_pairs={{0,2},{1,3},{2,0},{3,1},{4,6},{5,7},{6,4},{7,5},{8,10},{9,11},{10,... | collective-permute-start | bytes 786440 | tf_op jit(solution)/shard_map/ppermute | solution.py:238
  51.0 3.1 %collective-permute-start.4 = (f32[2,2,128,128]{3,2,1,0:T(8,128)S(1)}, f32[2,2,128,128]{3,2,1,0:T(8,128)S(1)}, u32[]{:S(2)}, u32[]{:S(2)}) collective-permute-start(f32[2,2,128,128]{3,2,1,0:T(8,128)S(1)} %get-tuple-element.45), channel_id=1, source_target_pairs={{0,3},{1,0},{2,1},{3,2},{4,7},{5,4},{6,5},{7,6},{8,11},{9,8},{10,9... | collective-permute-start | bytes 786440 | tf_op jit(solution)/shard_map/ppermute | solution.py:238
  54.1 0.0 all-to-all-done.1.rows
  54.1 0.7 total.2
  54.8 13.8 %all-to-all-start.2 = ((f32[16,8,128]{2,1,0:T(8,128)}), f32[16,8,128]{2,1,0:T(8,128)S(1)}, u32[]{:S(2)}, u32[]{:S(2)}) async-start(f32[16,8,128]{2,1,0:T(8,128)} %total.2), calls=%async_computation.2 | async-start | bytes 131072 | tf_op jit(solution)/shard_map/all_to_all | solution.py:242
  68.5 0.0 collective-permute-done.2.rest_1_
  68.5 0.0 collective-permute-done.3.rest_2_
  68.6 0.0 collective-permute-done.4.rest_3_
  68.6 0.7 scatter.14
  69.2 3.6 %collective-permute-start.5 = (f32[2,128,512]{2,1,0:T(8,128)S(1)}, f32[2,128,512]{2,1,0:T(8,128)S(1)}, u32[]{:S(2)}, u32[]{:S(2)}) collective-permute-start(f32[2,128,512]{2,1,0:T(8,128)S(1)} %get-tuple-element.47), channel_id=1, source_target_pairs={{0,4},{4,8},{8,12},{12,16},{16,20},{20,24},{24,28},{28,32},{32,36}... | collective-permute-start | bytes 1572872 | tf_op jit(solution)/shard_map/ppermute | solution.py:233
  72.8 3.6 %all-to-all-done.2.rows = f32[16,8,128]{2,1,0:T(8,128)S(1)} async-done(((f32[16,8,128]{2,1,0:T(8,128)}), f32[16,8,128]{2,1,0:T(8,128)S(1)}, u32[]{:S(2)}, u32[]{:S(2)}) %all-to-all-start.2) | async-done | bytes 65568 | tf_op jit(solution)/shard_map/all_to_all | solution.py:242
  76.4 13.0 %all_to_all.21.rows = f32[8,8,128]{2,1,0:T(8,128)S(1)} all-to-all(f32[8,8,128]{2,1,0:T(8,128)S(1)} %total.3), channel_id=1, replica_groups=mesh['z'=8,'y'=8,'core'=2,'cuts'=4] {'z'}, dimensions={0} | all-to-all | bytes 65536 | tf_op jit(solution)/shard_map/all_to_all | solution.py:242
  89.4 0.0 collective-permute-done.5.rim
  89.4 0.9 final.1
  (5 shorter events, 0.1 us)
Async XLA Ops:
  0.6 15.1 %collective-permute-start.1 = (f32[2,128,512]{2,1,0:T(8,128)}, f32[2,128,512]{2,1,0:T(8,128)S(1)}, u32[]{:S(2)}, u32[]{:S(2)}) collective-permute-start(f32[2,128,512]{2,1,0:T(8,128)} %bitcast.4), channel_id=1, source_target_pairs={{4,0},{8,4},{12,8},{16,12},{20,16},{24,20},{28,24},{32,28},{36,32}... | collective-permute-start | bytes 1572872 | tf_op jit(solution)/shard_map/ppermute | solution.py:233
  10.1 0.7 copy-start.4
  10.8 3.9 %collective-permute-start = (s32[3,8]{1,0:T(4,128)S(1)}, s32[3,8]{1,0:T(4,128)S(1)}, u32[]{:S(2)}, u32[]{:S(2)}) collective-permute-start(s32[3,8]{1,0:T(4,128)S(1)} %pad_add_fusion.info), channel_id=1, source_target_pairs={{0,4},{4,8},{8,12},{12,16},{16,20},{20,24},{24,28},{28,32},{32,36}... | collective-permute-start | bytes 296 | tf_op jit(solution)/shard_map/ppermute | solution.py:233
  12.7 1.0 %copy-start.1 = (f32[2,1,128,512]{3,2,1,0:T(8,128)S(1)}, f32[2,1,128,512]{3,2,1,0:T(8,128)}, u32[]{:S(2)}) copy-start(f32[2,1,128,512]{3,2,1,0:T(8,128)} %param.10) | copy-start | bytes 1572868
  13.8 0.9 %copy-start.3 = (f32[2,128,128]{2,1,0:T(8,128)S(1)}, f32[2,128,128]{2,1,0:T(8,128)}, u32[]{:S(2)}) copy-start(f32[2,128,128]{2,1,0:T(8,128)} %probe.1) | copy-start | bytes 393220
  16.6 17.5 %copy-start = (bf16[4,2,256,256]{3,2,1,0:T(8,128)(2,1)S(1)}, bf16[4,2,256,256]{3,2,1,0:T(8,128)(2,1)}, u32[]{:S(2)}) copy-start(bf16[4,2,256,256]{3,2,1,0:T(8,128)(2,1)} %constant.74.clone.tables) | copy-start | bytes 3145732
  16.6 17.5 %copy-start.2 = (f32[8,128,128]{2,1,0:T(8,128)S(1)}, f32[8,128,128]{2,1,0:T(8,128)}, u32[]{:S(2)}) copy-start(f32[8,128,128]{2,1,0:T(8,128)} %amplitude.1) | copy-start | bytes 1572868
  38.8 15.3 %all-to-all-start.1 = ((f32[32,8,128]{2,1,0:T(8,128)}), f32[32,8,128]{2,1,0:T(8,128)S(1)}, u32[]{:S(2)}, u32[]{:S(2)}) async-start(f32[32,8,128]{2,1,0:T(8,128)} %get-tuple-element.40), calls=%async_computation.1 | async-start | bytes 262144 | tf_op jit(solution)/shard_map/all_to_all | solution.py:242
  43.5 25.0 %collective-permute-start.2 = (f32[2,2,128,128]{3,2,1,0:T(8,128)S(1)}, f32[2,2,128,128]{3,2,1,0:T(8,128)S(1)}, u32[]{:S(2)}, u32[]{:S(2)}) collective-permute-start(f32[2,2,128,128]{3,2,1,0:T(8,128)S(1)} %get-tuple-element.43), channel_id=1, source_target_pairs={{0,1},{1,2},{2,3},{3,0},{4,5},{5,6},{6,7},{7,4},{8,9},{9,10},{10,1... | collective-permute-start | bytes 786440 | tf_op jit(solution)/shard_map/ppermute | solution.py:238
  46.7 21.9 %collective-permute-start.3 = (f32[2,2,128,128]{3,2,1,0:T(8,128)S(1)}, f32[2,2,128,128]{3,2,1,0:T(8,128)S(1)}, u32[]{:S(2)}, u32[]{:S(2)}) collective-permute-start(f32[2,2,128,128]{3,2,1,0:T(8,128)S(1)} %get-tuple-element.44), channel_id=1, source_target_pairs={{0,2},{1,3},{2,0},{3,1},{4,6},{5,7},{6,4},{7,5},{8,10},{9,11},{10,... | collective-permute-start | bytes 786440 | tf_op jit(solution)/shard_map/ppermute | solution.py:238
  51.0 17.6 %collective-permute-start.4 = (f32[2,2,128,128]{3,2,1,0:T(8,128)S(1)}, f32[2,2,128,128]{3,2,1,0:T(8,128)S(1)}, u32[]{:S(2)}, u32[]{:S(2)}) collective-permute-start(f32[2,2,128,128]{3,2,1,0:T(8,128)S(1)} %get-tuple-element.45), channel_id=1, source_target_pairs={{0,3},{1,0},{2,1},{3,2},{4,7},{5,4},{6,5},{7,6},{8,11},{9,8},{10,9... | collective-permute-start | bytes 786440 | tf_op jit(solution)/shard_map/ppermute | solution.py:238
  54.8 21.6 %all-to-all-start.2 = ((f32[16,8,128]{2,1,0:T(8,128)}), f32[16,8,128]{2,1,0:T(8,128)S(1)}, u32[]{:S(2)}, u32[]{:S(2)}) async-start(f32[16,8,128]{2,1,0:T(8,128)} %total.2), calls=%async_computation.2 | async-start | bytes 131072 | tf_op jit(solution)/shard_map/all_to_all | solution.py:242
  69.2 20.2 %collective-permute-start.5 = (f32[2,128,512]{2,1,0:T(8,128)S(1)}, f32[2,128,512]{2,1,0:T(8,128)S(1)}, u32[]{:S(2)}, u32[]{:S(2)}) collective-permute-start(f32[2,128,512]{2,1,0:T(8,128)S(1)} %get-tuple-element.47), channel_id=1, source_target_pairs={{0,4},{4,8},{8,12},{12,16},{16,20},{20,24},{24,28},{28,32},{32,36}... | collective-permute-start | bytes 1572872 | tf_op jit(solution)/shard_map/ppermute | solution.py:233

commit v9 on v8

--- a/solution.py
+++ b/solution.py
@@ -71,9 +71,8 @@
     return a[0] * b[0] + a[1] * b[1], a[0] * b[1] - a[1] * b[0]
 
 
-def scalars(info):
-    values = info[...]
-    return [[values[line, slot] for slot in range(values.shape[1])] for line in range(values.shape[0])]
+def scalars(info, slots):
+    return [[info[line, slot] for slot in range(slots)] for line in range(3)]
 
 
 def choose(values, index):
@@ -117,31 +116,29 @@
     probe_copy[...] = probe[...]
 
 
-def light_kernel(info, former, probe, light, canvas):
+def lit(slots, places, probe, canvas):
     n = probe.shape[1]
-    stripe, columns = light.shape
+    columns = canvas.shape[1]
     power = probe[0] * probe[0] + probe[1] * probe[1]
-
-    def fill(source):
-        rows, cols, (live, *_) = scalars(source)
-        canvas[...] = jnp.zeros_like(canvas)
-        for slot in range(len(rows)):
-
-            @pl.when(slot < live)
-            def _():
-                at, down, right = spot(rows[slot], cols[slot], columns, n)
-                canvas[at] = canvas[at] + placed(power, down, right)
-
-    fill(former)
-    light[...] = canvas[stripe:]
-    fill(info)
-    light[...] += canvas[:stripe]
+    rows, cols, (live, *_) = scalars(places, slots)
+    canvas[...] = jnp.zeros_like(canvas)
+    for slot in range(slots):
+
+        @pl.when(slot < live)
+        def _():
+            at, down, right = spot(rows[slot], cols[slot], columns, n)
+            canvas[at] = canvas[at] + placed(power, down, right)
+
+
+def light_kernel(slots, info, probe, light, canvas):
+    lit(slots, info[...], probe, canvas)
+    light[...] = canvas[: light.shape[0]]
 
 
 def window_kernel(info, own, following, out, ext):
     cuts, pair, _, n, _ = out.shape
     stripe, columns = own.shape[1:]
-    rows, cols, _ = scalars(info)
+    rows, cols, _ = scalars(info[...], cuts * pair)
     ext[:, :stripe] = own[...]
     ext[:, stripe:] = following[...]
     for target in range(cuts):
@@ -155,7 +152,7 @@
 def wave_kernel(scale, info, probe, amplitude, tables, patch, *rest):
     cuts, pair, _, n, _ = patch.shape
     sent, (probe_out, terms, amp, sems) = rest[:cuts], rest[cuts:]
-    _, _, (live, me, *_) = scalars(info)
+    _, _, (live, me, *_) = scalars(info[...], cuts * pair)
     copies = [
         pltpu.make_async_copy(amplitude.at[me + which * cuts], amp.at[which], sems.at[which]) for which in range(pair)
     ]
@@ -203,7 +200,7 @@
     cuts = len(arrived)
     pair, _, n, _ = arrived[0].shape
     stripe, columns = inner.shape[1:]
-    rows, cols, (_, me, *_) = scalars(info)
+    rows, cols, (_, me, *_) = scalars(info[...], cuts * pair)
     canvas[...] = jnp.zeros_like(canvas)
     for away in range(cuts):
         source = lax.rem(me + cuts - away, cuts)
@@ -214,17 +211,22 @@
                 spread = placed(arrived[away][which, part], down, right)
                 canvas[(part, *at)] = canvas[(part, *at)] + spread
     inner[...] = canvas[:, :stripe]
-    rim[...] = canvas[:, stripe:]
+    rim[:, :n] = canvas[:, stripe:]
+    rim[:, n:] = jnp.zeros_like(rim[:, n:])
+    rim[0, n:, :n] = info[...].astype(jnp.float32)
 
 
 def total_kernel(rows, out):
     out[...] = jnp.broadcast_to(jnp.sum(rows[...], axis=0)[None], out.shape)
 
 
-def final_kernel(inner, rim, light, rows, slice_grad, probe_grad):
-    whole = light[...] + 1.0
+def final_kernel(slots, inner, rim, light, probe, rows, slice_grad, probe_grad, canvas):
+    n = probe.shape[1]
+    stripe = light.shape[0]
+    lit(slots, rim[0, n:, :n].astype(jnp.int32), probe, canvas)
+    whole = light[...] + canvas[stripe:] + 1.0
     for part in range(2):
-        slice_grad[part, 0] = (inner[part] + rim[part]) / whole
+        slice_grad[part, 0] = (inner[part] + rim[part, :n]) / whole
     probe_grad[...] = rows[...].reshape(probe_grad.shape)
 
 
@@ -258,7 +260,7 @@
     following = along(own, -1)
     row = offsets[0] - lax.axis_index(POS) * stripe
     extra = jnp.zeros((slots,), jnp.int32).at[0].set(live[0]).at[1].set(me)
-    info = jnp.stack([row, offsets[1], extra])
+    info = jnp.pad(jnp.stack([row, offsets[1], extra]), ((0, 5), (0, n - slots)))
     vmem = pl.BlockSpec(memory_space=pltpu.VMEM)
     hbm = pl.BlockSpec(memory_space=pltpu.HBM)
     tables = jnp.asarray(table_stack(n))
@@ -266,7 +268,6 @@
     plane_shape = jax.ShapeDtypeStruct((stripe, columns), jnp.float32)
     packet = jax.ShapeDtypeStruct((cuts, pair, 2, n, n), jnp.float32)
 
-    former = along(info, 1)
     own, probe = pl.pallas_call(
         stage_kernel,
         out_shape=[stripe_shape, jax.ShapeDtypeStruct(probe.shape, jnp.float32)],
@@ -276,14 +277,14 @@
         name="stage",
     )(own, probe)
     light = pl.pallas_call(
-        light_kernel,
+        functools.partial(light_kernel, slots),
         out_shape=plane_shape,
-        in_specs=[vmem] * 3,
+        in_specs=[vmem] * 2,
         out_specs=vmem,
         scratch_shapes=[pltpu.VMEM((stripe + n, columns), jnp.float32)],
         compiler_params=VMEM,
         name="light",
-    )(info, former, probe)
+    )(info, probe)
 
     windows = pl.pallas_call(
         window_kernel,
@@ -330,7 +331,7 @@
 
     inner, rim = pl.pallas_call(
         scatter_kernel,
-        out_shape=[stripe_shape] * 2,
+        out_shape=[stripe_shape, jax.ShapeDtypeStruct((2, n + 8, columns), jnp.float32)],
         in_specs=[vmem] * (cuts + 1),
         out_specs=[vmem] * 2,
         scratch_shapes=[pltpu.VMEM((2, stripe + n, columns), jnp.float32)],
@@ -340,16 +341,17 @@
     rim_in = along(rim, 1)
     probe_rows = swap(probe_rows, "z")
     slice_grad, probe_grad = pl.pallas_call(
-        final_kernel,
+        functools.partial(final_kernel, slots),
         out_shape=[
             jax.ShapeDtypeStruct((2, 1, stripe, columns), jnp.float32),
             jax.ShapeDtypeStruct((2, n // cuts, n), jnp.float32),
         ],
-        in_specs=[vmem] * 4,
+        in_specs=[vmem] * 5,
         out_specs=[vmem] * 2,
+        scratch_shapes=[pltpu.VMEM((stripe + n, columns), jnp.float32)],
         compiler_params=VMEM,
         name="final",
-    )(inner, rim_in, light, probe_rows)
+    )(inner, rim_in, light, probe, probe_rows)
     return slice_grad, probe_grad
 
 

time: 90.8 us -> 90.5 us (level)
    ppermute x3 -> x2, starting transfers between devices: 14.3 us -> 12.3 us  [along(): lax.ppermute(block, POS, [(i - distance, i) for i in devices if i - dista...]
    all_to_all x2, starting transfers between devices: 18.5 us -> 20.1 us  [swap(): return lax.all_to_all(block, axes, 0, 0)]
  transfers between devices with their start and end apart: 8 -> 7, of which waited for: 1 -> 1; matrix products, arithmetic and copies ran while one was open for 0% -> 0% of each run, Pallas kernels for 3% -> 2%
where the time goes in v9:
time: 90.5 us; the launch traced here: 90 us
  starting transfers between devices  43 us (48%)
  blocking collectives  30.4 us (34%)
  Pallas kernels  8.87 us (10%)
  waiting for transfers between devices  3.59 us (4%)
  local copies, waits for them, and re-layouts  2.64 us (3%)
  between operations  1.45 us (2%)
    all_to_all x2, blocking collectives, swap(): return lax.all_to_all(block, axes, 0, 0)  30.4 us
    all_to_all x2, starting transfers between devices, swap(): return lax.all_to_all(block, axes, 0, 0)  20.1 us
    ppermute x2, starting transfers between devices, along(): lax.ppermute(block, POS, [(i - distance, i) for i in devices if i - dista...  12.3 us
    ppermute x3, starting transfers between devices, around(): lax.ppermute(block, 'cuts', [(i, (i + distance) % count) for i in range(c...  10.5 us
    pallas_call x1, Pallas kernels, local(): pl.pallas_call(functools.partial(wave_kernel, 1.0 / math.sqrt(slots * acr...  4.73 us
    all_to_all x2, waiting for transfers between devices, swap(): return lax.all_to_all(block, axes, 0, 0)  3.58 us
    unnamed x10, local copies, waits for them, and re-layouts  2.52 us
  transfers between devices with their start and end apart: 7, of which 1 were waited for; matrix products, arithmetic and copies ran while one was open for 0% of the time, Pallas kernels for 2%

profile of v9, /device:TPU:1, one launch (start us, length us, event | category | flops | bytes accessed | tf_op | source)
XLA Modules:
  0.0 90.0 jit_solution(12443611646266922657)
XLA Ops:
  0.6 8.8 %collective-permute-start = (f32[2,128,512]{2,1,0:T(8,128)}, f32[2,128,512]{2,1,0:T(8,128)S(1)}, u32[]{:S(2)}, u32[]{:S(2)}) collective-permute-start(f32[2,128,512]{2,1,0:T(8,128)} %bitcast.4), channel_id=1, source_target_pairs={{4,0},{8,4},{12,8},{16,12},{20,16},{24,20},{28,24},{32,28},{36,32}... | collective-permute-start | bytes 1572872 | tf_op jit(solution)/shard_map/ppermute | solution.py:235
  10.1 0.0 copy-start.4
  10.1 0.1 scatter.12
  10.2 0.6 copy-done.4
  10.8 0.0 copy-start.1
  10.8 1.0 %copy-done.1 = f32[2,1,128,512]{3,2,1,0:T(8,128)S(1)} copy-done((f32[2,1,128,512]{3,2,1,0:T(8,128)S(1)}, f32[2,1,128,512]{3,2,1,0:T(8,128)}, u32[]{:S(2)}) %copy-start.1) | copy-done | bytes 524312
  11.8 0.0 copy-start.3
  11.9 0.9 %copy-done.3 = f32[2,128,128]{2,1,0:T(8,128)S(1)} copy-done((f32[2,128,128]{2,1,0:T(8,128)S(1)}, f32[2,128,128]{2,1,0:T(8,128)}, u32[]{:S(2)}) %copy-start.3) | copy-done | bytes 131096
  12.8 0.7 light.1
  13.5 0.0 collective-permute-done.following
  13.5 0.8 windows.1
  14.4 0.0 copy-start
  14.4 0.0 copy-start.2
  14.4 17.4 %all_to_all.20.patch = f32[4,2,2,128,128]{4,3,2,1,0:T(8,128)S(1)} all-to-all(f32[4,2,2,128,128]{4,3,2,1,0:T(8,128)S(1)} %windows.1), channel_id=1, replica_groups=mesh['z'=8,'y'=8,'core'=2,'cuts'=4] {'cuts'}, dimensions={0} | all-to-all | bytes 2097152 | tf_op jit(solution)/shard_map/all_to_all | solution.py:244
  31.8 0.0 copy-done
  31.8 0.0 copy-done.2
  31.8 4.7 %waves.1 = (f32[2,2,128,128]{3,2,1,0:T(8,128)S(1)}, f32[2,2,128,128]{3,2,1,0:T(8,128)S(1)}, f32[2,2,128,128]{3,2,1,0:T(8,128)S(1)}, f32[2,2,128,128]{3,2,1,0:T(8,128)S(1)}, f32[32,8,128]{2,1,0:T(8,128)}) custom-call(s32[8,128]{1,0:T(8,128)S(1)} %pad.9.info, f32[2,128,128]{2,1,0:T(8,128)S(1)} %get-tuple-element.37.probe, f32[8,128,128]{2,1,0:T(8,128)S(1)} %copy-done.2, ...), custom_call_target="tpu_custom_call" | custom-call | tf_op jit(solution)/shard_map/waves/pallas_call | solution.py:302
  36.5 10.4 %all-to-all-start.1 = ((f32[32,8,128]{2,1,0:T(8,128)}), f32[32,8,128]{2,1,0:T(8,128)S(1)}, u32[]{:S(2)}, u32[]{:S(2)}) async-start(f32[32,8,128]{2,1,0:T(8,128)} %get-tuple-element.40), calls=%async_computation.1 | async-start | bytes 262144 | tf_op jit(solution)/shard_map/all_to_all | solution.py:244
  46.9 3.1 %collective-permute-start.1 = (f32[2,2,128,128]{3,2,1,0:T(8,128)S(1)}, f32[2,2,128,128]{3,2,1,0:T(8,128)S(1)}, u32[]{:S(2)}, u32[]{:S(2)}) collective-permute-start(f32[2,2,128,128]{3,2,1,0:T(8,128)S(1)} %get-tuple-element.43), channel_id=1, source_target_pairs={{0,1},{1,2},{2,3},{3,0},{4,5},{5,6},{6,7},{7,4},{8,9},{9,10},{10,1... | collective-permute-start | bytes 786440 | tf_op jit(solution)/shard_map/ppermute | solution.py:240
  50.1 4.3 %collective-permute-start.2 = (f32[2,2,128,128]{3,2,1,0:T(8,128)S(1)}, f32[2,2,128,128]{3,2,1,0:T(8,128)S(1)}, u32[]{:S(2)}, u32[]{:S(2)}) collective-permute-start(f32[2,2,128,128]{3,2,1,0:T(8,128)S(1)} %get-tuple-element.44), channel_id=1, source_target_pairs={{0,2},{1,3},{2,0},{3,1},{4,6},{5,7},{6,4},{7,5},{8,10},{9,11},{10,... | collective-permute-start | bytes 786440 | tf_op jit(solution)/shard_map/ppermute | solution.py:240
  54.4 3.1 %collective-permute-start.3 = (f32[2,2,128,128]{3,2,1,0:T(8,128)S(1)}, f32[2,2,128,128]{3,2,1,0:T(8,128)S(1)}, u32[]{:S(2)}, u32[]{:S(2)}) collective-permute-start(f32[2,2,128,128]{3,2,1,0:T(8,128)S(1)} %get-tuple-element.45), channel_id=1, source_target_pairs={{0,3},{1,0},{2,1},{3,2},{4,7},{5,4},{6,5},{7,6},{8,11},{9,8},{10,9... | collective-permute-start | bytes 786440 | tf_op jit(solution)/shard_map/ppermute | solution.py:240
  57.5 0.0 all-to-all-done.1.rows
  57.5 0.7 total.2
  58.2 9.7 %all-to-all-start.2 = ((f32[16,8,128]{2,1,0:T(8,128)}), f32[16,8,128]{2,1,0:T(8,128)S(1)}, u32[]{:S(2)}, u32[]{:S(2)}) async-start(f32[16,8,128]{2,1,0:T(8,128)} %total.2), calls=%async_computation.2 | async-start | bytes 131072 | tf_op jit(solution)/shard_map/all_to_all | solution.py:244
  67.9 0.0 collective-permute-done.1.rest_1_
  67.9 0.0 collective-permute-done.2.rest_2_
  67.9 0.0 collective-permute-done.3.rest_3_
  67.9 0.6 scatter.14
  68.6 3.5 %collective-permute-start.4 = (f32[2,136,512]{2,1,0:T(8,128)S(1)}, f32[2,136,512]{2,1,0:T(8,128)S(1)}, u32[]{:S(2)}, u32[]{:S(2)}) collective-permute-start(f32[2,136,512]{2,1,0:T(8,128)S(1)} %get-tuple-element.47), channel_id=1, source_target_pairs={{0,4},{4,8},{8,12},{12,16},{16,20},{20,24},{24,28},{28,32},{32,36}... | collective-permute-start | bytes 1671176 | tf_op jit(solution)/shard_map/ppermute | solution.py:235
  72.1 3.6 %all-to-all-done.2.rows = f32[16,8,128]{2,1,0:T(8,128)S(1)} async-done(((f32[16,8,128]{2,1,0:T(8,128)}), f32[16,8,128]{2,1,0:T(8,128)S(1)}, u32[]{:S(2)}, u32[]{:S(2)}) %all-to-all-start.2) | async-done | bytes 65568 | tf_op jit(solution)/shard_map/all_to_all | solution.py:244
  75.7 13.0 %all_to_all.21.rows = f32[8,8,128]{2,1,0:T(8,128)S(1)} all-to-all(f32[8,8,128]{2,1,0:T(8,128)S(1)} %total.3), channel_id=1, replica_groups=mesh['z'=8,'y'=8,'core'=2,'cuts'=4] {'z'}, dimensions={0} | all-to-all | bytes 65536 | tf_op jit(solution)/shard_map/all_to_all | solution.py:244
  88.8 0.0 collective-permute-done.4.rim
  88.8 1.2 %final.1 = (f32[2,1,128,512]{3,2,1,0:T(8,128)}, f32[2,32,128]{2,1,0:T(8,128)}) custom-call(f32[2,128,512]{2,1,0:T(8,128)S(1)} %get-tuple-element.46.inner, f32[2,136,512]{2,1,0:T(8,128)S(1)} %collective-permute-done.4.rim, f32[128,512]{1,0:T(8,128)S(1)} %light.1, f32[2,128,128]{2,1,0:T(8,128)S(1)} %get-tuple-element.37.probe, f32[8,8,128]{2,1,0:T(8,128)S(1)} %all_to_all.21.rows), custom_call_target="tpu_custom_call" | custom-call | tf_op jit(solution)/shard_map/final/pallas_call | solution.py:343
  (6 shorter events, 0.1 us)
Async XLA Ops:
  0.6 12.9 %collective-permute-start = (f32[2,128,512]{2,1,0:T(8,128)}, f32[2,128,512]{2,1,0:T(8,128)S(1)}, u32[]{:S(2)}, u32[]{:S(2)}) collective-permute-start(f32[2,128,512]{2,1,0:T(8,128)} %bitcast.4), channel_id=1, source_target_pairs={{4,0},{8,4},{12,8},{16,12},{20,16},{24,20},{28,24},{32,28},{36,32}... | collective-permute-start | bytes 1572872 | tf_op jit(solution)/shard_map/ppermute | solution.py:235
  10.1 0.7 copy-start.4
  10.8 1.0 %copy-start.1 = (f32[2,1,128,512]{3,2,1,0:T(8,128)S(1)}, f32[2,1,128,512]{3,2,1,0:T(8,128)}, u32[]{:S(2)}) copy-start(f32[2,1,128,512]{3,2,1,0:T(8,128)} %param.10) | copy-start | bytes 1572868
  11.8 0.9 %copy-start.3 = (f32[2,128,128]{2,1,0:T(8,128)S(1)}, f32[2,128,128]{2,1,0:T(8,128)}, u32[]{:S(2)}) copy-start(f32[2,128,128]{2,1,0:T(8,128)} %probe.1) | copy-start | bytes 393220
  14.4 17.4 %copy-start = (bf16[4,2,256,256]{3,2,1,0:T(8,128)(2,1)S(1)}, bf16[4,2,256,256]{3,2,1,0:T(8,128)(2,1)}, u32[]{:S(2)}) copy-start(bf16[4,2,256,256]{3,2,1,0:T(8,128)(2,1)} %constant.75.clone.tables) | copy-start | bytes 3145732
  14.4 17.4 %copy-start.2 = (f32[8,128,128]{2,1,0:T(8,128)S(1)}, f32[8,128,128]{2,1,0:T(8,128)}, u32[]{:S(2)}) copy-start(f32[8,128,128]{2,1,0:T(8,128)} %amplitude.1) | copy-start | bytes 1572868
  36.5 21.0 %all-to-all-start.1 = ((f32[32,8,128]{2,1,0:T(8,128)}), f32[32,8,128]{2,1,0:T(8,128)S(1)}, u32[]{:S(2)}, u32[]{:S(2)}) async-start(f32[32,8,128]{2,1,0:T(8,128)} %get-tuple-element.40), calls=%async_computation.1 | async-start | bytes 262144 | tf_op jit(solution)/shard_map/all_to_all | solution.py:244
  46.9 20.9 %collective-permute-start.1 = (f32[2,2,128,128]{3,2,1,0:T(8,128)S(1)}, f32[2,2,128,128]{3,2,1,0:T(8,128)S(1)}, u32[]{:S(2)}, u32[]{:S(2)}) collective-permute-start(f32[2,2,128,128]{3,2,1,0:T(8,128)S(1)} %get-tuple-element.43), channel_id=1, source_target_pairs={{0,1},{1,2},{2,3},{3,0},{4,5},{5,6},{6,7},{7,4},{8,9},{9,10},{10,1... | collective-permute-start | bytes 786440 | tf_op jit(solution)/shard_map/ppermute | solution.py:240
  50.1 17.8 %collective-permute-start.2 = (f32[2,2,128,128]{3,2,1,0:T(8,128)S(1)}, f32[2,2,128,128]{3,2,1,0:T(8,128)S(1)}, u32[]{:S(2)}, u32[]{:S(2)}) collective-permute-start(f32[2,2,128,128]{3,2,1,0:T(8,128)S(1)} %get-tuple-element.44), channel_id=1, source_target_pairs={{0,2},{1,3},{2,0},{3,1},{4,6},{5,7},{6,4},{7,5},{8,10},{9,11},{10,... | collective-permute-start | bytes 786440 | tf_op jit(solution)/shard_map/ppermute | solution.py:240
  54.4 13.5 %collective-permute-start.3 = (f32[2,2,128,128]{3,2,1,0:T(8,128)S(1)}, f32[2,2,128,128]{3,2,1,0:T(8,128)S(1)}, u32[]{:S(2)}, u32[]{:S(2)}) collective-permute-start(f32[2,2,128,128]{3,2,1,0:T(8,128)S(1)} %get-tuple-element.45), channel_id=1, source_target_pairs={{0,3},{1,0},{2,1},{3,2},{4,7},{5,4},{6,5},{7,6},{8,11},{9,8},{10,9... | collective-permute-start | bytes 786440 | tf_op jit(solution)/shard_map/ppermute | solution.py:240
  58.2 17.5 %all-to-all-start.2 = ((f32[16,8,128]{2,1,0:T(8,128)}), f32[16,8,128]{2,1,0:T(8,128)S(1)}, u32[]{:S(2)}, u32[]{:S(2)}) async-start(f32[16,8,128]{2,1,0:T(8,128)} %total.2), calls=%async_computation.2 | async-start | bytes 131072 | tf_op jit(solution)/shard_map/all_to_all | solution.py:244
  68.6 20.2 %collective-permute-start.4 = (f32[2,136,512]{2,1,0:T(8,128)S(1)}, f32[2,136,512]{2,1,0:T(8,128)S(1)}, u32[]{:S(2)}, u32[]{:S(2)}) collective-permute-start(f32[2,136,512]{2,1,0:T(8,128)S(1)} %get-tuple-element.47), channel_id=1, source_target_pairs={{0,4},{4,8},{8,12},{12,16},{16,20},{20,24},{24,28},{28,32},{32,36}... | collective-permute-start | bytes 1671176 | tf_op jit(solution)/shard_map/ppermute | solution.py:235

commit v10 on v9

--- a/solution.py
+++ b/solution.py
@@ -323,8 +323,10 @@
             **kwargs,
         )(rows)
 
-    probe_rows = total(swap(probe_parts, ("z", "cuts")), ("y", "core"))
     gathered = [terms[0]] + [around(terms[away], away) for away in range(1, cuts)]
+    probe_rows = swap(probe_parts, ("z", "cuts"))
+    probe_rows, gathered[2] = lax.optimization_barrier((probe_rows, gathered[2]))
+    probe_rows = total(probe_rows, ("y", "core"))
     later = after(info, probe_rows)
     estimate = pl.CostEstimate(flops=10**11, bytes_accessed=10**8, transcendentals=0)
     probe_rows = total(swap(probe_rows, ("y", "core")), "z", cost_estimate=estimate)

time: 90.5 us -> 90.5 us (level)
  waiting for transfers between devices: 3.59 us -> 6.46 us
  blocking collectives: 30.4 us -> 27.6 us
    all_to_all x2, blocking collectives: 30.4 us -> 27.6 us  [swap(): return lax.all_to_all(block, axes, 0, 0)]
    all_to_all x2, waiting for transfers between devices: 3.58 us -> 6.44 us  [swap(): return lax.all_to_all(block, axes, 0, 0)]
    all_to_all x2, starting transfers between devices: 20.1 us -> 21.9 us  [swap(): return lax.all_to_all(block, axes, 0, 0)]
    ppermute x3, starting transfers between devices: 10.5 us -> 8.94 us  [around(): lax.ppermute(block, 'cuts', [(i, (i + distance) % count) for i in range(c...]
  transfers between devices with their start and end apart: 7 -> 7, of which waited for: 1 -> 2; matrix products, arithmetic and copies ran while one was open for 0% -> 0% of each run, Pallas kernels for 2% -> 2%
where the time goes in v10:
time: 90.5 us; the launch traced here: 90 us
  starting transfers between devices  43.2 us (48%)
  blocking collectives  27.6 us (30%)
  Pallas kernels  8.68 us (10%)
  waiting for transfers between devices  6.46 us (7%)
  local copies, waits for them, and re-layouts  2.64 us (3%)
  between operations  1.43 us (2%)
    all_to_all x2, blocking collectives, swap(): return lax.all_to_all(block, axes, 0, 0)  27.6 us
    all_to_all x2, starting transfers between devices, swap(): return lax.all_to_all(block, axes, 0, 0)  21.9 us
    ppermute x2, starting transfers between devices, along(): lax.ppermute(block, POS, [(i - distance, i) for i in devices if i - dista...  12.3 us
    ppermute x3, starting transfers between devices, around(): lax.ppermute(block, 'cuts', [(i, (i + distance) % count) for i in range(c...  8.94 us
    all_to_all x2, waiting for transfers between devices, swap(): return lax.all_to_all(block, axes, 0, 0)  6.44 us
    pallas_call x1, Pallas kernels, local(): pl.pallas_call(functools.partial(wave_kernel, 1.0 / math.sqrt(slots * acr...  4.72 us
    unnamed x10, local copies, waits for them, and re-layouts  2.52 us
  transfers between devices with their start and end apart: 7, of which 2 were waited for; matrix products, arithmetic and copies ran while one was open for 0% of the time, Pallas kernels for 2%

profile of v10, /device:TPU:1, one launch (start us, length us, event | category | flops | bytes accessed | tf_op | source)
XLA Modules:
  0.0 90.0 jit_solution(8711095579223208408)
XLA Ops:
  0.6 8.8 %collective-permute-start = (f32[2,128,512]{2,1,0:T(8,128)}, f32[2,128,512]{2,1,0:T(8,128)S(1)}, u32[]{:S(2)}, u32[]{:S(2)}) collective-permute-start(f32[2,128,512]{2,1,0:T(8,128)} %bitcast.4), channel_id=1, source_target_pairs={{4,0},{8,4},{12,8},{16,12},{20,16},{24,20},{28,24},{32,28},{36,32}... | collective-permute-start | bytes 1572872 | tf_op jit(solution)/shard_map/ppermute | solution.py:235
  10.1 0.0 copy-start.4
  10.1 0.1 scatter.12
  10.2 0.6 copy-done.4
  10.8 0.0 copy-start.1
  10.8 1.0 %copy-done.1 = f32[2,1,128,512]{3,2,1,0:T(8,128)S(1)} copy-done((f32[2,1,128,512]{3,2,1,0:T(8,128)S(1)}, f32[2,1,128,512]{3,2,1,0:T(8,128)}, u32[]{:S(2)}) %copy-start.1) | copy-done | bytes 524312
  11.8 0.0 copy-start.3
  11.9 0.9 %copy-done.3 = f32[2,128,128]{2,1,0:T(8,128)S(1)} copy-done((f32[2,128,128]{2,1,0:T(8,128)S(1)}, f32[2,128,128]{2,1,0:T(8,128)}, u32[]{:S(2)}) %copy-start.3) | copy-done | bytes 131096
  12.8 0.5 light.1
  13.3 0.0 collective-permute-done.following
  13.4 0.8 windows.1
  14.2 0.0 copy-start
  14.2 0.0 copy-start.2
  14.2 17.6 %all_to_all.20.patch = f32[4,2,2,128,128]{4,3,2,1,0:T(8,128)S(1)} all-to-all(f32[4,2,2,128,128]{4,3,2,1,0:T(8,128)S(1)} %windows.1), channel_id=1, replica_groups=mesh['z'=8,'y'=8,'core'=2,'cuts'=4] {'cuts'}, dimensions={0} | all-to-all | bytes 2097152 | tf_op jit(solution)/shard_map/all_to_all | solution.py:244
  31.8 0.0 copy-done
  31.8 0.0 copy-done.2
  31.8 4.7 %waves.1 = (f32[2,2,128,128]{3,2,1,0:T(8,128)S(1)}, f32[2,2,128,128]{3,2,1,0:T(8,128)S(1)}, f32[2,2,128,128]{3,2,1,0:T(8,128)S(1)}, f32[2,2,128,128]{3,2,1,0:T(8,128)S(1)}, f32[32,8,128]{2,1,0:T(8,128)}) custom-call(s32[8,128]{1,0:T(8,128)S(1)} %pad.9.info, f32[2,128,128]{2,1,0:T(8,128)S(1)} %get-tuple-element.39.probe, f32[8,128,128]{2,1,0:T(8,128)S(1)} %copy-done.2, ...), custom_call_target="tpu_custom_call" | custom-call | tf_op jit(solution)/shard_map/waves/pallas_call | solution.py:302
  36.5 2.4 %collective-permute-start.1 = (f32[2,2,128,128]{3,2,1,0:T(8,128)S(1)}, f32[2,2,128,128]{3,2,1,0:T(8,128)S(1)}, u32[]{:S(2)}, u32[]{:S(2)}) collective-permute-start(f32[2,2,128,128]{3,2,1,0:T(8,128)S(1)} %get-tuple-element.43), channel_id=1, source_target_pairs={{0,2},{1,3},{2,0},{3,1},{4,6},{5,7},{6,4},{7,5},{8,10},{9,11},{10,... | collective-permute-start | bytes 786440 | tf_op jit(solution)/shard_map/ppermute | solution.py:240
  39.0 12.0 %all-to-all-start.1 = ((f32[32,8,128]{2,1,0:T(8,128)}), f32[32,8,128]{2,1,0:T(8,128)S(1)}, u32[]{:S(2)}, u32[]{:S(2)}) async-start(f32[32,8,128]{2,1,0:T(8,128)} %get-tuple-element.42), calls=%async_computation.1 | async-start | bytes 262144 | tf_op jit(solution)/shard_map/all_to_all | solution.py:244
  50.9 3.1 %collective-permute-start.2 = (f32[2,2,128,128]{3,2,1,0:T(8,128)S(1)}, f32[2,2,128,128]{3,2,1,0:T(8,128)S(1)}, u32[]{:S(2)}, u32[]{:S(2)}) collective-permute-start(f32[2,2,128,128]{3,2,1,0:T(8,128)S(1)} %get-tuple-element.47), channel_id=1, source_target_pairs={{0,1},{1,2},{2,3},{3,0},{4,5},{5,6},{6,7},{7,4},{8,9},{9,10},{10,1... | collective-permute-start | bytes 786440 | tf_op jit(solution)/shard_map/ppermute | solution.py:240
  54.1 3.4 %collective-permute-start.3 = (f32[2,2,128,128]{3,2,1,0:T(8,128)S(1)}, f32[2,2,128,128]{3,2,1,0:T(8,128)S(1)}, u32[]{:S(2)}, u32[]{:S(2)}) collective-permute-start(f32[2,2,128,128]{3,2,1,0:T(8,128)S(1)} %get-tuple-element.49), channel_id=1, source_target_pairs={{0,3},{1,0},{2,1},{3,2},{4,7},{5,4},{6,5},{7,6},{8,11},{9,8},{10,9... | collective-permute-start | bytes 786440 | tf_op jit(solution)/shard_map/ppermute | solution.py:240
  57.4 2.8 %all-to-all-done.1.rows = f32[32,8,128]{2,1,0:T(8,128)S(1)} async-done(((f32[32,8,128]{2,1,0:T(8,128)}), f32[32,8,128]{2,1,0:T(8,128)S(1)}, u32[]{:S(2)}, u32[]{:S(2)}) %all-to-all-start.1) | async-done | bytes 131104 | tf_op jit(solution)/shard_map/all_to_all | solution.py:244
  60.3 0.0 collective-permute-done.1.rest_2_
  60.3 0.7 total.2
  61.0 10.0 %all-to-all-start.2 = ((f32[16,8,128]{2,1,0:T(8,128)}), f32[16,8,128]{2,1,0:T(8,128)S(1)}, u32[]{:S(2)}, u32[]{:S(2)}) async-start(f32[16,8,128]{2,1,0:T(8,128)} %total.2), calls=%async_computation.2 | async-start | bytes 131072 | tf_op jit(solution)/shard_map/all_to_all | solution.py:244
  70.9 0.0 collective-permute-done.2.rest_1_
  70.9 0.0 collective-permute-done.3.rest_3_
  70.9 0.6 scatter.14
  71.6 3.5 %collective-permute-start.4 = (f32[2,136,512]{2,1,0:T(8,128)S(1)}, f32[2,136,512]{2,1,0:T(8,128)S(1)}, u32[]{:S(2)}, u32[]{:S(2)}) collective-permute-start(f32[2,136,512]{2,1,0:T(8,128)S(1)} %get-tuple-element.51), channel_id=1, source_target_pairs={{0,4},{4,8},{8,12},{12,16},{16,20},{20,24},{24,28},{28,32},{32,36}... | collective-permute-start | bytes 1671176 | tf_op jit(solution)/shard_map/ppermute | solution.py:235
  75.1 3.6 %all-to-all-done.2.rows = f32[16,8,128]{2,1,0:T(8,128)S(1)} async-done(((f32[16,8,128]{2,1,0:T(8,128)}), f32[16,8,128]{2,1,0:T(8,128)S(1)}, u32[]{:S(2)}, u32[]{:S(2)}) %all-to-all-start.2) | async-done | bytes 65568 | tf_op jit(solution)/shard_map/all_to_all | solution.py:244
  78.8 10.0 %all_to_all.21.rows = f32[8,8,128]{2,1,0:T(8,128)S(1)} all-to-all(f32[8,8,128]{2,1,0:T(8,128)S(1)} %total.3), channel_id=1, replica_groups=mesh['z'=8,'y'=8,'core'=2,'cuts'=4] {'z'}, dimensions={0} | all-to-all | bytes 65536 | tf_op jit(solution)/shard_map/all_to_all | solution.py:244
  88.8 0.0 collective-permute-done.4.rim
  88.8 1.2 %final.1 = (f32[2,1,128,512]{3,2,1,0:T(8,128)}, f32[2,32,128]{2,1,0:T(8,128)}) custom-call(f32[2,128,512]{2,1,0:T(8,128)S(1)} %get-tuple-element.50.inner, f32[2,136,512]{2,1,0:T(8,128)S(1)} %collective-permute-done.4.rim, f32[128,512]{1,0:T(8,128)S(1)} %light.1, f32[2,128,128]{2,1,0:T(8,128)S(1)} %get-tuple-element.39.probe, f32[8,8,128]{2,1,0:T(8,128)S(1)} %all_to_all.21.rows), custom_call_target="tpu_custom_call" | custom-call | tf_op jit(solution)/shard_map/final/pallas_call | solution.py:345
  (6 shorter events, 0.1 us)
Async XLA Ops:
  0.6 12.7 %collective-permute-start = (f32[2,128,512]{2,1,0:T(8,128)}, f32[2,128,512]{2,1,0:T(8,128)S(1)}, u32[]{:S(2)}, u32[]{:S(2)}) collective-permute-start(f32[2,128,512]{2,1,0:T(8,128)} %bitcast.4), channel_id=1, source_target_pairs={{4,0},{8,4},{12,8},{16,12},{20,16},{24,20},{28,24},{32,28},{36,32}... | collective-permute-start | bytes 1572872 | tf_op jit(solution)/shard_map/ppermute | solution.py:235
  10.1 0.7 copy-start.4
  10.8 1.0 %copy-start.1 = (f32[2,1,128,512]{3,2,1,0:T(8,128)S(1)}, f32[2,1,128,512]{3,2,1,0:T(8,128)}, u32[]{:S(2)}) copy-start(f32[2,1,128,512]{3,2,1,0:T(8,128)} %param.10) | copy-start | bytes 1572868
  11.8 0.9 %copy-start.3 = (f32[2,128,128]{2,1,0:T(8,128)S(1)}, f32[2,128,128]{2,1,0:T(8,128)}, u32[]{:S(2)}) copy-start(f32[2,128,128]{2,1,0:T(8,128)} %probe.1) | copy-start | bytes 393220
  14.2 17.6 %copy-start = (bf16[4,2,256,256]{3,2,1,0:T(8,128)(2,1)S(1)}, bf16[4,2,256,256]{3,2,1,0:T(8,128)(2,1)}, u32[]{:S(2)}) copy-start(bf16[4,2,256,256]{3,2,1,0:T(8,128)(2,1)} %constant.75.clone.tables) | copy-start | bytes 3145732
  14.2 17.6 %copy-start.2 = (f32[8,128,128]{2,1,0:T(8,128)S(1)}, f32[8,128,128]{2,1,0:T(8,128)}, u32[]{:S(2)}) copy-start(f32[8,128,128]{2,1,0:T(8,128)} %amplitude.1) | copy-start | bytes 1572868
  36.5 23.8 %collective-permute-start.1 = (f32[2,2,128,128]{3,2,1,0:T(8,128)S(1)}, f32[2,2,128,128]{3,2,1,0:T(8,128)S(1)}, u32[]{:S(2)}, u32[]{:S(2)}) collective-permute-start(f32[2,2,128,128]{3,2,1,0:T(8,128)S(1)} %get-tuple-element.43), channel_id=1, source_target_pairs={{0,2},{1,3},{2,0},{3,1},{4,6},{5,7},{6,4},{7,5},{8,10},{9,11},{10,... | collective-permute-start | bytes 786440 | tf_op jit(solution)/shard_map/ppermute | solution.py:240
  39.0 21.3 %all-to-all-start.1 = ((f32[32,8,128]{2,1,0:T(8,128)}), f32[32,8,128]{2,1,0:T(8,128)S(1)}, u32[]{:S(2)}, u32[]{:S(2)}) async-start(f32[32,8,128]{2,1,0:T(8,128)} %get-tuple-element.42), calls=%async_computation.1 | async-start | bytes 262144 | tf_op jit(solution)/shard_map/all_to_all | solution.py:244
  50.9 20.0 %collective-permute-start.2 = (f32[2,2,128,128]{3,2,1,0:T(8,128)S(1)}, f32[2,2,128,128]{3,2,1,0:T(8,128)S(1)}, u32[]{:S(2)}, u32[]{:S(2)}) collective-permute-start(f32[2,2,128,128]{3,2,1,0:T(8,128)S(1)} %get-tuple-element.47), channel_id=1, source_target_pairs={{0,1},{1,2},{2,3},{3,0},{4,5},{5,6},{6,7},{7,4},{8,9},{9,10},{10,1... | collective-permute-start | bytes 786440 | tf_op jit(solution)/shard_map/ppermute | solution.py:240
  54.1 16.9 %collective-permute-start.3 = (f32[2,2,128,128]{3,2,1,0:T(8,128)S(1)}, f32[2,2,128,128]{3,2,1,0:T(8,128)S(1)}, u32[]{:S(2)}, u32[]{:S(2)}) collective-permute-start(f32[2,2,128,128]{3,2,1,0:T(8,128)S(1)} %get-tuple-element.49), channel_id=1, source_target_pairs={{0,3},{1,0},{2,1},{3,2},{4,7},{5,4},{6,5},{7,6},{8,11},{9,8},{10,9... | collective-permute-start | bytes 786440 | tf_op jit(solution)/shard_map/ppermute | solution.py:240
  61.0 17.8 %all-to-all-start.2 = ((f32[16,8,128]{2,1,0:T(8,128)}), f32[16,8,128]{2,1,0:T(8,128)S(1)}, u32[]{:S(2)}, u32[]{:S(2)}) async-start(f32[16,8,128]{2,1,0:T(8,128)} %total.2), calls=%async_computation.2 | async-start | bytes 131072 | tf_op jit(solution)/shard_map/all_to_all | solution.py:244
  71.6 17.2 %collective-permute-start.4 = (f32[2,136,512]{2,1,0:T(8,128)S(1)}, f32[2,136,512]{2,1,0:T(8,128)S(1)}, u32[]{:S(2)}, u32[]{:S(2)}) collective-permute-start(f32[2,136,512]{2,1,0:T(8,128)S(1)} %get-tuple-element.51), channel_id=1, source_target_pairs={{0,4},{4,8},{8,12},{12,16},{16,20},{20,24},{24,28},{28,32},{32,36}... | collective-permute-start | bytes 1671176 | tf_op jit(solution)/shard_map/ppermute | solution.py:235

commit v11 on v10

--- a/solution.py
+++ b/solution.py
@@ -121,16 +121,13 @@
     columns = canvas.shape[1]
     power = probe[0] * probe[0] + probe[1] * probe[1]
     rows, cols, (live, *_) = scalars(places, slots)
-    canvas[...] = jnp.zeros_like(canvas)
     for slot in range(slots):
-
-        @pl.when(slot < live)
-        def _():
-            at, down, right = spot(rows[slot], cols[slot], columns, n)
-            canvas[at] = canvas[at] + placed(power, down, right)
+        at, down, right = spot(rows[slot], cols[slot], columns, n)
+        canvas[at] = canvas[at] + placed(jnp.where(slot < live, power, 0.0), down, right)
 
 
 def light_kernel(slots, info, probe, light, canvas):
+    canvas[...] = jnp.ones_like(canvas)
     lit(slots, info[...], probe, canvas)
     light[...] = canvas[: light.shape[0]]
 
@@ -223,8 +220,10 @@
 def final_kernel(slots, inner, rim, light, probe, rows, slice_grad, probe_grad, canvas):
     n = probe.shape[1]
     stripe = light.shape[0]
+    canvas[:stripe] = jnp.zeros_like(light)
+    canvas[stripe:] = light[...]
     lit(slots, rim[0, n:, :n].astype(jnp.int32), probe, canvas)
-    whole = light[...] + canvas[stripe:] + 1.0
+    whole = canvas[stripe:]
     for part in range(2):
         slice_grad[part, 0] = (inner[part] + rim[part, :n]) / whole
     probe_grad[...] = rows[...].reshape(probe_grad.shape)

time: 90.5 us -> 90.6 us (level)
  no operation moved by 1% of the time
where the time goes in v11:
time: 90.6 us; the launch traced here: 90.1 us
  starting transfers between devices  43.1 us (48%)
  blocking collectives  27.8 us (31%)
  Pallas kernels  8.63 us (10%)
  waiting for transfers between devices  6.45 us (7%)
  local copies, waits for them, and re-layouts  2.64 us (3%)
  between operations  1.43 us (2%)
    all_to_all x2, blocking collectives, swap(): return lax.all_to_all(block, axes, 0, 0)  27.8 us
    all_to_all x2, starting transfers between devices, swap(): return lax.all_to_all(block, axes, 0, 0)  21.9 us
    ppermute x2, starting transfers between devices, along(): lax.ppermute(block, POS, [(i - distance, i) for i in devices if i - dista...  12.3 us
    ppermute x3, starting transfers between devices, around(): lax.ppermute(block, 'cuts', [(i, (i + distance) % count) for i in range(c...  8.94 us
    all_to_all x2, waiting for transfers between devices, swap(): return lax.all_to_all(block, axes, 0, 0)  6.44 us
    pallas_call x1, Pallas kernels, local(): pl.pallas_call(functools.partial(wave_kernel, 1.0 / math.sqrt(slots * acr...  4.72 us
    unnamed x10, local copies, waits for them, and re-layouts  2.52 us
  transfers between devices with their start and end apart: 7, of which 2 were waited for; matrix products, arithmetic and copies ran while one was open for 0% of the time, Pallas kernels for 2%

profile of v11, /device:TPU:1, one launch (start us, length us, event | category | flops | bytes accessed | tf_op | source)
XLA Modules:
  0.0 90.1 jit_solution(17366204717545696892)
XLA Ops:
  0.6 8.8 %collective-permute-start = (f32[2,128,512]{2,1,0:T(8,128)}, f32[2,128,512]{2,1,0:T(8,128)S(1)}, u32[]{:S(2)}, u32[]{:S(2)}) collective-permute-start(f32[2,128,512]{2,1,0:T(8,128)} %bitcast.4), channel_id=1, source_target_pairs={{4,0},{8,4},{12,8},{16,12},{20,16},{24,20},{28,24},{32,28},{36,32}... | collective-permute-start | bytes 1572872 | tf_op jit(solution)/shard_map/ppermute | solution.py:234
  10.1 0.0 copy-start.4
  10.1 0.1 scatter.12
  10.2 0.6 copy-done.4
  10.8 0.0 copy-start.1
  10.8 1.0 %copy-done.1 = f32[2,1,128,512]{3,2,1,0:T(8,128)S(1)} copy-done((f32[2,1,128,512]{3,2,1,0:T(8,128)S(1)}, f32[2,1,128,512]{3,2,1,0:T(8,128)}, u32[]{:S(2)}) %copy-start.1) | copy-done | bytes 524312
  11.8 0.0 copy-start.3
  11.9 0.9 %copy-done.3 = f32[2,128,128]{2,1,0:T(8,128)S(1)} copy-done((f32[2,128,128]{2,1,0:T(8,128)S(1)}, f32[2,128,128]{2,1,0:T(8,128)}, u32[]{:S(2)}) %copy-start.3) | copy-done | bytes 131096
  12.8 0.4 light.1
  13.2 0.0 collective-permute-done.following
  13.3 0.8 windows.1
  14.1 0.0 copy-start
  14.1 0.0 copy-start.2
  14.1 17.8 %all_to_all.20.patch = f32[4,2,2,128,128]{4,3,2,1,0:T(8,128)S(1)} all-to-all(f32[4,2,2,128,128]{4,3,2,1,0:T(8,128)S(1)} %windows.1), channel_id=1, replica_groups=mesh['z'=8,'y'=8,'core'=2,'cuts'=4] {'cuts'}, dimensions={0} | all-to-all | bytes 2097152 | tf_op jit(solution)/shard_map/all_to_all | solution.py:243
  31.9 0.0 copy-done
  31.9 0.0 copy-done.2
  31.9 4.7 %waves.1 = (f32[2,2,128,128]{3,2,1,0:T(8,128)S(1)}, f32[2,2,128,128]{3,2,1,0:T(8,128)S(1)}, f32[2,2,128,128]{3,2,1,0:T(8,128)S(1)}, f32[2,2,128,128]{3,2,1,0:T(8,128)S(1)}, f32[32,8,128]{2,1,0:T(8,128)}) custom-call(s32[8,128]{1,0:T(8,128)S(1)} %pad.9.info, f32[2,128,128]{2,1,0:T(8,128)S(1)} %get-tuple-element.39.probe, f32[8,128,128]{2,1,0:T(8,128)S(1)} %copy-done.2, ...), custom_call_target="tpu_custom_call" | custom-call | tf_op jit(solution)/shard_map/waves/pallas_call | solution.py:301
  36.6 2.4 %collective-permute-start.1 = (f32[2,2,128,128]{3,2,1,0:T(8,128)S(1)}, f32[2,2,128,128]{3,2,1,0:T(8,128)S(1)}, u32[]{:S(2)}, u32[]{:S(2)}) collective-permute-start(f32[2,2,128,128]{3,2,1,0:T(8,128)S(1)} %get-tuple-element.43), channel_id=1, source_target_pairs={{0,2},{1,3},{2,0},{3,1},{4,6},{5,7},{6,4},{7,5},{8,10},{9,11},{10,... | collective-permute-start | bytes 786440 | tf_op jit(solution)/shard_map/ppermute | solution.py:239
  39.0 11.9 %all-to-all-start.1 = ((f32[32,8,128]{2,1,0:T(8,128)}), f32[32,8,128]{2,1,0:T(8,128)S(1)}, u32[]{:S(2)}, u32[]{:S(2)}) async-start(f32[32,8,128]{2,1,0:T(8,128)} %get-tuple-element.42), calls=%async_computation.1 | async-start | bytes 262144 | tf_op jit(solution)/shard_map/all_to_all | solution.py:243
  50.9 3.1 %collective-permute-start.2 = (f32[2,2,128,128]{3,2,1,0:T(8,128)S(1)}, f32[2,2,128,128]{3,2,1,0:T(8,128)S(1)}, u32[]{:S(2)}, u32[]{:S(2)}) collective-permute-start(f32[2,2,128,128]{3,2,1,0:T(8,128)S(1)} %get-tuple-element.47), channel_id=1, source_target_pairs={{0,1},{1,2},{2,3},{3,0},{4,5},{5,6},{6,7},{7,4},{8,9},{9,10},{10,1... | collective-permute-start | bytes 786440 | tf_op jit(solution)/shard_map/ppermute | solution.py:239
  54.1 3.4 %collective-permute-start.3 = (f32[2,2,128,128]{3,2,1,0:T(8,128)S(1)}, f32[2,2,128,128]{3,2,1,0:T(8,128)S(1)}, u32[]{:S(2)}, u32[]{:S(2)}) collective-permute-start(f32[2,2,128,128]{3,2,1,0:T(8,128)S(1)} %get-tuple-element.49), channel_id=1, source_target_pairs={{0,3},{1,0},{2,1},{3,2},{4,7},{5,4},{6,5},{7,6},{8,11},{9,8},{10,9... | collective-permute-start | bytes 786440 | tf_op jit(solution)/shard_map/ppermute | solution.py:239
  57.4 2.8 %all-to-all-done.1.rows = f32[32,8,128]{2,1,0:T(8,128)S(1)} async-done(((f32[32,8,128]{2,1,0:T(8,128)}), f32[32,8,128]{2,1,0:T(8,128)S(1)}, u32[]{:S(2)}, u32[]{:S(2)}) %all-to-all-start.1) | async-done | bytes 131104 | tf_op jit(solution)/shard_map/all_to_all | solution.py:243
  60.3 0.0 collective-permute-done.1.rest_2_
  60.3 0.7 total.2
  61.0 10.0 %all-to-all-start.2 = ((f32[16,8,128]{2,1,0:T(8,128)}), f32[16,8,128]{2,1,0:T(8,128)S(1)}, u32[]{:S(2)}, u32[]{:S(2)}) async-start(f32[16,8,128]{2,1,0:T(8,128)} %total.2), calls=%async_computation.2 | async-start | bytes 131072 | tf_op jit(solution)/shard_map/all_to_all | solution.py:243
  70.9 0.0 collective-permute-done.2.rest_1_
  70.9 0.0 collective-permute-done.3.rest_3_
  70.9 0.6 scatter.14
  71.6 3.6 %collective-permute-start.4 = (f32[2,136,512]{2,1,0:T(8,128)S(1)}, f32[2,136,512]{2,1,0:T(8,128)S(1)}, u32[]{:S(2)}, u32[]{:S(2)}) collective-permute-start(f32[2,136,512]{2,1,0:T(8,128)S(1)} %get-tuple-element.51), channel_id=1, source_target_pairs={{0,4},{4,8},{8,12},{12,16},{16,20},{20,24},{24,28},{28,32},{32,36}... | collective-permute-start | bytes 1671176 | tf_op jit(solution)/shard_map/ppermute | solution.py:234
  75.1 3.6 %all-to-all-done.2.rows = f32[16,8,128]{2,1,0:T(8,128)S(1)} async-done(((f32[16,8,128]{2,1,0:T(8,128)}), f32[16,8,128]{2,1,0:T(8,128)S(1)}, u32[]{:S(2)}, u32[]{:S(2)}) %all-to-all-start.2) | async-done | bytes 65568 | tf_op jit(solution)/shard_map/all_to_all | solution.py:243
  78.8 10.0 %all_to_all.21.rows = f32[8,8,128]{2,1,0:T(8,128)S(1)} all-to-all(f32[8,8,128]{2,1,0:T(8,128)S(1)} %total.3), channel_id=1, replica_groups=mesh['z'=8,'y'=8,'core'=2,'cuts'=4] {'z'}, dimensions={0} | all-to-all | bytes 65536 | tf_op jit(solution)/shard_map/all_to_all | solution.py:243
  88.8 0.0 collective-permute-done.4.rim
  88.8 1.3 %final.1 = (f32[2,1,128,512]{3,2,1,0:T(8,128)}, f32[2,32,128]{2,1,0:T(8,128)}) custom-call(f32[2,128,512]{2,1,0:T(8,128)S(1)} %get-tuple-element.50.inner, f32[2,136,512]{2,1,0:T(8,128)S(1)} %collective-permute-done.4.rim, f32[128,512]{1,0:T(8,128)S(1)} %light.1, f32[2,128,128]{2,1,0:T(8,128)S(1)} %get-tuple-element.39.probe, f32[8,8,128]{2,1,0:T(8,128)S(1)} %all_to_all.21.rows), custom_call_target="tpu_custom_call" | custom-call | tf_op jit(solution)/shard_map/final/pallas_call | solution.py:344
  (6 shorter events, 0.1 us)
Async XLA Ops:
  0.6 12.6 %collective-permute-start = (f32[2,128,512]{2,1,0:T(8,128)}, f32[2,128,512]{2,1,0:T(8,128)S(1)}, u32[]{:S(2)}, u32[]{:S(2)}) collective-permute-start(f32[2,128,512]{2,1,0:T(8,128)} %bitcast.4), channel_id=1, source_target_pairs={{4,0},{8,4},{12,8},{16,12},{20,16},{24,20},{28,24},{32,28},{36,32}... | collective-permute-start | bytes 1572872 | tf_op jit(solution)/shard_map/ppermute | solution.py:234
  10.1 0.7 copy-start.4
  10.8 1.0 %copy-start.1 = (f32[2,1,128,512]{3,2,1,0:T(8,128)S(1)}, f32[2,1,128,512]{3,2,1,0:T(8,128)}, u32[]{:S(2)}) copy-start(f32[2,1,128,512]{3,2,1,0:T(8,128)} %param.10) | copy-start | bytes 1572868
  11.8 0.9 %copy-start.3 = (f32[2,128,128]{2,1,0:T(8,128)S(1)}, f32[2,128,128]{2,1,0:T(8,128)}, u32[]{:S(2)}) copy-start(f32[2,128,128]{2,1,0:T(8,128)} %probe.1) | copy-start | bytes 393220
  14.1 17.8 %copy-start = (bf16[4,2,256,256]{3,2,1,0:T(8,128)(2,1)S(1)}, bf16[4,2,256,256]{3,2,1,0:T(8,128)(2,1)}, u32[]{:S(2)}) copy-start(bf16[4,2,256,256]{3,2,1,0:T(8,128)(2,1)} %constant.75.clone.tables) | copy-start | bytes 3145732
  14.1 17.8 %copy-start.2 = (f32[8,128,128]{2,1,0:T(8,128)S(1)}, f32[8,128,128]{2,1,0:T(8,128)}, u32[]{:S(2)}) copy-start(f32[8,128,128]{2,1,0:T(8,128)} %amplitude.1) | copy-start | bytes 1572868
  36.6 23.7 %collective-permute-start.1 = (f32[2,2,128,128]{3,2,1,0:T(8,128)S(1)}, f32[2,2,128,128]{3,2,1,0:T(8,128)S(1)}, u32[]{:S(2)}, u32[]{:S(2)}) collective-permute-start(f32[2,2,128,128]{3,2,1,0:T(8,128)S(1)} %get-tuple-element.43), channel_id=1, source_target_pairs={{0,2},{1,3},{2,0},{3,1},{4,6},{5,7},{6,4},{7,5},{8,10},{9,11},{10,... | collective-permute-start | bytes 786440 | tf_op jit(solution)/shard_map/ppermute | solution.py:239
  39.0 21.2 %all-to-all-start.1 = ((f32[32,8,128]{2,1,0:T(8,128)}), f32[32,8,128]{2,1,0:T(8,128)S(1)}, u32[]{:S(2)}, u32[]{:S(2)}) async-start(f32[32,8,128]{2,1,0:T(8,128)} %get-tuple-element.42), calls=%async_computation.1 | async-start | bytes 262144 | tf_op jit(solution)/shard_map/all_to_all | solution.py:243
  50.9 20.0 %collective-permute-start.2 = (f32[2,2,128,128]{3,2,1,0:T(8,128)S(1)}, f32[2,2,128,128]{3,2,1,0:T(8,128)S(1)}, u32[]{:S(2)}, u32[]{:S(2)}) collective-permute-start(f32[2,2,128,128]{3,2,1,0:T(8,128)S(1)} %get-tuple-element.47), channel_id=1, source_target_pairs={{0,1},{1,2},{2,3},{3,0},{4,5},{5,6},{6,7},{7,4},{8,9},{9,10},{10,1... | collective-permute-start | bytes 786440 | tf_op jit(solution)/shard_map/ppermute | solution.py:239
  54.1 16.9 %collective-permute-start.3 = (f32[2,2,128,128]{3,2,1,0:T(8,128)S(1)}, f32[2,2,128,128]{3,2,1,0:T(8,128)S(1)}, u32[]{:S(2)}, u32[]{:S(2)}) collective-permute-start(f32[2,2,128,128]{3,2,1,0:T(8,128)S(1)} %get-tuple-element.49), channel_id=1, source_target_pairs={{0,3},{1,0},{2,1},{3,2},{4,7},{5,4},{6,5},{7,6},{8,11},{9,8},{10,9... | collective-permute-start | bytes 786440 | tf_op jit(solution)/shard_map/ppermute | solution.py:239
  61.0 17.8 %all-to-all-start.2 = ((f32[16,8,128]{2,1,0:T(8,128)}), f32[16,8,128]{2,1,0:T(8,128)S(1)}, u32[]{:S(2)}, u32[]{:S(2)}) async-start(f32[16,8,128]{2,1,0:T(8,128)} %total.2), calls=%async_computation.2 | async-start | bytes 131072 | tf_op jit(solution)/shard_map/all_to_all | solution.py:243
  71.6 17.2 %collective-permute-start.4 = (f32[2,136,512]{2,1,0:T(8,128)S(1)}, f32[2,136,512]{2,1,0:T(8,128)S(1)}, u32[]{:S(2)}, u32[]{:S(2)}) collective-permute-start(f32[2,136,512]{2,1,0:T(8,128)S(1)} %get-tuple-element.51), channel_id=1, source_target_pairs={{0,4},{4,8},{8,12},{12,16},{16,20},{20,24},{24,28},{28,32},{32,36}... | collective-permute-start | bytes 1671176 | tf_op jit(solution)/shard_map/ppermute | solution.py:234

commit v12 on v11

--- a/solution.py
+++ b/solution.py
@@ -296,7 +296,7 @@
     )(after(info, light), own, following)
     patches = swap(windows, "cuts")
 
-    shares = lax.axis_size(("z", "cuts"))
+    shares = lax.axis_size(("y", "cuts"))
     packet = jax.ShapeDtypeStruct((pair, 2, n, n), jnp.float32)
     *terms, probe_parts = pl.pallas_call(
         functools.partial(wave_kernel, 1.0 / math.sqrt(slots * across)),
@@ -323,12 +323,12 @@
         )(rows)
 
     gathered = [terms[0]] + [around(terms[away], away) for away in range(1, cuts)]
-    probe_rows = swap(probe_parts, ("z", "cuts"))
+    probe_rows = swap(probe_parts, ("y", "cuts"))
     probe_rows, gathered[2] = lax.optimization_barrier((probe_rows, gathered[2]))
-    probe_rows = total(probe_rows, ("y", "core"))
+    probe_rows = total(probe_rows, ("z", "core"))
     later = after(info, probe_rows)
     estimate = pl.CostEstimate(flops=10**11, bytes_accessed=10**8, transcendentals=0)
-    probe_rows = total(swap(probe_rows, ("y", "core")), "z", cost_estimate=estimate)
+    probe_rows = total(swap(probe_rows, ("z", "core")), "y", cost_estimate=estimate)
 
     inner, rim = pl.pallas_call(
         scatter_kernel,
@@ -340,7 +340,7 @@
         name="scatter",
     )(later, *gathered)
     rim_in = along(rim, 1)
-    probe_rows = swap(probe_rows, "z")
+    probe_rows = swap(probe_rows, "y")
     slice_grad, probe_grad = pl.pallas_call(
         functools.partial(final_kernel, slots),
         out_shape=[

time: 90.6 us -> 90.6 us (level)
  waiting for transfers between devices: 6.45 us -> 7.37 us
    ppermute x2, starting transfers between devices: 12.3 us -> 11.4 us  [along(): lax.ppermute(block, POS, [(i - distance, i) for i in devices if i - dista...]
    all_to_all x2, waiting for transfers between devices: 6.44 us -> 7.35 us  [swap(): return lax.all_to_all(block, axes, 0, 0)]
where the time goes in v12:
time: 90.6 us; the launch traced here: 90.1 us
  starting transfers between devices  42.2 us (47%)
  blocking collectives  27.8 us (31%)
  Pallas kernels  8.65 us (10%)
  waiting for transfers between devices  7.37 us (8%)
  local copies, waits for them, and re-layouts  2.64 us (3%)
  between operations  1.43 us (2%)
    all_to_all x2, blocking collectives, swap(): return lax.all_to_all(block, axes, 0, 0)  27.8 us
    all_to_all x2, starting transfers between devices, swap(): return lax.all_to_all(block, axes, 0, 0)  21.9 us
    ppermute x2, starting transfers between devices, along(): lax.ppermute(block, POS, [(i - distance, i) for i in devices if i - dista...  11.4 us
    ppermute x3, starting transfers between devices, around(): lax.ppermute(block, 'cuts', [(i, (i + distance) % count) for i in range(c...  8.94 us
    all_to_all x2, waiting for transfers between devices, swap(): return lax.all_to_all(block, axes, 0, 0)  7.35 us
    pallas_call x1, Pallas kernels, local(): pl.pallas_call(functools.partial(wave_kernel, 1.0 / math.sqrt(slots * acr...  4.72 us
    unnamed x10, local copies, waits for them, and re-layouts  2.52 us
  transfers between devices with their start and end apart: 7, of which 2 were waited for; matrix products, arithmetic and copies ran while one was open for 0% of the time, Pallas kernels for 2%

profile of v12, /device:TPU:1, one launch (start us, length us, event | category | flops | bytes accessed | tf_op | source)
XLA Modules:
  0.0 90.1 jit_solution(4011017180339721511)
XLA Ops:
  0.6 8.8 %collective-permute-start = (f32[2,128,512]{2,1,0:T(8,128)}, f32[2,128,512]{2,1,0:T(8,128)S(1)}, u32[]{:S(2)}, u32[]{:S(2)}) collective-permute-start(f32[2,128,512]{2,1,0:T(8,128)} %bitcast.4), channel_id=1, source_target_pairs={{4,0},{8,4},{12,8},{16,12},{20,16},{24,20},{28,24},{32,28},{36,32}... | collective-permute-start | bytes 1572872 | tf_op jit(solution)/shard_map/ppermute | solution.py:234
  10.1 0.0 copy-start.4
  10.1 0.1 scatter.12
  10.2 0.6 copy-done.4
  10.8 0.0 copy-start.1
  10.8 1.0 %copy-done.1 = f32[2,1,128,512]{3,2,1,0:T(8,128)S(1)} copy-done((f32[2,1,128,512]{3,2,1,0:T(8,128)S(1)}, f32[2,1,128,512]{3,2,1,0:T(8,128)}, u32[]{:S(2)}) %copy-start.1) | copy-done | bytes 524312
  11.8 0.0 copy-start.3
  11.9 0.9 %copy-done.3 = f32[2,128,128]{2,1,0:T(8,128)S(1)} copy-done((f32[2,128,128]{2,1,0:T(8,128)S(1)}, f32[2,128,128]{2,1,0:T(8,128)}, u32[]{:S(2)}) %copy-start.3) | copy-done | bytes 131096
  12.8 0.4 light.1
  13.2 0.0 collective-permute-done.following
  13.3 0.8 windows.1
  14.1 0.0 copy-start
  14.1 0.0 copy-start.2
  14.1 17.8 %all_to_all.20.patch = f32[4,2,2,128,128]{4,3,2,1,0:T(8,128)S(1)} all-to-all(f32[4,2,2,128,128]{4,3,2,1,0:T(8,128)S(1)} %windows.1), channel_id=1, replica_groups=mesh['z'=8,'y'=8,'core'=2,'cuts'=4] {'cuts'}, dimensions={0} | all-to-all | bytes 2097152 | tf_op jit(solution)/shard_map/all_to_all | solution.py:243
  31.9 0.0 copy-done
  31.9 0.0 copy-done.2
  31.9 4.7 %waves.1 = (f32[2,2,128,128]{3,2,1,0:T(8,128)S(1)}, f32[2,2,128,128]{3,2,1,0:T(8,128)S(1)}, f32[2,2,128,128]{3,2,1,0:T(8,128)S(1)}, f32[2,2,128,128]{3,2,1,0:T(8,128)S(1)}, f32[32,8,128]{2,1,0:T(8,128)}) custom-call(s32[8,128]{1,0:T(8,128)S(1)} %pad.9.info, f32[2,128,128]{2,1,0:T(8,128)S(1)} %get-tuple-element.39.probe, f32[8,128,128]{2,1,0:T(8,128)S(1)} %copy-done.2, ...), custom_call_target="tpu_custom_call" | custom-call | tf_op jit(solution)/shard_map/waves/pallas_call | solution.py:301
  36.6 2.4 %collective-permute-start.1 = (f32[2,2,128,128]{3,2,1,0:T(8,128)S(1)}, f32[2,2,128,128]{3,2,1,0:T(8,128)S(1)}, u32[]{:S(2)}, u32[]{:S(2)}) collective-permute-start(f32[2,2,128,128]{3,2,1,0:T(8,128)S(1)} %get-tuple-element.43), channel_id=1, source_target_pairs={{0,2},{1,3},{2,0},{3,1},{4,6},{5,7},{6,4},{7,5},{8,10},{9,11},{10,... | collective-permute-start | bytes 786440 | tf_op jit(solution)/shard_map/ppermute | solution.py:239
  39.0 9.5 %all-to-all-start.1 = ((f32[32,8,128]{2,1,0:T(8,128)}), f32[32,8,128]{2,1,0:T(8,128)S(1)}, u32[]{:S(2)}, u32[]{:S(2)}) async-start(f32[32,8,128]{2,1,0:T(8,128)} %get-tuple-element.42), calls=%async_computation.1 | async-start | bytes 262144 | tf_op jit(solution)/shard_map/all_to_all | solution.py:243
  48.5 3.1 %collective-permute-start.2 = (f32[2,2,128,128]{3,2,1,0:T(8,128)S(1)}, f32[2,2,128,128]{3,2,1,0:T(8,128)S(1)}, u32[]{:S(2)}, u32[]{:S(2)}) collective-permute-start(f32[2,2,128,128]{3,2,1,0:T(8,128)S(1)} %get-tuple-element.47), channel_id=1, source_target_pairs={{0,1},{1,2},{2,3},{3,0},{4,5},{5,6},{6,7},{7,4},{8,9},{9,10},{10,1... | collective-permute-start | bytes 786440 | tf_op jit(solution)/shard_map/ppermute | solution.py:239
  51.7 3.4 %collective-permute-start.3 = (f32[2,2,128,128]{3,2,1,0:T(8,128)S(1)}, f32[2,2,128,128]{3,2,1,0:T(8,128)S(1)}, u32[]{:S(2)}, u32[]{:S(2)}) collective-permute-start(f32[2,2,128,128]{3,2,1,0:T(8,128)S(1)} %get-tuple-element.49), channel_id=1, source_target_pairs={{0,3},{1,0},{2,1},{3,2},{4,7},{5,4},{6,5},{7,6},{8,11},{9,8},{10,9... | collective-permute-start | bytes 786440 | tf_op jit(solution)/shard_map/ppermute | solution.py:239
  55.0 2.8 %all-to-all-done.1.rows = f32[32,8,128]{2,1,0:T(8,128)S(1)} async-done(((f32[32,8,128]{2,1,0:T(8,128)}), f32[32,8,128]{2,1,0:T(8,128)S(1)}, u32[]{:S(2)}, u32[]{:S(2)}) %all-to-all-start.1) | async-done | bytes 131104 | tf_op jit(solution)/shard_map/all_to_all | solution.py:243
  57.9 0.0 collective-permute-done.1.rest_2_
  57.9 0.7 total.2
  58.5 12.4 %all-to-all-start.2 = ((f32[16,8,128]{2,1,0:T(8,128)}), f32[16,8,128]{2,1,0:T(8,128)S(1)}, u32[]{:S(2)}, u32[]{:S(2)}) async-start(f32[16,8,128]{2,1,0:T(8,128)} %total.2), calls=%async_computation.2 | async-start | bytes 131072 | tf_op jit(solution)/shard_map/all_to_all | solution.py:243
  70.9 0.0 collective-permute-done.2.rest_1_
  70.9 0.0 collective-permute-done.3.rest_3_
  71.0 0.7 scatter.14
  71.6 2.6 %collective-permute-start.4 = (f32[2,136,512]{2,1,0:T(8,128)S(1)}, f32[2,136,512]{2,1,0:T(8,128)S(1)}, u32[]{:S(2)}, u32[]{:S(2)}) collective-permute-start(f32[2,136,512]{2,1,0:T(8,128)S(1)} %get-tuple-element.51), channel_id=1, source_target_pairs={{0,4},{4,8},{8,12},{12,16},{16,20},{20,24},{24,28},{28,32},{32,36}... | collective-permute-start | bytes 1671176 | tf_op jit(solution)/shard_map/ppermute | solution.py:234
  74.2 4.5 %all-to-all-done.2.rows = f32[16,8,128]{2,1,0:T(8,128)S(1)} async-done(((f32[16,8,128]{2,1,0:T(8,128)}), f32[16,8,128]{2,1,0:T(8,128)S(1)}, u32[]{:S(2)}, u32[]{:S(2)}) %all-to-all-start.2) | async-done | bytes 65568 | tf_op jit(solution)/shard_map/all_to_all | solution.py:243
  78.8 10.0 %all_to_all.21.rows = f32[8,8,128]{2,1,0:T(8,128)S(1)} all-to-all(f32[8,8,128]{2,1,0:T(8,128)S(1)} %total.3), channel_id=1, replica_groups=mesh['z'=8,'y'=8,'core'=2,'cuts'=4] {'y'}, dimensions={0} | all-to-all | bytes 65536 | tf_op jit(solution)/shard_map/all_to_all | solution.py:243
  88.8 0.0 collective-permute-done.4.rim
  88.8 1.3 %final.1 = (f32[2,1,128,512]{3,2,1,0:T(8,128)}, f32[2,32,128]{2,1,0:T(8,128)}) custom-call(f32[2,128,512]{2,1,0:T(8,128)S(1)} %get-tuple-element.50.inner, f32[2,136,512]{2,1,0:T(8,128)S(1)} %collective-permute-done.4.rim, f32[128,512]{1,0:T(8,128)S(1)} %light.1, f32[2,128,128]{2,1,0:T(8,128)S(1)} %get-tuple-element.39.probe, f32[8,8,128]{2,1,0:T(8,128)S(1)} %all_to_all.21.rows), custom_call_target="tpu_custom_call" | custom-call | tf_op jit(solution)/shard_map/final/pallas_call | solution.py:344
  (6 shorter events, 0.1 us)
Async XLA Ops:
  0.6 12.6 %collective-permute-start = (f32[2,128,512]{2,1,0:T(8,128)}, f32[2,128,512]{2,1,0:T(8,128)S(1)}, u32[]{:S(2)}, u32[]{:S(2)}) collective-permute-start(f32[2,128,512]{2,1,0:T(8,128)} %bitcast.4), channel_id=1, source_target_pairs={{4,0},{8,4},{12,8},{16,12},{20,16},{24,20},{28,24},{32,28},{36,32}... | collective-permute-start | bytes 1572872 | tf_op jit(solution)/shard_map/ppermute | solution.py:234
  10.1 0.7 copy-start.4
  10.8 1.0 %copy-start.1 = (f32[2,1,128,512]{3,2,1,0:T(8,128)S(1)}, f32[2,1,128,512]{3,2,1,0:T(8,128)}, u32[]{:S(2)}) copy-start(f32[2,1,128,512]{3,2,1,0:T(8,128)} %param.10) | copy-start | bytes 1572868
  11.8 0.9 %copy-start.3 = (f32[2,128,128]{2,1,0:T(8,128)S(1)}, f32[2,128,128]{2,1,0:T(8,128)}, u32[]{:S(2)}) copy-start(f32[2,128,128]{2,1,0:T(8,128)} %probe.1) | copy-start | bytes 393220
  14.1 17.8 %copy-start = (bf16[4,2,256,256]{3,2,1,0:T(8,128)(2,1)S(1)}, bf16[4,2,256,256]{3,2,1,0:T(8,128)(2,1)}, u32[]{:S(2)}) copy-start(bf16[4,2,256,256]{3,2,1,0:T(8,128)(2,1)} %constant.75.clone.tables) | copy-start | bytes 3145732
  14.1 17.8 %copy-start.2 = (f32[8,128,128]{2,1,0:T(8,128)S(1)}, f32[8,128,128]{2,1,0:T(8,128)}, u32[]{:S(2)}) copy-start(f32[8,128,128]{2,1,0:T(8,128)} %amplitude.1) | copy-start | bytes 1572868
  36.6 21.3 %collective-permute-start.1 = (f32[2,2,128,128]{3,2,1,0:T(8,128)S(1)}, f32[2,2,128,128]{3,2,1,0:T(8,128)S(1)}, u32[]{:S(2)}, u32[]{:S(2)}) collective-permute-start(f32[2,2,128,128]{3,2,1,0:T(8,128)S(1)} %get-tuple-element.43), channel_id=1, source_target_pairs={{0,2},{1,3},{2,0},{3,1},{4,6},{5,7},{6,4},{7,5},{8,10},{9,11},{10,... | collective-permute-start | bytes 786440 | tf_op jit(solution)/shard_map/ppermute | solution.py:239
  39.0 18.8 %all-to-all-start.1 = ((f32[32,8,128]{2,1,0:T(8,128)}), f32[32,8,128]{2,1,0:T(8,128)S(1)}, u32[]{:S(2)}, u32[]{:S(2)}) async-start(f32[32,8,128]{2,1,0:T(8,128)} %get-tuple-element.42), calls=%async_computation.1 | async-start | bytes 262144 | tf_op jit(solution)/shard_map/all_to_all | solution.py:243
  48.5 22.4 %collective-permute-start.2 = (f32[2,2,128,128]{3,2,1,0:T(8,128)S(1)}, f32[2,2,128,128]{3,2,1,0:T(8,128)S(1)}, u32[]{:S(2)}, u32[]{:S(2)}) collective-permute-start(f32[2,2,128,128]{3,2,1,0:T(8,128)S(1)} %get-tuple-element.47), channel_id=1, source_target_pairs={{0,1},{1,2},{2,3},{3,0},{4,5},{5,6},{6,7},{7,4},{8,9},{9,10},{10,1... | collective-permute-start | bytes 786440 | tf_op jit(solution)/shard_map/ppermute | solution.py:239
  51.7 19.3 %collective-permute-start.3 = (f32[2,2,128,128]{3,2,1,0:T(8,128)S(1)}, f32[2,2,128,128]{3,2,1,0:T(8,128)S(1)}, u32[]{:S(2)}, u32[]{:S(2)}) collective-permute-start(f32[2,2,128,128]{3,2,1,0:T(8,128)S(1)} %get-tuple-element.49), channel_id=1, source_target_pairs={{0,3},{1,0},{2,1},{3,2},{4,7},{5,4},{6,5},{7,6},{8,11},{9,8},{10,9... | collective-permute-start | bytes 786440 | tf_op jit(solution)/shard_map/ppermute | solution.py:239
  58.5 20.2 %all-to-all-start.2 = ((f32[16,8,128]{2,1,0:T(8,128)}), f32[16,8,128]{2,1,0:T(8,128)S(1)}, u32[]{:S(2)}, u32[]{:S(2)}) async-start(f32[16,8,128]{2,1,0:T(8,128)} %total.2), calls=%async_computation.2 | async-start | bytes 131072 | tf_op jit(solution)/shard_map/all_to_all | solution.py:243
  71.6 17.2 %collective-permute-start.4 = (f32[2,136,512]{2,1,0:T(8,128)S(1)}, f32[2,136,512]{2,1,0:T(8,128)S(1)}, u32[]{:S(2)}, u32[]{:S(2)}) collective-permute-start(f32[2,136,512]{2,1,0:T(8,128)S(1)} %get-tuple-element.51), channel_id=1, source_target_pairs={{0,4},{4,8},{8,12},{12,16},{16,20},{20,24},{24,28},{28,32},{32,36}... | collective-permute-start | bytes 1671176 | tf_op jit(solution)/shard_map/ppermute | solution.py:234

commit v13 on v12

--- a/solution.py
+++ b/solution.py
@@ -90,12 +90,12 @@
 
 def cut_out(box, down, right):
     n = box.shape[1] // 2
-    turn = lax.rem(n - right, n)
     lane = lax.broadcasted_iota(jnp.int32, (n + 8, n), 1)
-    wide = jnp.where(lane < n - right, pltpu.roll(box[:, :n], turn, axis=1), pltpu.roll(box[:, n:], turn, axis=1))
-    groups = pltpu.roll(wide.reshape(n // 8 + 1, 8, n), lax.rem(8 - down, 8), axis=1)
+    wide = jnp.where(lane >= right, box[:, :n], box[:, n:])
+    groups = pltpu.roll(wide, lax.rem(n - right, n), axis=1).reshape(n // 8 + 1, 8, n)
     line = lax.broadcasted_iota(jnp.int32, (n // 8, 8, n), 1)
-    return jnp.where(line < 8 - down, groups[:-1], groups[1:]).reshape(n, n)
+    chosen = jnp.where(line >= down, groups[:-1], groups[1:])
+    return pltpu.roll(chosen, lax.rem(8 - down, 8), axis=1).reshape(n, n)
 
 
 def placed(value, down, right):

time: 90.6 us -> 90.3 us (level)
  no operation moved by 1% of the time
where the time goes in v13:
time: 90.3 us; the launch traced here: 89.8 us
  starting transfers between devices  42.2 us (47%)
  blocking collectives  27.8 us (31%)
  Pallas kernels  8.37 us (9%)
  waiting for transfers between devices  7.37 us (8%)
  local copies, waits for them, and re-layouts  2.64 us (3%)
  between operations  1.43 us (2%)
    all_to_all x2, blocking collectives, swap(): return lax.all_to_all(block, axes, 0, 0)  27.8 us
    all_to_all x2, starting transfers between devices, swap(): return lax.all_to_all(block, axes, 0, 0)  21.9 us
    ppermute x2, starting transfers between devices, along(): lax.ppermute(block, POS, [(i - distance, i) for i in devices if i - dista...  11.4 us
    ppermute x3, starting transfers between devices, around(): lax.ppermute(block, 'cuts', [(i, (i + distance) % count) for i in range(c...  8.94 us
    all_to_all x2, waiting for transfers between devices, swap(): return lax.all_to_all(block, axes, 0, 0)  7.36 us
    pallas_call x1, Pallas kernels, local(): pl.pallas_call(functools.partial(wave_kernel, 1.0 / math.sqrt(slots * acr...  4.72 us
    unnamed x10, local copies, waits for them, and re-layouts  2.52 us
  transfers between devices with their start and end apart: 7, of which 2 were waited for; matrix products, arithmetic and copies ran while one was open for 0% of the time, Pallas kernels for 2%

profile of v13, /device:TPU:1, one launch (start us, length us, event | category | flops | bytes accessed | tf_op | source)
XLA Modules:
  0.0 89.8 jit_solution(10888428481461647074)
XLA Ops:
  0.6 8.8 %collective-permute-start = (f32[2,128,512]{2,1,0:T(8,128)}, f32[2,128,512]{2,1,0:T(8,128)S(1)}, u32[]{:S(2)}, u32[]{:S(2)}) collective-permute-start(f32[2,128,512]{2,1,0:T(8,128)} %bitcast.4), channel_id=1, source_target_pairs={{4,0},{8,4},{12,8},{16,12},{20,16},{24,20},{28,24},{32,28},{36,32}... | collective-permute-start | bytes 1572872 | tf_op jit(solution)/shard_map/ppermute | solution.py:234
  10.1 0.0 copy-start.4
  10.1 0.1 scatter.12
  10.2 0.6 copy-done.4
  10.8 0.0 copy-start.1
  10.8 1.0 %copy-done.1 = f32[2,1,128,512]{3,2,1,0:T(8,128)S(1)} copy-done((f32[2,1,128,512]{3,2,1,0:T(8,128)S(1)}, f32[2,1,128,512]{3,2,1,0:T(8,128)}, u32[]{:S(2)}) %copy-start.1) | copy-done | bytes 524312
  11.8 0.0 copy-start.3
  11.9 0.9 %copy-done.3 = f32[2,128,128]{2,1,0:T(8,128)S(1)} copy-done((f32[2,128,128]{2,1,0:T(8,128)S(1)}, f32[2,128,128]{2,1,0:T(8,128)}, u32[]{:S(2)}) %copy-start.3) | copy-done | bytes 131096
  12.8 0.4 light.1
  13.2 0.0 collective-permute-done.following
  13.3 0.5 windows.1
  13.8 0.0 copy-start
  13.8 0.0 copy-start.2
  13.8 17.8 %all_to_all.20.patch = f32[4,2,2,128,128]{4,3,2,1,0:T(8,128)S(1)} all-to-all(f32[4,2,2,128,128]{4,3,2,1,0:T(8,128)S(1)} %windows.1), channel_id=1, replica_groups=mesh['z'=8,'y'=8,'core'=2,'cuts'=4] {'cuts'}, dimensions={0} | all-to-all | bytes 2097152 | tf_op jit(solution)/shard_map/all_to_all | solution.py:243
  31.6 0.0 copy-done
  31.6 0.0 copy-done.2
  31.6 4.7 %waves.1 = (f32[2,2,128,128]{3,2,1,0:T(8,128)S(1)}, f32[2,2,128,128]{3,2,1,0:T(8,128)S(1)}, f32[2,2,128,128]{3,2,1,0:T(8,128)S(1)}, f32[2,2,128,128]{3,2,1,0:T(8,128)S(1)}, f32[32,8,128]{2,1,0:T(8,128)}) custom-call(s32[8,128]{1,0:T(8,128)S(1)} %pad.9.info, f32[2,128,128]{2,1,0:T(8,128)S(1)} %get-tuple-element.39.probe, f32[8,128,128]{2,1,0:T(8,128)S(1)} %copy-done.2, ...), custom_call_target="tpu_custom_call" | custom-call | tf_op jit(solution)/shard_map/waves/pallas_call | solution.py:301
  36.3 2.4 %collective-permute-start.1 = (f32[2,2,128,128]{3,2,1,0:T(8,128)S(1)}, f32[2,2,128,128]{3,2,1,0:T(8,128)S(1)}, u32[]{:S(2)}, u32[]{:S(2)}) collective-permute-start(f32[2,2,128,128]{3,2,1,0:T(8,128)S(1)} %get-tuple-element.43), channel_id=1, source_target_pairs={{0,2},{1,3},{2,0},{3,1},{4,6},{5,7},{6,4},{7,5},{8,10},{9,11},{10,... | collective-permute-start | bytes 786440 | tf_op jit(solution)/shard_map/ppermute | solution.py:239
  38.8 9.5 %all-to-all-start.1 = ((f32[32,8,128]{2,1,0:T(8,128)}), f32[32,8,128]{2,1,0:T(8,128)S(1)}, u32[]{:S(2)}, u32[]{:S(2)}) async-start(f32[32,8,128]{2,1,0:T(8,128)} %get-tuple-element.42), calls=%async_computation.1 | async-start | bytes 262144 | tf_op jit(solution)/shard_map/all_to_all | solution.py:243
  48.3 3.1 %collective-permute-start.2 = (f32[2,2,128,128]{3,2,1,0:T(8,128)S(1)}, f32[2,2,128,128]{3,2,1,0:T(8,128)S(1)}, u32[]{:S(2)}, u32[]{:S(2)}) collective-permute-start(f32[2,2,128,128]{3,2,1,0:T(8,128)S(1)} %get-tuple-element.47), channel_id=1, source_target_pairs={{0,1},{1,2},{2,3},{3,0},{4,5},{5,6},{6,7},{7,4},{8,9},{9,10},{10,1... | collective-permute-start | bytes 786440 | tf_op jit(solution)/shard_map/ppermute | solution.py:239
  51.4 3.4 %collective-permute-start.3 = (f32[2,2,128,128]{3,2,1,0:T(8,128)S(1)}, f32[2,2,128,128]{3,2,1,0:T(8,128)S(1)}, u32[]{:S(2)}, u32[]{:S(2)}) collective-permute-start(f32[2,2,128,128]{3,2,1,0:T(8,128)S(1)} %get-tuple-element.49), channel_id=1, source_target_pairs={{0,3},{1,0},{2,1},{3,2},{4,7},{5,4},{6,5},{7,6},{8,11},{9,8},{10,9... | collective-permute-start | bytes 786440 | tf_op jit(solution)/shard_map/ppermute | solution.py:239
  54.8 2.8 %all-to-all-done.1.rows = f32[32,8,128]{2,1,0:T(8,128)S(1)} async-done(((f32[32,8,128]{2,1,0:T(8,128)}), f32[32,8,128]{2,1,0:T(8,128)S(1)}, u32[]{:S(2)}, u32[]{:S(2)}) %all-to-all-start.1) | async-done | bytes 131104 | tf_op jit(solution)/shard_map/all_to_all | solution.py:243
  57.6 0.0 collective-permute-done.1.rest_2_
  57.6 0.7 total.2
  58.3 12.4 %all-to-all-start.2 = ((f32[16,8,128]{2,1,0:T(8,128)}), f32[16,8,128]{2,1,0:T(8,128)S(1)}, u32[]{:S(2)}, u32[]{:S(2)}) async-start(f32[16,8,128]{2,1,0:T(8,128)} %total.2), calls=%async_computation.2 | async-start | bytes 131072 | tf_op jit(solution)/shard_map/all_to_all | solution.py:243
  70.7 0.0 collective-permute-done.2.rest_1_
  70.7 0.0 collective-permute-done.3.rest_3_
  70.7 0.6 scatter.14
  71.3 2.6 %collective-permute-start.4 = (f32[2,136,512]{2,1,0:T(8,128)S(1)}, f32[2,136,512]{2,1,0:T(8,128)S(1)}, u32[]{:S(2)}, u32[]{:S(2)}) collective-permute-start(f32[2,136,512]{2,1,0:T(8,128)S(1)} %get-tuple-element.51), channel_id=1, source_target_pairs={{0,4},{4,8},{8,12},{12,16},{16,20},{20,24},{24,28},{28,32},{32,36}... | collective-permute-start | bytes 1671176 | tf_op jit(solution)/shard_map/ppermute | solution.py:234
  74.0 4.5 %all-to-all-done.2.rows = f32[16,8,128]{2,1,0:T(8,128)S(1)} async-done(((f32[16,8,128]{2,1,0:T(8,128)}), f32[16,8,128]{2,1,0:T(8,128)S(1)}, u32[]{:S(2)}, u32[]{:S(2)}) %all-to-all-start.2) | async-done | bytes 65568 | tf_op jit(solution)/shard_map/all_to_all | solution.py:243
  78.5 10.0 %all_to_all.21.rows = f32[8,8,128]{2,1,0:T(8,128)S(1)} all-to-all(f32[8,8,128]{2,1,0:T(8,128)S(1)} %total.3), channel_id=1, replica_groups=mesh['z'=8,'y'=8,'core'=2,'cuts'=4] {'y'}, dimensions={0} | all-to-all | bytes 65536 | tf_op jit(solution)/shard_map/all_to_all | solution.py:243
  88.5 0.0 collective-permute-done.4.rim
  88.5 1.3 %final.1 = (f32[2,1,128,512]{3,2,1,0:T(8,128)}, f32[2,32,128]{2,1,0:T(8,128)}) custom-call(f32[2,128,512]{2,1,0:T(8,128)S(1)} %get-tuple-element.50.inner, f32[2,136,512]{2,1,0:T(8,128)S(1)} %collective-permute-done.4.rim, f32[128,512]{1,0:T(8,128)S(1)} %light.1, f32[2,128,128]{2,1,0:T(8,128)S(1)} %get-tuple-element.39.probe, f32[8,8,128]{2,1,0:T(8,128)S(1)} %all_to_all.21.rows), custom_call_target="tpu_custom_call" | custom-call | tf_op jit(solution)/shard_map/final/pallas_call | solution.py:344
  (6 shorter events, 0.1 us)
Async XLA Ops:
  0.6 12.6 %collective-permute-start = (f32[2,128,512]{2,1,0:T(8,128)}, f32[2,128,512]{2,1,0:T(8,128)S(1)}, u32[]{:S(2)}, u32[]{:S(2)}) collective-permute-start(f32[2,128,512]{2,1,0:T(8,128)} %bitcast.4), channel_id=1, source_target_pairs={{4,0},{8,4},{12,8},{16,12},{20,16},{24,20},{28,24},{32,28},{36,32}... | collective-permute-start | bytes 1572872 | tf_op jit(solution)/shard_map/ppermute | solution.py:234
  10.1 0.7 copy-start.4
  10.8 1.0 %copy-start.1 = (f32[2,1,128,512]{3,2,1,0:T(8,128)S(1)}, f32[2,1,128,512]{3,2,1,0:T(8,128)}, u32[]{:S(2)}) copy-start(f32[2,1,128,512]{3,2,1,0:T(8,128)} %param.10) | copy-start | bytes 1572868
  11.8 0.9 %copy-start.3 = (f32[2,128,128]{2,1,0:T(8,128)S(1)}, f32[2,128,128]{2,1,0:T(8,128)}, u32[]{:S(2)}) copy-start(f32[2,128,128]{2,1,0:T(8,128)} %probe.1) | copy-start | bytes 393220
  13.8 17.8 %copy-start = (bf16[4,2,256,256]{3,2,1,0:T(8,128)(2,1)S(1)}, bf16[4,2,256,256]{3,2,1,0:T(8,128)(2,1)}, u32[]{:S(2)}) copy-start(bf16[4,2,256,256]{3,2,1,0:T(8,128)(2,1)} %constant.75.clone.tables) | copy-start | bytes 3145732
  13.8 17.8 %copy-start.2 = (f32[8,128,128]{2,1,0:T(8,128)S(1)}, f32[8,128,128]{2,1,0:T(8,128)}, u32[]{:S(2)}) copy-start(f32[8,128,128]{2,1,0:T(8,128)} %amplitude.1) | copy-start | bytes 1572868
  36.3 21.3 %collective-permute-start.1 = (f32[2,2,128,128]{3,2,1,0:T(8,128)S(1)}, f32[2,2,128,128]{3,2,1,0:T(8,128)S(1)}, u32[]{:S(2)}, u32[]{:S(2)}) collective-permute-start(f32[2,2,128,128]{3,2,1,0:T(8,128)S(1)} %get-tuple-element.43), channel_id=1, source_target_pairs={{0,2},{1,3},{2,0},{3,1},{4,6},{5,7},{6,4},{7,5},{8,10},{9,11},{10,... | collective-permute-start | bytes 786440 | tf_op jit(solution)/shard_map/ppermute | solution.py:239
  38.8 18.8 %all-to-all-start.1 = ((f32[32,8,128]{2,1,0:T(8,128)}), f32[32,8,128]{2,1,0:T(8,128)S(1)}, u32[]{:S(2)}, u32[]{:S(2)}) async-start(f32[32,8,128]{2,1,0:T(8,128)} %get-tuple-element.42), calls=%async_computation.1 | async-start | bytes 262144 | tf_op jit(solution)/shard_map/all_to_all | solution.py:243
  48.3 22.4 %collective-permute-start.2 = (f32[2,2,128,128]{3,2,1,0:T(8,128)S(1)}, f32[2,2,128,128]{3,2,1,0:T(8,128)S(1)}, u32[]{:S(2)}, u32[]{:S(2)}) collective-permute-start(f32[2,2,128,128]{3,2,1,0:T(8,128)S(1)} %get-tuple-element.47), channel_id=1, source_target_pairs={{0,1},{1,2},{2,3},{3,0},{4,5},{5,6},{6,7},{7,4},{8,9},{9,10},{10,1... | collective-permute-start | bytes 786440 | tf_op jit(solution)/shard_map/ppermute | solution.py:239
  51.4 19.3 %collective-permute-start.3 = (f32[2,2,128,128]{3,2,1,0:T(8,128)S(1)}, f32[2,2,128,128]{3,2,1,0:T(8,128)S(1)}, u32[]{:S(2)}, u32[]{:S(2)}) collective-permute-start(f32[2,2,128,128]{3,2,1,0:T(8,128)S(1)} %get-tuple-element.49), channel_id=1, source_target_pairs={{0,3},{1,0},{2,1},{3,2},{4,7},{5,4},{6,5},{7,6},{8,11},{9,8},{10,9... | collective-permute-start | bytes 786440 | tf_op jit(solution)/shard_map/ppermute | solution.py:239
  58.3 20.2 %all-to-all-start.2 = ((f32[16,8,128]{2,1,0:T(8,128)}), f32[16,8,128]{2,1,0:T(8,128)S(1)}, u32[]{:S(2)}, u32[]{:S(2)}) async-start(f32[16,8,128]{2,1,0:T(8,128)} %total.2), calls=%async_computation.2 | async-start | bytes 131072 | tf_op jit(solution)/shard_map/all_to_all | solution.py:243
  71.3 17.2 %collective-permute-start.4 = (f32[2,136,512]{2,1,0:T(8,128)S(1)}, f32[2,136,512]{2,1,0:T(8,128)S(1)}, u32[]{:S(2)}, u32[]{:S(2)}) collective-permute-start(f32[2,136,512]{2,1,0:T(8,128)S(1)} %get-tuple-element.51), channel_id=1, source_target_pairs={{0,4},{4,8},{8,12},{12,16},{16,20},{20,24},{24,28},{28,32},{32,36}... | collective-permute-start | bytes 1671176 | tf_op jit(solution)/shard_map/ppermute | solution.py:234

commit v14 on v13

--- a/solution.py
+++ b/solution.py
@@ -100,13 +100,13 @@
 
 def placed(value, down, right):
     n = value.shape[0]
+    value = pltpu.roll(value, lax.rem(right, n), axis=1)
     groups = pltpu.roll(value.reshape(n // 8, 8, n), down, axis=1)
     empty = jnp.zeros((1, 8, n), jnp.float32)
     line = lax.broadcasted_iota(jnp.int32, (n // 8 + 1, 8, n), 1)
     tall = jnp.where(
         line >= down, jnp.concatenate([groups, empty], axis=0), jnp.concatenate([empty, groups], axis=0)
     ).reshape(n + 8, n)
-    tall = pltpu.roll(tall, lax.rem(right, n), axis=1)
     lane = lax.broadcasted_iota(jnp.int32, (n + 8, n), 1)
     return jnp.concatenate([jnp.where(lane >= right, tall, 0.0), jnp.where(lane < right, tall, 0.0)], axis=1)
 

time: 90.3 us -> 90.3 us (level)
  no operation moved by 1% of the time
where the time goes in v14:
time: 90.3 us; the launch traced here: 89.8 us
  starting transfers between devices  42.2 us (47%)
  blocking collectives  27.8 us (31%)
  Pallas kernels  8.33 us (9%)
  waiting for transfers between devices  7.38 us (8%)
  local copies, waits for them, and re-layouts  2.64 us (3%)
  between operations  1.43 us (2%)
    all_to_all x2, blocking collectives, swap(): return lax.all_to_all(block, axes, 0, 0)  27.8 us
    all_to_all x2, starting transfers between devices, swap(): return lax.all_to_all(block, axes, 0, 0)  21.9 us
    ppermute x2, starting transfers between devices, along(): lax.ppermute(block, POS, [(i - distance, i) for i in devices if i - dista...  11.4 us
    ppermute x3, starting transfers between devices, around(): lax.ppermute(block, 'cuts', [(i, (i + distance) % count) for i in range(c...  8.94 us
    all_to_all x2, waiting for transfers between devices, swap(): return lax.all_to_all(block, axes, 0, 0)  7.37 us
    pallas_call x1, Pallas kernels, local(): pl.pallas_call(functools.partial(wave_kernel, 1.0 / math.sqrt(slots * acr...  4.72 us
    unnamed x10, local copies, waits for them, and re-layouts  2.52 us
  transfers between devices with their start and end apart: 7, of which 2 were waited for; matrix products, arithmetic and copies ran while one was open for 0% of the time, Pallas kernels for 2%

profile of v14, /device:TPU:1, one launch (start us, length us, event | category | flops | bytes accessed | tf_op | source)
XLA Modules:
  0.0 89.8 jit_solution(4893586574212221653)
XLA Ops:
  0.6 8.8 %collective-permute-start = (f32[2,128,512]{2,1,0:T(8,128)}, f32[2,128,512]{2,1,0:T(8,128)S(1)}, u32[]{:S(2)}, u32[]{:S(2)}) collective-permute-start(f32[2,128,512]{2,1,0:T(8,128)} %bitcast.4), channel_id=1, source_target_pairs={{4,0},{8,4},{12,8},{16,12},{20,16},{24,20},{28,24},{32,28},{36,32}... | collective-permute-start | bytes 1572872 | tf_op jit(solution)/shard_map/ppermute | solution.py:234
  10.1 0.0 copy-start.4
  10.1 0.1 scatter.12
  10.2 0.6 copy-done.4
  10.8 0.0 copy-start.1
  10.8 1.0 %copy-done.1 = f32[2,1,128,512]{3,2,1,0:T(8,128)S(1)} copy-done((f32[2,1,128,512]{3,2,1,0:T(8,128)S(1)}, f32[2,1,128,512]{3,2,1,0:T(8,128)}, u32[]{:S(2)}) %copy-start.1) | copy-done | bytes 524312
  11.8 0.0 copy-start.3
  11.9 0.9 %copy-done.3 = f32[2,128,128]{2,1,0:T(8,128)S(1)} copy-done((f32[2,128,128]{2,1,0:T(8,128)S(1)}, f32[2,128,128]{2,1,0:T(8,128)}, u32[]{:S(2)}) %copy-start.3) | copy-done | bytes 131096
  12.8 0.4 light.1
  13.2 0.0 collective-permute-done.following
  13.2 0.5 windows.1
  13.8 0.0 copy-start
  13.8 0.0 copy-start.2
  13.8 17.8 %all_to_all.20.patch = f32[4,2,2,128,128]{4,3,2,1,0:T(8,128)S(1)} all-to-all(f32[4,2,2,128,128]{4,3,2,1,0:T(8,128)S(1)} %windows.1), channel_id=1, replica_groups=mesh['z'=8,'y'=8,'core'=2,'cuts'=4] {'cuts'}, dimensions={0} | all-to-all | bytes 2097152 | tf_op jit(solution)/shard_map/all_to_all | solution.py:243
  31.6 0.0 copy-done
  31.6 0.0 copy-done.2
  31.6 4.7 %waves.1 = (f32[2,2,128,128]{3,2,1,0:T(8,128)S(1)}, f32[2,2,128,128]{3,2,1,0:T(8,128)S(1)}, f32[2,2,128,128]{3,2,1,0:T(8,128)S(1)}, f32[2,2,128,128]{3,2,1,0:T(8,128)S(1)}, f32[32,8,128]{2,1,0:T(8,128)}) custom-call(s32[8,128]{1,0:T(8,128)S(1)} %pad.9.info, f32[2,128,128]{2,1,0:T(8,128)S(1)} %get-tuple-element.39.probe, f32[8,128,128]{2,1,0:T(8,128)S(1)} %copy-done.2, ...), custom_call_target="tpu_custom_call" | custom-call | tf_op jit(solution)/shard_map/waves/pallas_call | solution.py:301
  36.3 2.4 %collective-permute-start.1 = (f32[2,2,128,128]{3,2,1,0:T(8,128)S(1)}, f32[2,2,128,128]{3,2,1,0:T(8,128)S(1)}, u32[]{:S(2)}, u32[]{:S(2)}) collective-permute-start(f32[2,2,128,128]{3,2,1,0:T(8,128)S(1)} %get-tuple-element.43), channel_id=1, source_target_pairs={{0,2},{1,3},{2,0},{3,1},{4,6},{5,7},{6,4},{7,5},{8,10},{9,11},{10,... | collective-permute-start | bytes 786440 | tf_op jit(solution)/shard_map/ppermute | solution.py:239
  38.8 9.5 %all-to-all-start.1 = ((f32[32,8,128]{2,1,0:T(8,128)}), f32[32,8,128]{2,1,0:T(8,128)S(1)}, u32[]{:S(2)}, u32[]{:S(2)}) async-start(f32[32,8,128]{2,1,0:T(8,128)} %get-tuple-element.42), calls=%async_computation.1 | async-start | bytes 262144 | tf_op jit(solution)/shard_map/all_to_all | solution.py:243
  48.2 3.1 %collective-permute-start.2 = (f32[2,2,128,128]{3,2,1,0:T(8,128)S(1)}, f32[2,2,128,128]{3,2,1,0:T(8,128)S(1)}, u32[]{:S(2)}, u32[]{:S(2)}) collective-permute-start(f32[2,2,128,128]{3,2,1,0:T(8,128)S(1)} %get-tuple-element.47), channel_id=1, source_target_pairs={{0,1},{1,2},{2,3},{3,0},{4,5},{5,6},{6,7},{7,4},{8,9},{9,10},{10,1... | collective-permute-start | bytes 786440 | tf_op jit(solution)/shard_map/ppermute | solution.py:239
  51.4 3.4 %collective-permute-start.3 = (f32[2,2,128,128]{3,2,1,0:T(8,128)S(1)}, f32[2,2,128,128]{3,2,1,0:T(8,128)S(1)}, u32[]{:S(2)}, u32[]{:S(2)}) collective-permute-start(f32[2,2,128,128]{3,2,1,0:T(8,128)S(1)} %get-tuple-element.49), channel_id=1, source_target_pairs={{0,3},{1,0},{2,1},{3,2},{4,7},{5,4},{6,5},{7,6},{8,11},{9,8},{10,9... | collective-permute-start | bytes 786440 | tf_op jit(solution)/shard_map/ppermute | solution.py:239
  54.8 2.8 %all-to-all-done.1.rows = f32[32,8,128]{2,1,0:T(8,128)S(1)} async-done(((f32[32,8,128]{2,1,0:T(8,128)}), f32[32,8,128]{2,1,0:T(8,128)S(1)}, u32[]{:S(2)}, u32[]{:S(2)}) %all-to-all-start.1) | async-done | bytes 131104 | tf_op jit(solution)/shard_map/all_to_all | solution.py:243
  57.6 0.0 collective-permute-done.1.rest_2_
  57.6 0.7 total.2
  58.3 12.4 %all-to-all-start.2 = ((f32[16,8,128]{2,1,0:T(8,128)}), f32[16,8,128]{2,1,0:T(8,128)S(1)}, u32[]{:S(2)}, u32[]{:S(2)}) async-start(f32[16,8,128]{2,1,0:T(8,128)} %total.2), calls=%async_computation.2 | async-start | bytes 131072 | tf_op jit(solution)/shard_map/all_to_all | solution.py:243
  70.7 0.0 collective-permute-done.2.rest_1_
  70.7 0.0 collective-permute-done.3.rest_3_
  70.7 0.6 scatter.14
  71.3 2.6 %collective-permute-start.4 = (f32[2,136,512]{2,1,0:T(8,128)S(1)}, f32[2,136,512]{2,1,0:T(8,128)S(1)}, u32[]{:S(2)}, u32[]{:S(2)}) collective-permute-start(f32[2,136,512]{2,1,0:T(8,128)S(1)} %get-tuple-element.51), channel_id=1, source_target_pairs={{0,4},{4,8},{8,12},{12,16},{16,20},{20,24},{24,28},{28,32},{32,36}... | collective-permute-start | bytes 1671176 | tf_op jit(solution)/shard_map/ppermute | solution.py:234
  73.9 4.5 %all-to-all-done.2.rows = f32[16,8,128]{2,1,0:T(8,128)S(1)} async-done(((f32[16,8,128]{2,1,0:T(8,128)}), f32[16,8,128]{2,1,0:T(8,128)S(1)}, u32[]{:S(2)}, u32[]{:S(2)}) %all-to-all-start.2) | async-done | bytes 65568 | tf_op jit(solution)/shard_map/all_to_all | solution.py:243
  78.5 10.0 %all_to_all.21.rows = f32[8,8,128]{2,1,0:T(8,128)S(1)} all-to-all(f32[8,8,128]{2,1,0:T(8,128)S(1)} %total.3), channel_id=1, replica_groups=mesh['z'=8,'y'=8,'core'=2,'cuts'=4] {'y'}, dimensions={0} | all-to-all | bytes 65536 | tf_op jit(solution)/shard_map/all_to_all | solution.py:243
  88.5 0.0 collective-permute-done.4.rim
  88.5 1.3 %final.1 = (f32[2,1,128,512]{3,2,1,0:T(8,128)}, f32[2,32,128]{2,1,0:T(8,128)}) custom-call(f32[2,128,512]{2,1,0:T(8,128)S(1)} %get-tuple-element.50.inner, f32[2,136,512]{2,1,0:T(8,128)S(1)} %collective-permute-done.4.rim, f32[128,512]{1,0:T(8,128)S(1)} %light.1, f32[2,128,128]{2,1,0:T(8,128)S(1)} %get-tuple-element.39.probe, f32[8,8,128]{2,1,0:T(8,128)S(1)} %all_to_all.21.rows), custom_call_target="tpu_custom_call" | custom-call | tf_op jit(solution)/shard_map/final/pallas_call | solution.py:344
  (6 shorter events, 0.1 us)
Async XLA Ops:
  0.6 12.6 %collective-permute-start = (f32[2,128,512]{2,1,0:T(8,128)}, f32[2,128,512]{2,1,0:T(8,128)S(1)}, u32[]{:S(2)}, u32[]{:S(2)}) collective-permute-start(f32[2,128,512]{2,1,0:T(8,128)} %bitcast.4), channel_id=1, source_target_pairs={{4,0},{8,4},{12,8},{16,12},{20,16},{24,20},{28,24},{32,28},{36,32}... | collective-permute-start | bytes 1572872 | tf_op jit(solution)/shard_map/ppermute | solution.py:234
  10.1 0.7 copy-start.4
  10.8 1.0 %copy-start.1 = (f32[2,1,128,512]{3,2,1,0:T(8,128)S(1)}, f32[2,1,128,512]{3,2,1,0:T(8,128)}, u32[]{:S(2)}) copy-start(f32[2,1,128,512]{3,2,1,0:T(8,128)} %param.10) | copy-start | bytes 1572868
  11.8 0.9 %copy-start.3 = (f32[2,128,128]{2,1,0:T(8,128)S(1)}, f32[2,128,128]{2,1,0:T(8,128)}, u32[]{:S(2)}) copy-start(f32[2,128,128]{2,1,0:T(8,128)} %probe.1) | copy-start | bytes 393220
  13.8 17.8 %copy-start = (bf16[4,2,256,256]{3,2,1,0:T(8,128)(2,1)S(1)}, bf16[4,2,256,256]{3,2,1,0:T(8,128)(2,1)}, u32[]{:S(2)}) copy-start(bf16[4,2,256,256]{3,2,1,0:T(8,128)(2,1)} %constant.75.clone.tables) | copy-start | bytes 3145732
  13.8 17.8 %copy-start.2 = (f32[8,128,128]{2,1,0:T(8,128)S(1)}, f32[8,128,128]{2,1,0:T(8,128)}, u32[]{:S(2)}) copy-start(f32[8,128,128]{2,1,0:T(8,128)} %amplitude.1) | copy-start | bytes 1572868
  36.3 21.3 %collective-permute-start.1 = (f32[2,2,128,128]{3,2,1,0:T(8,128)S(1)}, f32[2,2,128,128]{3,2,1,0:T(8,128)S(1)}, u32[]{:S(2)}, u32[]{:S(2)}) collective-permute-start(f32[2,2,128,128]{3,2,1,0:T(8,128)S(1)} %get-tuple-element.43), channel_id=1, source_target_pairs={{0,2},{1,3},{2,0},{3,1},{4,6},{5,7},{6,4},{7,5},{8,10},{9,11},{10,... | collective-permute-start | bytes 786440 | tf_op jit(solution)/shard_map/ppermute | solution.py:239
  38.8 18.8 %all-to-all-start.1 = ((f32[32,8,128]{2,1,0:T(8,128)}), f32[32,8,128]{2,1,0:T(8,128)S(1)}, u32[]{:S(2)}, u32[]{:S(2)}) async-start(f32[32,8,128]{2,1,0:T(8,128)} %get-tuple-element.42), calls=%async_computation.1 | async-start | bytes 262144 | tf_op jit(solution)/shard_map/all_to_all | solution.py:243
  48.2 22.4 %collective-permute-start.2 = (f32[2,2,128,128]{3,2,1,0:T(8,128)S(1)}, f32[2,2,128,128]{3,2,1,0:T(8,128)S(1)}, u32[]{:S(2)}, u32[]{:S(2)}) collective-permute-start(f32[2,2,128,128]{3,2,1,0:T(8,128)S(1)} %get-tuple-element.47), channel_id=1, source_target_pairs={{0,1},{1,2},{2,3},{3,0},{4,5},{5,6},{6,7},{7,4},{8,9},{9,10},{10,1... | collective-permute-start | bytes 786440 | tf_op jit(solution)/shard_map/ppermute | solution.py:239
  51.4 19.3 %collective-permute-start.3 = (f32[2,2,128,128]{3,2,1,0:T(8,128)S(1)}, f32[2,2,128,128]{3,2,1,0:T(8,128)S(1)}, u32[]{:S(2)}, u32[]{:S(2)}) collective-permute-start(f32[2,2,128,128]{3,2,1,0:T(8,128)S(1)} %get-tuple-element.49), channel_id=1, source_target_pairs={{0,3},{1,0},{2,1},{3,2},{4,7},{5,4},{6,5},{7,6},{8,11},{9,8},{10,9... | collective-permute-start | bytes 786440 | tf_op jit(solution)/shard_map/ppermute | solution.py:239
  58.3 20.2 %all-to-all-start.2 = ((f32[16,8,128]{2,1,0:T(8,128)}), f32[16,8,128]{2,1,0:T(8,128)S(1)}, u32[]{:S(2)}, u32[]{:S(2)}) async-start(f32[16,8,128]{2,1,0:T(8,128)} %total.2), calls=%async_computation.2 | async-start | bytes 131072 | tf_op jit(solution)/shard_map/all_to_all | solution.py:243
  71.3 17.2 %collective-permute-start.4 = (f32[2,136,512]{2,1,0:T(8,128)S(1)}, f32[2,136,512]{2,1,0:T(8,128)S(1)}, u32[]{:S(2)}, u32[]{:S(2)}) collective-permute-start(f32[2,136,512]{2,1,0:T(8,128)S(1)} %get-tuple-element.51), channel_id=1, source_target_pairs={{0,4},{4,8},{8,12},{12,16},{16,20},{20,24},{24,28},{28,32},{32,36}... | collective-permute-start | bytes 1671176 | tf_op jit(solution)/shard_map/ppermute | solution.py:234
